TPU v7x, 256 devices: a whole 4x4x8 slice. The times are simulated.
256 devices in a mesh: master: 8 (over x, core), region: 32 (over z, y).
Axes of the slice: x: 4, y: 4, z: 8, core: 2. Of those that a mesh axis runs over, the one named last changes fastest.
Arguments:
- masters: float32 [1024, 128, 128], P('master'), may hold values from 0 to 1
- inst_master: int32 [8, 32, 16], P(None, 'region'), may hold values from 0 to 127
- inst_row: int32 [8, 32, 16], P(None, 'region'), may hold values from 0 to 256
- inst_col: int32 [8, 32, 16], P(None, 'region'), may hold values from 0 to 896
- def_index: int32 [32], P('region'), may hold values from 0 to 7
- def_weights: float32 [8, 12], replicated, may hold values from 0.1 to 1
- kernels: bfloat16 [24, 225], replicated, may hold values from -0.375 to 0.375
- target: bfloat16 [32, 384, 1024], P('region', 'master'), may hold values from 0 to 1
Outputs:
- master_grad: float32 [1024, 128, 128], P('master')
- resist: bfloat16 [32, 384, 1024], P('region', 'master')
Inputs may be any that keep to these rules, and one draw needn't show every extreme that they name: inst_master[s, r, i] names master s * 128 + inst_master[s, r, i], an instance in the tile of region r; panels of one tile may intersect. `inst_row`: every placed panel lies wholly inside its tile. `inst_col`: every placed panel lies wholly inside its tile.
All inputs are finite; a program needn't handle non-finite values.
Results may differ from a plain program's by a relative error of at most 0.0061.
Values may be sent and summed in bfloat16 or wider, within the bound.
No kernel may reach another device: no remote copies, remote signals or barrier semaphores. Data moves between devices by JAX's collectives and lax.ppermute only.
A program may use at most 128 MiB of HBM per device.

v0:
```python
import functools
import jax, jax.numpy as jnp
from jax import lax
from jax.experimental import pallas as pl
from jax.sharding import Mesh, PartitionSpec as P
from jax.experimental.pallas import tpu as pltpu

TC = 1024; TR = 48; KS = 15; KERN = 12; P_SIZE = 128; MAS_DEV = 128; INST_DEV = 16
STEEP = 1.5; THRESH = 3.0
BR, BC = 8, 16
H = 7
ROWB = 8
MROWB = ROWB + 2
COLB = TC // BC
M = ROWB * COLB
K = 6 * 128
F32, BF = jnp.float32, jnp.bfloat16


def swap_chunks(x):
    n = x.shape[0]
    row = lax.broadcasted_iota(jnp.int32, (n, 128), 0)
    chunk = lax.broadcasted_iota(jnp.int32, (n, 128), 1) // BC

    def sub(v, k):
        return pltpu.roll(v.reshape(n // 8, 8, 128), k, 1).reshape(n, 128)

    for k in (1, 2, 4):
        rbit = (row & k) != 0
        cbit = (chunk & k) != 0
        up = sub(pltpu.roll(x, 128 - BC * k, 1), k)
        if k == 4:
            dn = up
        else:
            dn = sub(pltpu.roll(x, BC * k, 1), 8 - k)
        x = jnp.where(rbit == cbit, x, jnp.where(rbit, up, dn))
    return x


def to_blocks(x):
    a, b = x.shape[0] // 8, x.shape[1] // 128
    tiles = [x[8 * i : 8 * i + 8, 128 * t : 128 * t + 128] for i in range(a) for t in range(b)]
    return swap_chunks(jnp.concatenate(tiles, axis=0))


def from_blocks(v, a, b):
    x = swap_chunks(v)
    rows = []
    for i in range(a):
        rows.append(jnp.concatenate([x[(i * b + t) * 8 : (i * b + t) * 8 + 8] for t in range(b)], axis=1))
    return jnp.concatenate(rows, axis=0)


def table_kernel(v_ref, w_ref):
    lane = lax.broadcasted_iota(jnp.int32, (16, 512), 1) % BC
    row = lax.broadcasted_iota(jnp.int32, (16, 512), 0)
    low = lane <= row

    def one(c, carry):
        at = pl.ds(pl.multiple_of(c * 128, 128), 128)
        x = jnp.broadcast_to(v_ref[c], (16, 512))
        r = pltpu.roll(x, 1, 1, stride=1, stride_axis=0)
        lo = jnp.where(low, r, 0.0)
        hi = jnp.where(low, 0.0, r)
        for p in range(8):
            lp = (pltpu.roll(lo, 512 - 16 * p, 1) if p else lo).astype(BF)
            hp = (pltpu.roll(hi, 512 - 16 * p, 1) if p else hi).astype(BF)
            for wy in range(24):
                dy, yw = wy // 8, wy % 8
                if (24 - wy) % 8 == p:
                    q = (24 - wy) // 8
                    w_ref[(dy * 2) * 128 + yw * 16 : (dy * 2) * 128 + yw * 16 + 16, at] = lp[:, 128 * q : 128 * q + 128]
                if (23 - wy) % 8 == p:
                    q = (23 - wy) // 8
                    w_ref[(dy * 2 + 1) * 128 + yw * 16 : (dy * 2 + 1) * 128 + yw * 16 + 16, at] = hp[:, 128 * q : 128 * q + 128]
        return carry

    lax.fori_loop(0, 2 * KERN, one, 0)


def taps_rows(kernels):
    k = kernels.astype(F32).reshape(2, KERN, KS, KS).swapaxes(0, 1).reshape(2 * KERN, KS, KS)
    k = k[:, ::-1, ::-1]
    k = jnp.pad(k, ((0, 0), (9, 32 - 9 - KS), (1, 0)))
    return k.reshape(2 * KERN, 1, 512)


def make_table(kernels):
    return pl.pallas_call(
        table_kernel,
        out_shape=jax.ShapeDtypeStruct((K, 2 * KERN * 128), BF),
        in_specs=[pl.BlockSpec(memory_space=pltpu.VMEM)],
        out_specs=pl.BlockSpec(memory_space=pltpu.VMEM),
        compiler_params=pltpu.CompilerParams(vmem_limit_bytes=32 * 1024 * 1024),
        cost_estimate=pl.CostEstimate(flops=20_000_000, bytes_accessed=10_000_000, transcendentals=0),
        name="taps_table",
    )(taps_rows(kernels))


def image_kernel(level_ref, shard_ref, wgt_ref, m0_ref, m1_ref, m2_ref, m3_ref, tabove_ref, tmid_ref, tbelow_ref, info_ref, w_ref,
                 resist_ref, grad_ref, lhs_ref, fields_ref, cot_ref):
    level_at = level_ref[0]
    x = (m0_ref[...] + m1_ref[...] + m2_ref[...] + m3_ref[...]).astype(BF).astype(F32)
    x = pltpu.roll(x, 8 * MROWB - 1, 0)
    x = jnp.concatenate([x, jnp.zeros((8 * MROWB, 128), F32)], axis=1)
    x = pltpu.roll(x, H, 1)
    mb = to_blocks(x).reshape(MROWB, 72, 128)
    for dy in range(3):
        for dx in range(2):
            part = mb[dy : dy + ROWB, dx : dx + COLB, :]
            lhs_ref[:, (dy * 2 + dx) * 128 : (dy * 2 + dx) * 128 + 128] = part.reshape(M, 128).astype(BF)
    intensity = jnp.zeros((M, 128), F32)
    for c in range(KERN):
        f = jnp.dot(lhs_ref[...], w_ref[:, c * 256 : c * 256 + 256], preferred_element_type=F32)
        fields_ref[c] = f
        f = f * f
        intensity = intensity + wgt_ref[level_at, c] * (f[:, :128] + f[:, 128:])
    level = 1.0 / (1.0 + jnp.exp(-STEEP * (intensity - THRESH)))
    resist_ref[...] = from_blocks(level, ROWB, 8)[8 : 8 + TR].astype(BF)
    goal = jnp.concatenate([tabove_ref[...].astype(F32)[8:], tmid_ref[...].astype(F32), tbelow_ref[...].astype(F32)[:8]], axis=0)
    goal = to_blocks(goal)
    slope = STEEP * (level - goal) * level * (1.0 - level)
    row_block = lax.broadcasted_iota(jnp.int32, (M, 128), 0) // COLB
    in_block = lax.broadcasted_iota(jnp.int32, (M, 128), 1) // BC
    at = shard_ref[0] * TR - 8 + row_block * 8 + in_block
    slope = jnp.where((at >= 0) & (at < 8 * TR), slope, 0.0)
    for c in range(KERN):
        s = 2.0 * wgt_ref[level_at, c] * slope
        cot_ref[:, c * 256 : c * 256 + 256] = (jnp.concatenate([s, s], axis=1) * fields_ref[c]).astype(BF)
    out = [None] * 7
    for dy in range(3):
        acc = lax.dot_general(cot_ref[...], w_ref[dy * 256 : dy * 256 + 256, :], (((1,), (1,)), ((), ())), preferred_element_type=F32)
        for dx in range(2):
            for i in range(ROWB):
                j = i + dy
                if 1 <= j <= 7:
                    piece = acc[i * COLB : i * COLB + COLB, dx * 128 : dx * 128 + 128]
                    piece = jnp.concatenate([piece, jnp.zeros((8, 128), F32)], axis=0)
                    if dx:
                        piece = pltpu.roll(piece, 1, 0)
                    out[j - 1] = piece if out[j - 1] is None else out[j - 1] + piece
    nat = from_blocks(jnp.concatenate(out, axis=0), 7, 9)
    nat = pltpu.roll(nat, 9 * 128 - H, 1)
    grad_ref[:TR] = nat[H : H + TR, :TC].astype(BF)
    info = jnp.broadcast_to(info_ref[...], (16, 128))
    row = lax.broadcasted_iota(jnp.int32, (16, 128), 0)
    digits = jnp.where(row == 0, info >> 7, jnp.where(row == 1, info & 127, 0)).astype(F32)
    grad_ref[TR:] = jnp.concatenate([digits, jnp.zeros((16, TC - 128), F32)], axis=1).astype(BF)


def image(level, shard, weights, parts, tabove, tmid, tbelow, info, table):
    vm = pl.BlockSpec(memory_space=pltpu.VMEM)
    sm = pl.BlockSpec(memory_space=pltpu.SMEM)
    return pl.pallas_call(
        image_kernel,
        out_shape=(jax.ShapeDtypeStruct((TR, TC), BF), jax.ShapeDtypeStruct((TR + 16, TC), BF)),
        in_specs=[sm] * 3 + [vm] * 9,
        out_specs=(vm, vm),
        scratch_shapes=[pltpu.VMEM((M, K), BF), pltpu.VMEM((KERN, M, 256), F32), pltpu.VMEM((M, 2 * KERN * 128), BF)],
        compiler_params=pltpu.CompilerParams(vmem_limit_bytes=28 * 1024 * 1024),
        cost_estimate=pl.CostEstimate(flops=5_000_000_000, bytes_accessed=8_000_000, transcendentals=65536),
        name="image",
    )(level, shard, weights, *parts, tabove, tmid, tbelow, info, table)


NX, NC, NY, NZ = 4, 2, 4, 8
WIDE = TC + 128
LEAD = 16
EXT = TR + 2 * LEAD
INFO = 128
PLACE_GRANT = 58


def place_kernel(shard_ref, ids_hbm, rows_hbm, cols_hbm, masters_hbm, mine_ref, theirs_ref, info_ref, scalars, panels, canvas, sem, info_sem):
    shard = shard_ref[0]
    loads = [pltpu.make_async_copy(ref.at[shard], scalars.at[j], info_sem.at[j]) for j, ref in enumerate((ids_hbm, rows_hbm, cols_hbm))]
    for cp in loads:
        cp.start()
    for cp in loads:
        cp.wait()
    copies = []
    for i in range(INST_DEV):
        cp = pltpu.make_async_copy(masters_hbm.at[scalars[0, 0, i]], panels.at[i], sem.at[i])
        cp.start()
        copies.append(cp)
        for j in range(3):
            info_ref[0, j * INST_DEV + i] = scalars[j, 0, i]
    for i in range(3 * INST_DEV, INFO):
        info_ref[0, i] = 0
    canvas[...] = jnp.zeros(canvas.shape, F32)
    lane = lax.broadcasted_iota(jnp.int32, (P_SIZE, 128), 1)
    for i in range(INST_DEV):
        copies[i].wait()
        p = panels[i].astype(BF).astype(F32)
        c = scalars[2, 0, i]
        c0 = (c // 128) * 128
        d = c - c0
        p = pltpu.roll(p, d, 1)
        left = jnp.where(lane >= d, p, 0.0)
        right = jnp.where(lane >= d, 0.0, p)
        full = jnp.concatenate([jnp.concatenate([left, right], axis=1), jnp.zeros((8, 256), F32)], axis=0)
        r = scalars[1, 0, i] + LEAD
        r0 = (r // 8) * 8
        full = pltpu.roll(full, r - r0, 0)
        at = (pl.ds(pl.multiple_of(r0, 8), P_SIZE + 8), pl.ds(pl.multiple_of(c0, 128), 256))
        canvas[at] = canvas[at] + full
    core = shard % NC
    for d in range(NX):
        x = (shard // NC + d) % NX
        mine_ref[d] = canvas[pl.ds(pl.multiple_of((x * NC + core) * TR, 8), EXT), :TC]
        theirs_ref[d] = canvas[pl.ds(pl.multiple_of((x * NC + 1 - core) * TR, 8), EXT), :TC]


def place(shard, ids, rows, cols, masters):
    vm = pl.BlockSpec(memory_space=pltpu.VMEM)
    sm = pl.BlockSpec(memory_space=pltpu.SMEM)
    hbm = pl.BlockSpec(memory_space=pltpu.HBM)
    bands = jax.ShapeDtypeStruct((NX, EXT, TC), F32)
    return pl.pallas_call(
        place_kernel,
        out_shape=(bands, bands, jax.ShapeDtypeStruct((1, INFO), jnp.int32)),
        in_specs=[sm] + [hbm] * 4,
        out_specs=(vm, vm, sm),
        scratch_shapes=[
            pltpu.SMEM((3, 1, INST_DEV), jnp.int32),
            pltpu.VMEM((INST_DEV, P_SIZE, P_SIZE), F32),
            pltpu.VMEM((LEAD + 8 * TR + LEAD, WIDE), F32),
            pltpu.SemaphoreType.DMA((INST_DEV,)),
            pltpu.SemaphoreType.DMA((3,)),
        ],
        compiler_params=pltpu.CompilerParams(vmem_limit_bytes=PLACE_GRANT * 1024 * 1024),
        cost_estimate=pl.CostEstimate(flops=1_000_000, bytes_accessed=12_000_000, transcendentals=0),
        name="place",
    )(shard, ids, rows, cols, masters)


def cut_kernel(shard_ref, region_ref, g0, g1, g2, g3, own_ref, up_ref, down_ref, far_ref, *rest):
    outs, (canvas, sums, digits, lists, list_sem) = rest[:NZ], rest[NZ:]
    digits[...] = jnp.zeros(digits.shape, jnp.int32)
    for k, g in enumerate((g0, g1, g2, g3)):
        tile = g[TR:, :128].astype(F32)
        digits[k : k + 1] = (tile[0:1] * 128.0 + tile[1:2]).astype(jnp.int32)
    load = pltpu.make_async_copy(digits, lists, list_sem)
    load.start()
    x = shard_ref[0] // NC
    z, y = region_ref[0] // NY, region_ref[0] % NY
    sums[...] = jnp.zeros(sums.shape, F32)

    def lay(ref, n, at):
        for core in range(NC):
            row = ((x + n) % NX * NC + core) * TR
            canvas[at, pl.ds(pl.multiple_of(row, 8), TR), :TC] = ref[core, at].astype(F32)

    for k in range(NY):
        lay(own_ref, 0, k)
        lay(up_ref, 3, k)
        lay(down_ref, 1, k)
        lay(far_ref, 2, k)
    load.wait()
    for k in range(NY):

        def one(i, carry, k=k):
            m = lists[k, i]

            @pl.when((m // 4) % NY == y)
            def _():
                r, c = lists[k, INST_DEV + i], lists[k, 2 * INST_DEV + i]
                r0, c0 = (r // 8) * 8, (c // 128) * 128
                full = canvas[k, pl.ds(pl.multiple_of(r0, 8), P_SIZE + 8), pl.ds(pl.multiple_of(c0, 128), 256)]
                full = pltpu.roll(full, P_SIZE + 8 - (r - r0), 0)[:P_SIZE]
                full = pltpu.roll(full, 256 - (c - c0), 1)[:, :128]
                slot = (m // 16 - z + NZ) % NZ
                sums[slot, m % 4] = sums[slot, m % 4] + full

            return carry

        lax.fori_loop(0, INST_DEV, one, 0)
    for d in range(NZ):
        outs[d][...] = sums[d].astype(outs[d].dtype)


def cut(shard, region, grads, bands):
    vm = pl.BlockSpec(memory_space=pltpu.VMEM)
    sm = pl.BlockSpec(memory_space=pltpu.SMEM)
    slot = (4, P_SIZE, P_SIZE)
    return pl.pallas_call(
        cut_kernel,
        out_shape=[jax.ShapeDtypeStruct(slot, F32)] + [jax.ShapeDtypeStruct(slot, BF)] * (NZ - 1),
        in_specs=[sm] * 2 + [vm] * 8,
        out_specs=[vm] * NZ,
        scratch_shapes=[
            pltpu.VMEM((NY, 8 * TR + 8, WIDE), F32),
            pltpu.VMEM((NZ, 4, P_SIZE, P_SIZE), F32),
            pltpu.VMEM((8, 128), jnp.int32),
            pltpu.SMEM((8, 128), jnp.int32),
            pltpu.SemaphoreType.DMA,
        ],
        compiler_params=pltpu.CompilerParams(vmem_limit_bytes=40 * 1024 * 1024),
        cost_estimate=pl.CostEstimate(flops=1_000_000, bytes_accessed=12_000_000, transcendentals=0),
        name="cut",
    )(shard, region, *grads, *bands)


def deposit_kernel(places, n_in, region_ref, *refs):
    blocks, (out_ref, wide, sem) = refs[: len(places)], refs[n_in:]
    z, y = region_ref[0] // NY, region_ref[0] % NY
    copies = []
    for n, (dz, ys) in enumerate(places):
        wide[n] = blocks[n][...].astype(F32)
        for j, k in enumerate(ys):
            cp = pltpu.make_async_copy(wide.at[n, pl.ds(4 * j, 4)], out_ref.at[(z + dz + NZ) % NZ, (y - k + NY) % NY], sem.at[n, j])
            cp.start()
            copies.append(cp)
    for cp in copies:
        cp.wait()


def deposit(region, out, items):
    places = [item[1:] for item in items]
    blocks = [item[0] for item in items]
    n = len(items)
    hbm = pl.BlockSpec(memory_space=pltpu.HBM)
    old = [] if out is None else [out]
    return pl.pallas_call(
        functools.partial(deposit_kernel, places, n + len(old)),
        out_shape=jax.ShapeDtypeStruct((NZ, NY, 4, P_SIZE, P_SIZE), F32),
        in_specs=[pl.BlockSpec(memory_space=pltpu.SMEM)] + [pl.BlockSpec(memory_space=pltpu.VMEM)] * n + [hbm] * len(old),
        out_specs=hbm,
        input_output_aliases={n + 1: 0} if old else {},
        scratch_shapes=[pltpu.VMEM((n, 8, P_SIZE, P_SIZE), F32), pltpu.SemaphoreType.DMA((n, 2))],
        compiler_params=pltpu.CompilerParams(vmem_limit_bytes=16 * 1024 * 1024),
        cost_estimate=pl.CostEstimate(flops=500_000 * n, bytes_accessed=800_000 * n, transcendentals=0),
        name="deposit",
    )(region, *blocks, *old)


def shift(v, axis, by):
    n = lax.axis_size(axis)
    return lax.ppermute(v, axis, [(i, (i + by) % n) for i in range(n)])


def halo(v, axis, width):
    n = lax.axis_size(axis)
    above = lax.ppermute(v[-width:], axis, [(i, i + 1) for i in range(n - 1)])
    below = lax.ppermute(v[:width], axis, [(i + 1, i) for i in range(n - 1)])
    return above, below


def sum_along_z(slots):
    total = slots[0]
    for d in (4, 3, 5, 2, 6, 1, 7):
        total = total + shift(slots[d], "z", d).astype(F32)
    return total


def spread(part, region):
    before, after, across = shift(part, "y", 1), shift(part, "y", 3), shift(part, "y", 2)
    chunks = (jnp.concatenate([part, before]), jnp.concatenate([after, across]))
    backs = ((0, 1), (3, 2))
    out = deposit(region, None, [(chunks[h], 0, backs[h]) for h in range(2)])
    ups, downs = list(chunks), list(chunks)
    got = []
    for d in (1, 2, 3, 4):
        if d > 1:
            ups[0], downs[0], out = lax.optimization_barrier((ups[0], downs[0], out))
        came, got = got, []
        for h in range(2):
            if d < 4 or h == 0:
                ups[h] = shift(ups[h], "z", 1)
                got.append((ups[h], -d, backs[h]))
            if d < 4 or h == 1:
                downs[h] = shift(downs[h], "z", -1)
                got.append((downs[h], d, backs[h]))
        if came:
            out = deposit(region, out, came)
    out = deposit(region, out, got)
    return out.reshape(MAS_DEV, P_SIZE, P_SIZE)


def body(masters, inst_master, inst_row, inst_col, def_index, def_weights, kernels, target):
    shard = lax.axis_index(("x", "core")).reshape(1)
    region = lax.axis_index(("z", "y")).reshape(1)
    mine, theirs, info = place(shard, inst_master, inst_row, inst_col, masters)
    other = shift(theirs, "core", 1)
    sums = [mine[d] + other[d] for d in range(NX)]
    parts = [sums[0]] + [shift(sums[d], "x", d) for d in (2, 1, 3)]
    tmid = target[0]
    tabove, tbelow = halo(tmid, ("x", "core"), 16)
    table = make_table(kernels)
    resist, grad = image(def_index, shard, def_weights, parts, tabove, tmid, tbelow, info, table)
    grads = [grad] + [shift(grad, "y", k) for k in (1, 2, 3)]
    own = jnp.stack([g[:TR] for g in grads])
    up, down, far = [shift(own, "x", by) for by in (1, 3, 2)]
    bands = [lax.all_gather(v, "core") for v in (own, up, down, far)]
    part = sum_along_z(cut(shard, region, grads, bands)).astype(BF)
    return (spread(part, region), resist[None])


def solution(mesh):
    fine = Mesh(mesh.devices.reshape(NX, NC, NZ, NY), ("x", "core", "z", "y"))
    master, region = ("x", "core"), ("z", "y")
    return jax.shard_map(
        body,
        mesh=fine,
        in_specs=(
            P(master, None, None),
            P(None, region, None),
            P(None, region, None),
            P(None, region, None),
            P(region),
            P(),
            P(),
            P(region, master, None),
        ),
        out_specs=(P(master, None, None), P(region, master, None)),
        check_vma=False,
    )
```

profile of v0, /device:TPU:6, one launch (start us, length us, event | category | flops | bytes accessed | tf_op | source)
XLA Modules:
  0.0 165.0 jit_solution(5477701804851296098)
XLA Ops:
  0.7 5.5 %place.1 = (f32[4,80,1024]{2,1,0:T(8,128)}, f32[4,80,1024]{2,1,0:T(8,128)}, s32[1,128]{1,0:T(1,128)}) custom-call(s32[1]{0:T(128)} %bitcast.1.shard_ref, s32[8,1,16]{2,1,0:T(1,128)} %ids_hbm.1, s32[8,1,16]{2,1,0:T(1,128)} %rows_hbm.1, s32[8,1,16]{2,1,0:T(1,128)} %cols_hbm.1, f32[128,128,128]{2,1,0:T(8,128)} %masters_hbm.1), custom_call_target="tpu_custom_call" | custom-call | flops 1000000 | bytes 12000000 | tf_op jit(solution)/shard_map/place/pallas_call | solution.py:219
  6.3 3.2 %collective-permute-done = f32[4,80,1024]{2,1,0:T(8,128)S(1)} collective-permute-done((f32[4,80,1024]{2,1,0:T(8,128)}, f32[4,80,1024]{2,1,0:T(8,128)S(1)}, u32[]{:S(2)}, u32[]{:S(2)}) %collective-permute-start) | collective-permute-done | bytes 1310752 | tf_op jit(solution)/shard_map/ppermute | solution.py:339
  9.5 1.5 fusion
  11.0 1.5 collective-permute-start.1
  12.5 2.1 %collective-permute-start.2 = (f32[80,1024]{1,0:T(8,128)S(1)}, f32[80,1024]{1,0:T(8,128)S(1)}, u32[]{:S(2)}, u32[]{:S(2)}) collective-permute-start(f32[80,1024]{1,0:T(8,128)S(1)} %get-tuple-element.45), channel_id=1, source_target_pairs={{0,64},{64,128},{128,192},{192,0},{1,65},{65,129},{129,193},{193,1... | collective-permute-start | bytes 983048 | tf_op jit(solution)/shard_map/ppermute | solution.py:339
  14.6 1.9 %collective-permute-start.4 = (bf16[16,1024]{1,0:T(8,128)(2,1)S(1)}, bf16[16,1024]{1,0:T(8,128)(2,1)S(1)}, u32[]{:S(2)}, u32[]{:S(2)}) collective-permute-start(bf16[16,1024]{1,0:T(8,128)(2,1)S(1)} %get-tuple-element.49), channel_id=1, source_target_pairs={{0,32},{32,64},{64,96},{96,128},{128,160},{160,192},{192,224},{1,3... | collective-permute-start | bytes 98312 | tf_op jit(solution)/shard_map/ppermute | solution.py:344
  16.6 3.6 %collective-permute-start.5 = (bf16[16,1024]{1,0:T(8,128)(2,1)S(1)}, bf16[16,1024]{1,0:T(8,128)(2,1)S(1)}, u32[]{:S(2)}, u32[]{:S(2)}) collective-permute-start(bf16[16,1024]{1,0:T(8,128)(2,1)S(1)} %get-tuple-element.48), channel_id=1, source_target_pairs={{32,0},{64,32},{96,64},{128,96},{160,128},{192,160},{224,192},{33,... | collective-permute-start | bytes 98312 | tf_op jit(solution)/shard_map/ppermute | solution.py:345
  21.7 4.9 %taps_table.1.w_ref = bf16[768,3072]{1,0:T(8,128)(2,1)S(1)} custom-call(f32[24,1,512]{2,1,0:T(1,128)S(1)} %reshape.48.v_ref), custom_call_target="tpu_custom_call" | custom-call | flops 20000000 | bytes 10000000 | tf_op jit(solution)/shard_map/taps_table/pallas_call | solution.py:89
  26.6 2.3 %collective-permute-done.4.tabove_ref = bf16[16,1024]{1,0:T(8,128)(2,1)S(1)} collective-permute-done((bf16[16,1024]{1,0:T(8,128)(2,1)S(1)}, bf16[16,1024]{1,0:T(8,128)(2,1)S(1)}, u32[]{:S(2)}, u32[]{:S(2)}) %collective-permute-start.4) | collective-permute-done | bytes 32800 | tf_op jit(solution)/shard_map/ppermute | solution.py:344
  28.9 0.4 collective-permute-done.2.m2_ref
  29.4 9.1 %image.1 = (bf16[48,1024]{1,0:T(8,128)(2,1)}, bf16[64,1024]{1,0:T(8,128)(2,1)S(1)}) custom-call(s32[1]{0:T(128)S(6)} %copy.28.level_ref, s32[1]{0:T(128)} %bitcast.1.shard_ref, f32[8,12]{1,0:T(8,128)S(1)} %copy-done.1, f32[80,1024]{1,0:T(8,128)S(1)} %get-tuple-element.47.m0_ref, f32[80,1024]{1,0:T(8,128)S(1)} %collective-permute-done.1.m1_ref, ...), custom_call_target="tpu_custom_call" | custom-call | flops 5000000000 | bytes 8000000 | tf_op jit(solution)/shard_map/image/pallas_call | solution.py:154
  38.5 3.0 %collective-permute-start.8 = (bf16[64,1024]{1,0:T(8,128)(2,1)S(1)}, bf16[64,1024]{1,0:T(8,128)(2,1)S(1)}, u32[]{:S(2)}, u32[]{:S(2)}) collective-permute-start(bf16[64,1024]{1,0:T(8,128)(2,1)S(1)} %get-tuple-element.26.g0), channel_id=1, source_target_pairs={{0,3},{1,0},{2,1},{3,2},{4,7},{5,4},{6,5},{7,6},{8,11},{9,8},{10,9... | collective-permute-start | bytes 393224 | tf_op jit(solution)/shard_map/ppermute | solution.py:339
  41.5 0.6 collective-permute-start.7
  42.2 1.0 collective-permute-start.6
  43.1 4.1 %collective-permute-done.8.g3 = bf16[64,1024]{1,0:T(8,128)(2,1)S(1)} collective-permute-done((bf16[64,1024]{1,0:T(8,128)(2,1)S(1)}, bf16[64,1024]{1,0:T(8,128)(2,1)S(1)}, u32[]{:S(2)}, u32[]{:S(2)}) %collective-permute-start.8) | collective-permute-done | bytes 131104 | tf_op jit(solution)/shard_map/ppermute | solution.py:339
  47.3 2.2 %collective-permute-done.7.g2 = bf16[64,1024]{1,0:T(8,128)(2,1)S(1)} collective-permute-done((bf16[64,1024]{1,0:T(8,128)(2,1)S(1)}, bf16[64,1024]{1,0:T(8,128)(2,1)S(1)}, u32[]{:S(2)}, u32[]{:S(2)}) %collective-permute-start.7) | collective-permute-done | bytes 131104 | tf_op jit(solution)/shard_map/ppermute | solution.py:339
  49.4 1.5 collective-permute-done.6.g1
  51.0 0.9 collective-permute-start.9
  51.9 1.2 collective-permute-start.10
  53.2 1.9 %collective-permute-start.11 = (bf16[4,48,1024]{2,1,0:T(8,128)(2,1)S(1)}, bf16[4,48,1024]{2,1,0:T(8,128)(2,1)S(1)}, u32[]{:S(2)}, u32[]{:S(2)}) collective-permute-start(bf16[4,48,1024]{2,1,0:T(8,128)(2,1)S(1)} %pad_maximum_fusion), channel_id=1, source_target_pairs={{0,128},{64,192},{128,0},{192,64},{1,129},{65,193},{129,1},{193,65... | collective-permute-start | bytes 1179656 | tf_op jit(solution)/shard_map/ppermute | solution.py:339
  55.0 2.4 %all-gather = bf16[8,48,1024]{2,1,0:T(8,128)(2,1)S(1)} all-gather(bf16[4,48,1024]{2,1,0:T(8,128)(2,1)S(1)} %pad_maximum_fusion), channel_id=2, replica_groups=mesh['x'=4,'core'=2,'z'=8,'y'=4] {'core'}, dimensions={0}, use_global_device_ids=true | all-gather | bytes 1179648 | tf_op jit(solution)/shard_map/all_gather | solution.py:394
  57.4 5.7 %collective-permute-done.9 = bf16[4,48,1024]{2,1,0:T(8,128)(2,1)S(1)} collective-permute-done((bf16[4,48,1024]{2,1,0:T(8,128)(2,1)S(1)}, bf16[4,48,1024]{2,1,0:T(8,128)(2,1)S(1)}, u32[]{:S(2)}, u32[]{:S(2)}) %collective-permute-start.9) | collective-permute-done | bytes 393248 | tf_op jit(solution)/shard_map/ppermute | solution.py:339
  63.1 2.4 %all-gather.1 = bf16[8,48,1024]{2,1,0:T(8,128)(2,1)S(1)} all-gather(bf16[4,48,1024]{2,1,0:T(8,128)(2,1)S(1)} %collective-permute-done.9), channel_id=3, replica_groups=mesh['x'=4,'core'=2,'z'=8,'y'=4] {'core'}, dimensions={0}, use_global_device_ids=true | all-gather | bytes 1179648 | tf_op jit(solution)/shard_map/all_gather | solution.py:394
  65.5 6.9 %collective-permute-done.10 = bf16[4,48,1024]{2,1,0:T(8,128)(2,1)S(1)} collective-permute-done((bf16[4,48,1024]{2,1,0:T(8,128)(2,1)S(1)}, bf16[4,48,1024]{2,1,0:T(8,128)(2,1)S(1)}, u32[]{:S(2)}, u32[]{:S(2)}) %collective-permute-start.10) | collective-permute-done | bytes 393248 | tf_op jit(solution)/shard_map/ppermute | solution.py:339
  72.3 2.4 %all-gather.2 = bf16[8,48,1024]{2,1,0:T(8,128)(2,1)S(1)} all-gather(bf16[4,48,1024]{2,1,0:T(8,128)(2,1)S(1)} %collective-permute-done.10), channel_id=4, replica_groups=mesh['x'=4,'core'=2,'z'=8,'y'=4] {'core'}, dimensions={0}, use_global_device_ids=true | all-gather | bytes 1179648 | tf_op jit(solution)/shard_map/all_gather | solution.py:394
  74.7 2.4 %all-gather.3 = bf16[8,48,1024]{2,1,0:T(8,128)(2,1)S(1)} all-gather(bf16[4,48,1024]{2,1,0:T(8,128)(2,1)S(1)} %collective-permute-done.11), channel_id=5, replica_groups=mesh['x'=4,'core'=2,'z'=8,'y'=4] {'core'}, dimensions={0}, use_global_device_ids=true | all-gather | bytes 1179648 | tf_op jit(solution)/shard_map/all_gather | solution.py:394
  77.0 5.2 %cut.1 = (f32[4,128,128]{2,1,0:T(8,128)S(1)}, bf16[4,128,128]{2,1,0:T(8,128)(2,1)S(1)}, bf16[4,128,128]{2,1,0:T(8,128)(2,1)S(1)}, bf16[4,128,128]{2,1,0:T(8,128)...) custom-call(s32[1]{0:T(128)} %bitcast.1.shard_ref, ...), custom_call_target="tpu_custom_call" | custom-call | flops 1000000 | bytes 12000000 | tf_op jit(solution)/shard_map/cut/pallas_call | solution.py:286
  82.2 7.1 %collective-permute-start.12 = (bf16[4,128,128]{2,1,0:T(8,128)(2,1)S(1)}, bf16[4,128,128]{2,1,0:T(8,128)(2,1)S(1)}, u32[]{:S(2)}, u32[]{:S(2)}) collective-permute-start(bf16[4,128,128]{2,1,0:T(8,128)(2,1)S(1)} %get-tuple-element.28), channel_id=1, source_target_pairs={{0,16},{4,20},{8,24},{12,28},{16,0},{20,4},{24,8},{28,12},{1,17},{... | collective-permute-start | bytes 393224 | tf_op jit(solution)/shard_map/ppermute | solution.py:339
  89.4 2.3 %collective-permute-start.13 = (bf16[4,128,128]{2,1,0:T(8,128)(2,1)S(1)}, bf16[4,128,128]{2,1,0:T(8,128)(2,1)S(1)}, u32[]{:S(2)}, u32[]{:S(2)}) collective-permute-start(bf16[4,128,128]{2,1,0:T(8,128)(2,1)S(1)} %get-tuple-element.29), channel_id=1, source_target_pairs={{0,12},{4,16},{8,20},{12,24},{16,28},{20,0},{24,4},{28,8},{1,13},{... | collective-permute-start | bytes 393224 | tf_op jit(solution)/shard_map/ppermute | solution.py:339
  91.7 2.7 %collective-permute-start.14 = (bf16[4,128,128]{2,1,0:T(8,128)(2,1)S(1)}, bf16[4,128,128]{2,1,0:T(8,128)(2,1)S(1)}, u32[]{:S(2)}, u32[]{:S(2)}) collective-permute-start(bf16[4,128,128]{2,1,0:T(8,128)(2,1)S(1)} %get-tuple-element.30), channel_id=1, source_target_pairs={{0,20},{4,24},{8,28},{12,0},{16,4},{20,8},{24,12},{28,16},{1,21},{... | collective-permute-start | bytes 393224 | tf_op jit(solution)/shard_map/ppermute | solution.py:339
  94.4 2.1 %collective-permute-start.15 = (bf16[4,128,128]{2,1,0:T(8,128)(2,1)S(1)}, bf16[4,128,128]{2,1,0:T(8,128)(2,1)S(1)}, u32[]{:S(2)}, u32[]{:S(2)}) collective-permute-start(bf16[4,128,128]{2,1,0:T(8,128)(2,1)S(1)} %get-tuple-element.31), channel_id=1, source_target_pairs={{0,8},{4,12},{8,16},{12,20},{16,24},{20,28},{24,0},{28,4},{1,9},{5... | collective-permute-start | bytes 393224 | tf_op jit(solution)/shard_map/ppermute | solution.py:339
  96.5 2.0 %collective-permute-start.16 = (bf16[4,128,128]{2,1,0:T(8,128)(2,1)S(1)}, bf16[4,128,128]{2,1,0:T(8,128)(2,1)S(1)}, u32[]{:S(2)}, u32[]{:S(2)}) collective-permute-start(bf16[4,128,128]{2,1,0:T(8,128)(2,1)S(1)} %get-tuple-element.32), channel_id=1, source_target_pairs={{0,24},{4,28},{8,0},{12,4},{16,8},{20,12},{24,16},{28,20},{1,25},{... | collective-permute-start | bytes 393224 | tf_op jit(solution)/shard_map/ppermute | solution.py:339
  98.8 7.8 %collective-permute-done.13 = bf16[4,128,128]{2,1,0:T(8,128)(2,1)S(1)} collective-permute-done((bf16[4,128,128]{2,1,0:T(8,128)(2,1)S(1)}, bf16[4,128,128]{2,1,0:T(8,128)(2,1)S(1)}, u32[]{:S(2)}, u32[]{:S(2)}) %collective-permute-start.13) | collective-permute-done | bytes 131104 | tf_op jit(solution)/shard_map/ppermute | solution.py:339
  106.6 0.7 collective-permute-start.18
  107.4 2.6 %collective-permute-done.15 = bf16[4,128,128]{2,1,0:T(8,128)(2,1)S(1)} collective-permute-done((bf16[4,128,128]{2,1,0:T(8,128)(2,1)S(1)}, bf16[4,128,128]{2,1,0:T(8,128)(2,1)S(1)}, u32[]{:S(2)}, u32[]{:S(2)}) %collective-permute-start.15) | collective-permute-done | bytes 131104 | tf_op jit(solution)/shard_map/ppermute | solution.py:339
  110.0 0.4 collective-permute-done.16
  110.4 3.1 %collective-permute-done.17 = bf16[4,128,128]{2,1,0:T(8,128)(2,1)S(1)} collective-permute-done((bf16[4,128,128]{2,1,0:T(8,128)(2,1)S(1)}, bf16[4,128,128]{2,1,0:T(8,128)(2,1)S(1)}, u32[]{:S(2)}, u32[]{:S(2)}) %collective-permute-start.17) | collective-permute-done | bytes 131104 | tf_op jit(solution)/shard_map/ppermute | solution.py:339
  113.7 3.2 %collective-permute-start.22 = (bf16[4,128,128]{2,1,0:T(8,128)(2,1)S(1)}, bf16[4,128,128]{2,1,0:T(8,128)(2,1)S(1)}, u32[]{:S(2)}, u32[]{:S(2)}) collective-permute-start(bf16[4,128,128]{2,1,0:T(8,128)(2,1)S(1)} %add_convert_fusion), channel_id=1, source_target_pairs={{0,3},{1,0},{2,1},{3,2},{4,7},{5,4},{6,5},{7,6},{8,11},{9,8},{10,9... | collective-permute-start | bytes 393224 | tf_op jit(solution)/shard_map/ppermute | solution.py:339
  116.9 3.3 %collective-permute-done.19 = bf16[4,128,128]{2,1,0:T(8,128)(2,1)S(1)} collective-permute-done((bf16[4,128,128]{2,1,0:T(8,128)(2,1)S(1)}, bf16[4,128,128]{2,1,0:T(8,128)(2,1)S(1)}, u32[]{:S(2)}, u32[]{:S(2)}) %collective-permute-start.19) | collective-permute-done | bytes 131104 | tf_op jit(solution)/shard_map/ppermute | solution.py:339
  120.2 1.8 %collective-permute-start.20 = (bf16[8,128,128]{2,1,0:T(8,128)(2,1)S(1)}, bf16[8,128,128]{2,1,0:T(8,128)(2,1)S(1)}, u32[]{:S(2)}, u32[]{:S(2)}) collective-permute-start(bf16[8,128,128]{2,1,0:T(8,128)(2,1)S(1)} %pad_maximum_fusion.1.refs_0_), channel_id=1, source_target_pairs={{0,4},{4,8},{8,12},{12,16},{16,20},{20,24},{24,28},{28,0},{1,5},{5... | collective-permute-start | bytes 786440 | tf_op jit(solution)/shard_map/ppermute | solution.py:339
  122.0 1.5 collective-permute-start.21
  123.6 2.6 %collective-permute-start.27 = (bf16[8,128,128]{2,1,0:T(8,128)(2,1)S(1)}, bf16[8,128,128]{2,1,0:T(8,128)(2,1)S(1)}, u32[]{:S(2)}, u32[]{:S(2)}) collective-permute-start(bf16[8,128,128]{2,1,0:T(8,128)(2,1)S(1)} %constant_dynamic-update-slice_fusion.refs_1_), channel_id=1, source_target_pairs={{0,28},{4,0},{8,4},{12,8},{16,12},{20,16},{24,20},{28,24},{1,29},{... | collective-permute-start | bytes 786440 | tf_op jit(solution)/shard_map/ppermute | solution.py:339
  126.2 1.0 deposit.5.refs_4_
  127.2 2.3 %collective-permute-done.20.refs_0_ = bf16[8,128,128]{2,1,0:T(8,128)(2,1)S(1)} collective-permute-done((bf16[8,128,128]{2,1,0:T(8,128)(2,1)S(1)}, bf16[8,128,128]{2,1,0:T(8,128)(2,1)S(1)}, u32[]{:S(2)}, u32[]{:S(2)}) %collective-permute-start.20) | collective-permute-done | bytes 262176 | tf_op jit(solution)/shard_map/ppermute | solution.py:339
  129.5 1.7 %collective-permute-done.21.refs_1_ = bf16[8,128,128]{2,1,0:T(8,128)(2,1)S(1)} collective-permute-done((bf16[8,128,128]{2,1,0:T(8,128)(2,1)S(1)}, bf16[8,128,128]{2,1,0:T(8,128)(2,1)S(1)}, u32[]{:S(2)}, u32[]{:S(2)}) %collective-permute-start.21) | collective-permute-done | bytes 262176 | tf_op jit(solution)/shard_map/ppermute | solution.py:339
  131.3 0.4 collective-permute-start.24
  131.6 2.9 %collective-permute-start.25 = (bf16[8,128,128]{2,1,0:T(8,128)(2,1)S(1)}, bf16[8,128,128]{2,1,0:T(8,128)(2,1)S(1)}, u32[]{:S(2)}, u32[]{:S(2)}) collective-permute-start(bf16[8,128,128]{2,1,0:T(8,128)(2,1)S(1)} %collective-permute-done.21.refs_1_), channel_id=1, source_target_pairs={{0,28},{4,0},{8,4},{12,8},{16,12},{20,16},{24,20},{28,24},{1,29},{... | collective-permute-start | bytes 786440 | tf_op jit(solution)/shard_map/ppermute | solution.py:339
  134.5 2.4 %collective-permute-done.27.refs_3_ = bf16[8,128,128]{2,1,0:T(8,128)(2,1)S(1)} collective-permute-done((bf16[8,128,128]{2,1,0:T(8,128)(2,1)S(1)}, bf16[8,128,128]{2,1,0:T(8,128)(2,1)S(1)}, u32[]{:S(2)}, u32[]{:S(2)}) %collective-permute-start.27) | collective-permute-done | bytes 262176 | tf_op jit(solution)/shard_map/ppermute | solution.py:339
  136.9 2.8 %collective-permute-start.31 = (bf16[8,128,128]{2,1,0:T(8,128)(2,1)S(1)}, bf16[8,128,128]{2,1,0:T(8,128)(2,1)S(1)}, u32[]{:S(2)}, u32[]{:S(2)}) collective-permute-start(bf16[8,128,128]{2,1,0:T(8,128)(2,1)S(1)} %collective-permute-done.27.refs_3_), channel_id=1, source_target_pairs={{0,28},{4,0},{8,4},{12,8},{16,12},{20,16},{24,20},{28,24},{1,29},{... | collective-permute-start | bytes 786440 | tf_op jit(solution)/shard_map/ppermute | solution.py:339
  139.6 1.4 deposit.6.refs_4_
  141.2 1.3 collective-permute-done.25.refs_1_
  142.5 0.6 collective-permute-start.28
  143.1 2.6 %collective-permute-start.29 = (bf16[8,128,128]{2,1,0:T(8,128)(2,1)S(1)}, bf16[8,128,128]{2,1,0:T(8,128)(2,1)S(1)}, u32[]{:S(2)}, u32[]{:S(2)}) collective-permute-start(bf16[8,128,128]{2,1,0:T(8,128)(2,1)S(1)} %collective-permute-done.25.refs_1_), channel_id=1, source_target_pairs={{0,28},{4,0},{8,4},{12,8},{16,12},{20,16},{24,20},{28,24},{1,29},{... | collective-permute-start | bytes 786440 | tf_op jit(solution)/shard_map/ppermute | solution.py:339
  145.7 2.4 %collective-permute-done.31.refs_3_ = bf16[8,128,128]{2,1,0:T(8,128)(2,1)S(1)} collective-permute-done((bf16[8,128,128]{2,1,0:T(8,128)(2,1)S(1)}, bf16[8,128,128]{2,1,0:T(8,128)(2,1)S(1)}, u32[]{:S(2)}, u32[]{:S(2)}) %collective-permute-start.31) | collective-permute-done | bytes 262176 | tf_op jit(solution)/shard_map/ppermute | solution.py:339
  148.1 2.8 %collective-permute-start.33 = (bf16[8,128,128]{2,1,0:T(8,128)(2,1)S(1)}, bf16[8,128,128]{2,1,0:T(8,128)(2,1)S(1)}, u32[]{:S(2)}, u32[]{:S(2)}) collective-permute-start(bf16[8,128,128]{2,1,0:T(8,128)(2,1)S(1)} %collective-permute-done.31.refs_3_), channel_id=1, source_target_pairs={{0,28},{4,0},{8,4},{12,8},{16,12},{20,16},{24,20},{28,24},{1,29},{... | collective-permute-start | bytes 786440 | tf_op jit(solution)/shard_map/ppermute | solution.py:339
  150.9 1.4 deposit.7.refs_4_
  152.4 0.5 collective-permute-done.29.refs_1_
  152.9 1.2 collective-permute-start.32
  154.1 2.0 %collective-permute-done.33.refs_3_ = bf16[8,128,128]{2,1,0:T(8,128)(2,1)S(1)} collective-permute-done((bf16[8,128,128]{2,1,0:T(8,128)(2,1)S(1)}, bf16[8,128,128]{2,1,0:T(8,128)(2,1)S(1)}, u32[]{:S(2)}, u32[]{:S(2)}) %collective-permute-start.33) | collective-permute-done | bytes 262176 | tf_op jit(solution)/shard_map/ppermute | solution.py:339
  156.2 3.7 %collective-permute-start.34 = (bf16[8,128,128]{2,1,0:T(8,128)(2,1)S(1)}, bf16[8,128,128]{2,1,0:T(8,128)(2,1)S(1)}, u32[]{:S(2)}, u32[]{:S(2)}) collective-permute-start(bf16[8,128,128]{2,1,0:T(8,128)(2,1)S(1)} %collective-permute-done.33.refs_3_), channel_id=1, source_target_pairs={{0,28},{4,0},{8,4},{12,8},{16,12},{20,16},{24,20},{28,24},{1,29},{... | collective-permute-start | bytes 786440 | tf_op jit(solution)/shard_map/ppermute | solution.py:339
  159.9 1.4 deposit.8.refs_2_
  161.3 1.2 collective-permute-done.32.refs_0_
  162.5 1.3 collective-permute-done.34.refs_1_
  163.8 1.0 deposit.9
  (46 shorter events, 1.8 us)
Async XLA Ops:
  0.6 14.0 %copy-start = (bf16[1,48,1024]{2,1,0:T(8,128)(2,1)S(1)}, bf16[1,48,1024]{2,1,0:T(8,128)(2,1)}, u32[]{:S(2)}) copy-start(bf16[1,48,1024]{2,1,0:T(8,128)(2,1)} %param.15) | copy-start | bytes 294916
  0.6 19.6 %copy-start.3 = (bf16[24,225]{1,0:T(8,128)(2,1)S(1)}, bf16[24,225]{1,0:T(8,128)(2,1)}, u32[]{:S(2)}) copy-start(bf16[24,225]{1,0:T(8,128)(2,1)} %param.14) | copy-start | bytes 32404
  0.7 28.7 %copy-start.1 = (f32[8,12]{1,0:T(8,128)S(1)}, f32[8,12]{1,0:T(8,128)}, u32[]{:S(2)}) copy-start(f32[8,12]{1,0:T(8,128)} %wgt_ref.1) | copy-start | bytes 1156
  6.2 23.2 %copy-start.2 = (s32[1,128]{1,0:T(1,128)S(1)}, s32[1,128]{1,0:T(1,128)}, u32[]{:S(2)}) copy-start(s32[1,128]{1,0:T(1,128)} %get-tuple-element.25.info_ref) | copy-start | bytes 1540
  6.2 3.3 %collective-permute-start = (f32[4,80,1024]{2,1,0:T(8,128)}, f32[4,80,1024]{2,1,0:T(8,128)S(1)}, u32[]{:S(2)}, u32[]{:S(2)}) collective-permute-start(f32[4,80,1024]{2,1,0:T(8,128)} %get-tuple-element.24), channel_id=1, source_target_pairs={{0,32},{32,0},{1,33},{33,1},{2,34},{34,2},{3,35},{35,3},{4,36},{36... | collective-permute-start | bytes 3932168 | tf_op jit(solution)/shard_map/ppermute | solution.py:339
  11.0 17.9 %collective-permute-start.1 = (f32[80,1024]{1,0:T(8,128)S(1)}, f32[80,1024]{1,0:T(8,128)S(1)}, u32[]{:S(2)}, u32[]{:S(2)}) collective-permute-start(f32[80,1024]{1,0:T(8,128)S(1)} %get-tuple-element.46), channel_id=1, source_target_pairs={{0,128},{64,192},{128,0},{192,64},{1,129},{65,193},{129,1},{193,65... | collective-permute-start | bytes 983048 | tf_op jit(solution)/shard_map/ppermute | solution.py:339
  12.5 16.8 %collective-permute-start.2 = (f32[80,1024]{1,0:T(8,128)S(1)}, f32[80,1024]{1,0:T(8,128)S(1)}, u32[]{:S(2)}, u32[]{:S(2)}) collective-permute-start(f32[80,1024]{1,0:T(8,128)S(1)} %get-tuple-element.45), channel_id=1, source_target_pairs={{0,64},{64,128},{128,192},{192,0},{1,65},{65,129},{129,193},{193,1... | collective-permute-start | bytes 983048 | tf_op jit(solution)/shard_map/ppermute | solution.py:339
  14.6 14.8 %collective-permute-start.3 = (f32[80,1024]{1,0:T(8,128)S(1)}, f32[80,1024]{1,0:T(8,128)S(1)}, u32[]{:S(2)}, u32[]{:S(2)}) collective-permute-start(f32[80,1024]{1,0:T(8,128)S(1)} %get-tuple-element.44), channel_id=1, source_target_pairs={{0,192},{64,0},{128,64},{192,128},{1,193},{65,1},{129,65},{193,129... | collective-permute-start | bytes 983048 | tf_op jit(solution)/shard_map/ppermute | solution.py:339
  14.6 14.2 %collective-permute-start.4 = (bf16[16,1024]{1,0:T(8,128)(2,1)S(1)}, bf16[16,1024]{1,0:T(8,128)(2,1)S(1)}, u32[]{:S(2)}, u32[]{:S(2)}) collective-permute-start(bf16[16,1024]{1,0:T(8,128)(2,1)S(1)} %get-tuple-element.49), channel_id=1, source_target_pairs={{0,32},{32,64},{64,96},{96,128},{128,160},{160,192},{192,224},{1,3... | collective-permute-start | bytes 98312 | tf_op jit(solution)/shard_map/ppermute | solution.py:344
  16.6 12.3 %collective-permute-start.5 = (bf16[16,1024]{1,0:T(8,128)(2,1)S(1)}, bf16[16,1024]{1,0:T(8,128)(2,1)S(1)}, u32[]{:S(2)}, u32[]{:S(2)}) collective-permute-start(bf16[16,1024]{1,0:T(8,128)(2,1)S(1)} %get-tuple-element.48), channel_id=1, source_target_pairs={{32,0},{64,32},{96,64},{128,96},{160,128},{192,160},{224,192},{33,... | collective-permute-start | bytes 98312 | tf_op jit(solution)/shard_map/ppermute | solution.py:345
  38.5 8.8 %collective-permute-start.8 = (bf16[64,1024]{1,0:T(8,128)(2,1)S(1)}, bf16[64,1024]{1,0:T(8,128)(2,1)S(1)}, u32[]{:S(2)}, u32[]{:S(2)}) collective-permute-start(bf16[64,1024]{1,0:T(8,128)(2,1)S(1)} %get-tuple-element.26.g0), channel_id=1, source_target_pairs={{0,3},{1,0},{2,1},{3,2},{4,7},{5,4},{6,5},{7,6},{8,11},{9,8},{10,9... | collective-permute-start | bytes 393224 | tf_op jit(solution)/shard_map/ppermute | solution.py:339
  41.5 7.9 %collective-permute-start.7 = (bf16[64,1024]{1,0:T(8,128)(2,1)S(1)}, bf16[64,1024]{1,0:T(8,128)(2,1)S(1)}, u32[]{:S(2)}, u32[]{:S(2)}) collective-permute-start(bf16[64,1024]{1,0:T(8,128)(2,1)S(1)} %get-tuple-element.26.g0), channel_id=1, source_target_pairs={{0,2},{1,3},{2,0},{3,1},{4,6},{5,7},{6,4},{7,5},{8,10},{9,11},{10,... | collective-permute-start | bytes 393224 | tf_op jit(solution)/shard_map/ppermute | solution.py:339
  42.2 8.8 %collective-permute-start.6 = (bf16[64,1024]{1,0:T(8,128)(2,1)S(1)}, bf16[64,1024]{1,0:T(8,128)(2,1)S(1)}, u32[]{:S(2)}, u32[]{:S(2)}) collective-permute-start(bf16[64,1024]{1,0:T(8,128)(2,1)S(1)} %get-tuple-element.26.g0), channel_id=1, source_target_pairs={{0,1},{1,2},{2,3},{3,0},{4,5},{5,6},{6,7},{7,4},{8,9},{9,10},{10,1... | collective-permute-start | bytes 393224 | tf_op jit(solution)/shard_map/ppermute | solution.py:339
  51.0 12.1 %collective-permute-start.9 = (bf16[4,48,1024]{2,1,0:T(8,128)(2,1)S(1)}, bf16[4,48,1024]{2,1,0:T(8,128)(2,1)S(1)}, u32[]{:S(2)}, u32[]{:S(2)}) collective-permute-start(bf16[4,48,1024]{2,1,0:T(8,128)(2,1)S(1)} %pad_maximum_fusion), channel_id=1, source_target_pairs={{0,64},{64,128},{128,192},{192,0},{1,65},{65,129},{129,193},{193,1... | collective-permute-start | bytes 1179656 | tf_op jit(solution)/shard_map/ppermute | solution.py:339
  51.9 20.4 %collective-permute-start.10 = (bf16[4,48,1024]{2,1,0:T(8,128)(2,1)S(1)}, bf16[4,48,1024]{2,1,0:T(8,128)(2,1)S(1)}, u32[]{:S(2)}, u32[]{:S(2)}) collective-permute-start(bf16[4,48,1024]{2,1,0:T(8,128)(2,1)S(1)} %pad_maximum_fusion), channel_id=1, source_target_pairs={{0,192},{64,0},{128,64},{192,128},{1,193},{65,1},{129,65},{193,129... | collective-permute-start | bytes 1179656 | tf_op jit(solution)/shard_map/ppermute | solution.py:339
  53.2 21.5 %collective-permute-start.11 = (bf16[4,48,1024]{2,1,0:T(8,128)(2,1)S(1)}, bf16[4,48,1024]{2,1,0:T(8,128)(2,1)S(1)}, u32[]{:S(2)}, u32[]{:S(2)}) collective-permute-start(bf16[4,48,1024]{2,1,0:T(8,128)(2,1)S(1)} %pad_maximum_fusion), channel_id=1, source_target_pairs={{0,128},{64,192},{128,0},{192,64},{1,129},{65,193},{129,1},{193,65... | collective-permute-start | bytes 1179656 | tf_op jit(solution)/shard_map/ppermute | solution.py:339
  82.2 16.3 %collective-permute-start.12 = (bf16[4,128,128]{2,1,0:T(8,128)(2,1)S(1)}, bf16[4,128,128]{2,1,0:T(8,128)(2,1)S(1)}, u32[]{:S(2)}, u32[]{:S(2)}) collective-permute-start(bf16[4,128,128]{2,1,0:T(8,128)(2,1)S(1)} %get-tuple-element.28), channel_id=1, source_target_pairs={{0,16},{4,20},{8,24},{12,28},{16,0},{20,4},{24,8},{28,12},{1,17},{... | collective-permute-start | bytes 393224 | tf_op jit(solution)/shard_map/ppermute | solution.py:339
  89.4 17.3 %collective-permute-start.13 = (bf16[4,128,128]{2,1,0:T(8,128)(2,1)S(1)}, bf16[4,128,128]{2,1,0:T(8,128)(2,1)S(1)}, u32[]{:S(2)}, u32[]{:S(2)}) collective-permute-start(bf16[4,128,128]{2,1,0:T(8,128)(2,1)S(1)} %get-tuple-element.29), channel_id=1, source_target_pairs={{0,12},{4,16},{8,20},{12,24},{16,28},{20,0},{24,4},{28,8},{1,13},{... | collective-permute-start | bytes 393224 | tf_op jit(solution)/shard_map/ppermute | solution.py:339
  91.7 15.7 %collective-permute-start.14 = (bf16[4,128,128]{2,1,0:T(8,128)(2,1)S(1)}, bf16[4,128,128]{2,1,0:T(8,128)(2,1)S(1)}, u32[]{:S(2)}, u32[]{:S(2)}) collective-permute-start(bf16[4,128,128]{2,1,0:T(8,128)(2,1)S(1)} %get-tuple-element.30), channel_id=1, source_target_pairs={{0,20},{4,24},{8,28},{12,0},{16,4},{20,8},{24,12},{28,16},{1,21},{... | collective-permute-start | bytes 393224 | tf_op jit(solution)/shard_map/ppermute | solution.py:339
  94.4 15.6 %collective-permute-start.15 = (bf16[4,128,128]{2,1,0:T(8,128)(2,1)S(1)}, bf16[4,128,128]{2,1,0:T(8,128)(2,1)S(1)}, u32[]{:S(2)}, u32[]{:S(2)}) collective-permute-start(bf16[4,128,128]{2,1,0:T(8,128)(2,1)S(1)} %get-tuple-element.31), channel_id=1, source_target_pairs={{0,8},{4,12},{8,16},{12,20},{16,24},{20,28},{24,0},{28,4},{1,9},{5... | collective-permute-start | bytes 393224 | tf_op jit(solution)/shard_map/ppermute | solution.py:339
  96.5 13.9 %collective-permute-start.16 = (bf16[4,128,128]{2,1,0:T(8,128)(2,1)S(1)}, bf16[4,128,128]{2,1,0:T(8,128)(2,1)S(1)}, u32[]{:S(2)}, u32[]{:S(2)}) collective-permute-start(bf16[4,128,128]{2,1,0:T(8,128)(2,1)S(1)} %get-tuple-element.32), channel_id=1, source_target_pairs={{0,24},{4,28},{8,0},{12,4},{16,8},{20,12},{24,16},{28,20},{1,25},{... | collective-permute-start | bytes 393224 | tf_op jit(solution)/shard_map/ppermute | solution.py:339
  98.5 14.9 %collective-permute-start.17 = (bf16[4,128,128]{2,1,0:T(8,128)(2,1)S(1)}, bf16[4,128,128]{2,1,0:T(8,128)(2,1)S(1)}, u32[]{:S(2)}, u32[]{:S(2)}) collective-permute-start(bf16[4,128,128]{2,1,0:T(8,128)(2,1)S(1)} %get-tuple-element.33), channel_id=1, source_target_pairs={{0,4},{4,8},{8,12},{12,16},{16,20},{20,24},{24,28},{28,0},{1,5},{5... | collective-permute-start | bytes 393224 | tf_op jit(solution)/shard_map/ppermute | solution.py:339
  106.6 6.9 %collective-permute-start.18 = (bf16[4,128,128]{2,1,0:T(8,128)(2,1)S(1)}, bf16[4,128,128]{2,1,0:T(8,128)(2,1)S(1)}, u32[]{:S(2)}, u32[]{:S(2)}) collective-permute-start(bf16[4,128,128]{2,1,0:T(8,128)(2,1)S(1)} %get-tuple-element.34), channel_id=1, source_target_pairs={{0,28},{4,0},{8,4},{12,8},{16,12},{20,16},{24,20},{28,24},{1,29},{... | collective-permute-start | bytes 393224 | tf_op jit(solution)/shard_map/ppermute | solution.py:339
  113.6 6.6 %collective-permute-start.19 = (bf16[4,128,128]{2,1,0:T(8,128)(2,1)S(1)}, bf16[4,128,128]{2,1,0:T(8,128)(2,1)S(1)}, u32[]{:S(2)}, u32[]{:S(2)}) collective-permute-start(bf16[4,128,128]{2,1,0:T(8,128)(2,1)S(1)} %add_convert_fusion), channel_id=1, source_target_pairs={{0,1},{1,2},{2,3},{3,0},{4,5},{5,6},{6,7},{7,4},{8,9},{9,10},{10,1... | collective-permute-start | bytes 393224 | tf_op jit(solution)/shard_map/ppermute | solution.py:339
  113.7 9.9 %collective-permute-start.22 = (bf16[4,128,128]{2,1,0:T(8,128)(2,1)S(1)}, bf16[4,128,128]{2,1,0:T(8,128)(2,1)S(1)}, u32[]{:S(2)}, u32[]{:S(2)}) collective-permute-start(bf16[4,128,128]{2,1,0:T(8,128)(2,1)S(1)} %add_convert_fusion), channel_id=1, source_target_pairs={{0,3},{1,0},{2,1},{3,2},{4,7},{5,4},{6,5},{7,6},{8,11},{9,8},{10,9... | collective-permute-start | bytes 393224 | tf_op jit(solution)/shard_map/ppermute | solution.py:339
  116.9 6.6 %collective-permute-start.23 = (bf16[4,128,128]{2,1,0:T(8,128)(2,1)S(1)}, bf16[4,128,128]{2,1,0:T(8,128)(2,1)S(1)}, u32[]{:S(2)}, u32[]{:S(2)}) collective-permute-start(bf16[4,128,128]{2,1,0:T(8,128)(2,1)S(1)} %add_convert_fusion), channel_id=1, source_target_pairs={{0,2},{1,3},{2,0},{3,1},{4,6},{5,7},{6,4},{7,5},{8,10},{9,11},{10,... | collective-permute-start | bytes 393224 | tf_op jit(solution)/shard_map/ppermute | solution.py:339
  120.2 9.3 %collective-permute-start.20 = (bf16[8,128,128]{2,1,0:T(8,128)(2,1)S(1)}, bf16[8,128,128]{2,1,0:T(8,128)(2,1)S(1)}, u32[]{:S(2)}, u32[]{:S(2)}) collective-permute-start(bf16[8,128,128]{2,1,0:T(8,128)(2,1)S(1)} %pad_maximum_fusion.1.refs_0_), channel_id=1, source_target_pairs={{0,4},{4,8},{8,12},{12,16},{16,20},{20,24},{24,28},{28,0},{1,5},{5... | collective-permute-start | bytes 786440 | tf_op jit(solution)/shard_map/ppermute | solution.py:339
  122.0 9.2 %collective-permute-start.21 = (bf16[8,128,128]{2,1,0:T(8,128)(2,1)S(1)}, bf16[8,128,128]{2,1,0:T(8,128)(2,1)S(1)}, u32[]{:S(2)}, u32[]{:S(2)}) collective-permute-start(bf16[8,128,128]{2,1,0:T(8,128)(2,1)S(1)} %pad_maximum_fusion.1.refs_0_), channel_id=1, source_target_pairs={{0,28},{4,0},{8,4},{12,8},{16,12},{20,16},{24,20},{28,24},{1,29},{... | collective-permute-start | bytes 786440 | tf_op jit(solution)/shard_map/ppermute | solution.py:339
  123.6 13.3 %collective-permute-start.27 = (bf16[8,128,128]{2,1,0:T(8,128)(2,1)S(1)}, bf16[8,128,128]{2,1,0:T(8,128)(2,1)S(1)}, u32[]{:S(2)}, u32[]{:S(2)}) collective-permute-start(bf16[8,128,128]{2,1,0:T(8,128)(2,1)S(1)} %constant_dynamic-update-slice_fusion.refs_1_), channel_id=1, source_target_pairs={{0,28},{4,0},{8,4},{12,8},{16,12},{20,16},{24,20},{28,24},{1,29},{... | collective-permute-start | bytes 786440 | tf_op jit(solution)/shard_map/ppermute | solution.py:339
  126.2 13.5 %collective-permute-start.26 = (bf16[8,128,128]{2,1,0:T(8,128)(2,1)S(1)}, bf16[8,128,128]{2,1,0:T(8,128)(2,1)S(1)}, u32[]{:S(2)}, u32[]{:S(2)}) collective-permute-start(bf16[8,128,128]{2,1,0:T(8,128)(2,1)S(1)} %constant_dynamic-update-slice_fusion.refs_1_), channel_id=1, source_target_pairs={{0,4},{4,8},{8,12},{12,16},{16,20},{20,24},{24,28},{28,0},{1,5},{5... | collective-permute-start | bytes 786440 | tf_op jit(solution)/shard_map/ppermute | solution.py:339
  131.3 9.9 %collective-permute-start.24 = (bf16[8,128,128]{2,1,0:T(8,128)(2,1)S(1)}, bf16[8,128,128]{2,1,0:T(8,128)(2,1)S(1)}, u32[]{:S(2)}, u32[]{:S(2)}) collective-permute-start(bf16[8,128,128]{2,1,0:T(8,128)(2,1)S(1)} %collective-permute-done.20.refs_0_), channel_id=1, source_target_pairs={{0,4},{4,8},{8,12},{12,16},{16,20},{20,24},{24,28},{28,0},{1,5},{5... | collective-permute-start | bytes 786440 | tf_op jit(solution)/shard_map/ppermute | solution.py:339
  131.6 10.9 %collective-permute-start.25 = (bf16[8,128,128]{2,1,0:T(8,128)(2,1)S(1)}, bf16[8,128,128]{2,1,0:T(8,128)(2,1)S(1)}, u32[]{:S(2)}, u32[]{:S(2)}) collective-permute-start(bf16[8,128,128]{2,1,0:T(8,128)(2,1)S(1)} %collective-permute-done.21.refs_1_), channel_id=1, source_target_pairs={{0,28},{4,0},{8,4},{12,8},{16,12},{20,16},{24,20},{28,24},{1,29},{... | collective-permute-start | bytes 786440 | tf_op jit(solution)/shard_map/ppermute | solution.py:339
  136.9 11.2 %collective-permute-start.31 = (bf16[8,128,128]{2,1,0:T(8,128)(2,1)S(1)}, bf16[8,128,128]{2,1,0:T(8,128)(2,1)S(1)}, u32[]{:S(2)}, u32[]{:S(2)}) collective-permute-start(bf16[8,128,128]{2,1,0:T(8,128)(2,1)S(1)} %collective-permute-done.27.refs_3_), channel_id=1, source_target_pairs={{0,28},{4,0},{8,4},{12,8},{16,12},{20,16},{24,20},{28,24},{1,29},{... | collective-permute-start | bytes 786440 | tf_op jit(solution)/shard_map/ppermute | solution.py:339
  139.6 11.2 %collective-permute-start.30 = (bf16[8,128,128]{2,1,0:T(8,128)(2,1)S(1)}, bf16[8,128,128]{2,1,0:T(8,128)(2,1)S(1)}, u32[]{:S(2)}, u32[]{:S(2)}) collective-permute-start(bf16[8,128,128]{2,1,0:T(8,128)(2,1)S(1)} %collective-permute-done.26.refs_2_), channel_id=1, source_target_pairs={{0,4},{4,8},{8,12},{12,16},{16,20},{20,24},{24,28},{28,0},{1,5},{5... | collective-permute-start | bytes 786440 | tf_op jit(solution)/shard_map/ppermute | solution.py:339
  142.5 9.9 %collective-permute-start.28 = (bf16[8,128,128]{2,1,0:T(8,128)(2,1)S(1)}, bf16[8,128,128]{2,1,0:T(8,128)(2,1)S(1)}, u32[]{:S(2)}, u32[]{:S(2)}) collective-permute-start(bf16[8,128,128]{2,1,0:T(8,128)(2,1)S(1)} %collective-permute-done.24.refs_0_), channel_id=1, source_target_pairs={{0,4},{4,8},{8,12},{12,16},{16,20},{20,24},{24,28},{28,0},{1,5},{5... | collective-permute-start | bytes 786440 | tf_op jit(solution)/shard_map/ppermute | solution.py:339
  143.1 9.8 %collective-permute-start.29 = (bf16[8,128,128]{2,1,0:T(8,128)(2,1)S(1)}, bf16[8,128,128]{2,1,0:T(8,128)(2,1)S(1)}, u32[]{:S(2)}, u32[]{:S(2)}) collective-permute-start(bf16[8,128,128]{2,1,0:T(8,128)(2,1)S(1)} %collective-permute-done.25.refs_1_), channel_id=1, source_target_pairs={{0,28},{4,0},{8,4},{12,8},{16,12},{20,16},{24,20},{28,24},{1,29},{... | collective-permute-start | bytes 786440 | tf_op jit(solution)/shard_map/ppermute | solution.py:339
  148.1 8.1 %collective-permute-start.33 = (bf16[8,128,128]{2,1,0:T(8,128)(2,1)S(1)}, bf16[8,128,128]{2,1,0:T(8,128)(2,1)S(1)}, u32[]{:S(2)}, u32[]{:S(2)}) collective-permute-start(bf16[8,128,128]{2,1,0:T(8,128)(2,1)S(1)} %collective-permute-done.31.refs_3_), channel_id=1, source_target_pairs={{0,28},{4,0},{8,4},{12,8},{16,12},{20,16},{24,20},{28,24},{1,29},{... | collective-permute-start | bytes 786440 | tf_op jit(solution)/shard_map/ppermute | solution.py:339
  150.9 9.0 %collective-permute-start.35 = (bf16[8,128,128]{2,1,0:T(8,128)(2,1)S(1)}, bf16[8,128,128]{2,1,0:T(8,128)(2,1)S(1)}, u32[]{:S(2)}, u32[]{:S(2)}) collective-permute-start(bf16[8,128,128]{2,1,0:T(8,128)(2,1)S(1)} %collective-permute-done.30.refs_2_), channel_id=1, source_target_pairs={{0,4},{4,8},{8,12},{12,16},{16,20},{20,24},{24,28},{28,0},{1,5},{5... | collective-permute-start | bytes 786440 | tf_op jit(solution)/shard_map/ppermute | solution.py:339
  152.9 9.5 %collective-permute-start.32 = (bf16[8,128,128]{2,1,0:T(8,128)(2,1)S(1)}, bf16[8,128,128]{2,1,0:T(8,128)(2,1)S(1)}, u32[]{:S(2)}, u32[]{:S(2)}) collective-permute-start(bf16[8,128,128]{2,1,0:T(8,128)(2,1)S(1)} %collective-permute-done.28.refs_0_), channel_id=1, source_target_pairs={{0,4},{4,8},{8,12},{12,16},{16,20},{20,24},{24,28},{28,0},{1,5},{5... | collective-permute-start | bytes 786440 | tf_op jit(solution)/shard_map/ppermute | solution.py:339
  156.2 7.6 %collective-permute-start.34 = (bf16[8,128,128]{2,1,0:T(8,128)(2,1)S(1)}, bf16[8,128,128]{2,1,0:T(8,128)(2,1)S(1)}, u32[]{:S(2)}, u32[]{:S(2)}) collective-permute-start(bf16[8,128,128]{2,1,0:T(8,128)(2,1)S(1)} %collective-permute-done.33.refs_3_), channel_id=1, source_target_pairs={{0,28},{4,0},{8,4},{12,8},{16,12},{20,16},{24,20},{28,24},{1,29},{... | collective-permute-start | bytes 786440 | tf_op jit(solution)/shard_map/ppermute | solution.py:339
where the time goes:
time: 166 us; the launch traced here: 165 us
  starting transfers between devices  61.2 us (37%)
  waiting for transfers between devices  59 us (36%)
  Pallas kernels  31 us (19%)
  blocking collectives  9.43 us (6%)
  between operations  1.73 us (1%)
  other arithmetic  1.69 us (1%)
    ppermute x34, waiting for transfers between devices, shift(): return lax.ppermute(v, axis, [(i, (i + by) % n) for i in range(n)])  56.8 us
    ppermute x34, starting transfers between devices, shift(): return lax.ppermute(v, axis, [(i, (i + by) % n) for i in range(n)])  55.7 us
    all_gather x4, blocking collectives, body(): bands = [lax.all_gather(v, 'core') for v in (own, up, down, far)]  9.43 us
    pallas_call x1, Pallas kernels, image(): pl.pallas_call(image_kernel, out_shape=(jax.ShapeDtypeStruct((TR, TC), BF...  9.11 us
    pallas_call x5, Pallas kernels, deposit(): pl.pallas_call(functools.partial(deposit_kernel, places, n + len(old)), o...  6.29 us
    pallas_call x1, Pallas kernels, place(): pl.pallas_call(place_kernel, out_shape=(bands, bands, jax.ShapeDtypeStruc...  5.52 us
    pallas_call x1, Pallas kernels, cut(): pl.pallas_call(cut_kernel, out_shape=[jax.ShapeDtypeStruct(slot, F32)] +...  5.16 us
    pallas_call x1, Pallas kernels, make_table(): pl.pallas_call(table_kernel, out_shape=jax.ShapeDtypeStruct((K, 2 * KERN...  4.94 us
  transfers between devices with their start and end apart: 36, of which 25 were waited for; matrix products, arithmetic and copies ran while one was open for 1% of the time, Pallas kernels for 6%

commit v1 on v0

--- a/solution.py
+++ b/solution.py
@@ -100,7 +100,8 @@
 def image_kernel(level_ref, shard_ref, wgt_ref, m0_ref, m1_ref, m2_ref, m3_ref, tabove_ref, tmid_ref, tbelow_ref, info_ref, w_ref,
                  resist_ref, grad_ref, lhs_ref, fields_ref, cot_ref):
     level_at = level_ref[0]
-    x = (m0_ref[...] + m1_ref[...] + m2_ref[...] + m3_ref[...]).astype(BF).astype(F32)
+    x = m0_ref[...] + m1_ref[...].astype(F32) + m2_ref[...].astype(F32) + m3_ref[...].astype(F32)
+    x = x.astype(BF).astype(F32)
     x = pltpu.roll(x, 8 * MROWB - 1, 0)
     x = jnp.concatenate([x, jnp.zeros((8 * MROWB, 128), F32)], axis=1)
     x = pltpu.roll(x, H, 1)
@@ -168,7 +169,7 @@
 LEAD = 16
 EXT = TR + 2 * LEAD
 INFO = 128
-PLACE_GRANT = 58
+PLACE_GRANT = 56
 
 
 def place_kernel(shard_ref, ids_hbm, rows_hbm, cols_hbm, masters_hbm, mine_ref, theirs_ref, info_ref, scalars, panels, canvas, sem, info_sem):
@@ -189,6 +190,8 @@
         info_ref[0, i] = 0
     canvas[...] = jnp.zeros(canvas.shape, F32)
     lane = lax.broadcasted_iota(jnp.int32, (P_SIZE, 128), 1)
+    sub = lax.broadcasted_iota(jnp.int32, (P_SIZE // 8 + 1, 8, 256), 1)
+    none = jnp.zeros((1, 8, 256), F32)
     for i in range(INST_DEV):
         copies[i].wait()
         p = panels[i].astype(BF).astype(F32)
@@ -198,27 +201,29 @@
         p = pltpu.roll(p, d, 1)
         left = jnp.where(lane >= d, p, 0.0)
         right = jnp.where(lane >= d, 0.0, p)
-        full = jnp.concatenate([jnp.concatenate([left, right], axis=1), jnp.zeros((8, 256), F32)], axis=0)
         r = scalars[1, 0, i] + LEAD
         r0 = (r // 8) * 8
-        full = pltpu.roll(full, r - r0, 0)
+        full = jnp.concatenate([left, right], axis=1).reshape(P_SIZE // 8, 8, 256)
+        full = pltpu.roll(full, r - r0, 1)
+        full = jnp.where(sub >= r - r0, jnp.concatenate([full, none], axis=0), jnp.concatenate([none, full], axis=0))
+        full = full.reshape(P_SIZE + 8, 256)
         at = (pl.ds(pl.multiple_of(r0, 8), P_SIZE + 8), pl.ds(pl.multiple_of(c0, 128), 256))
         canvas[at] = canvas[at] + full
     core = shard % NC
     for d in range(NX):
         x = (shard // NC + d) % NX
         mine_ref[d] = canvas[pl.ds(pl.multiple_of((x * NC + core) * TR, 8), EXT), :TC]
-        theirs_ref[d] = canvas[pl.ds(pl.multiple_of((x * NC + 1 - core) * TR, 8), EXT), :TC]
+        theirs_ref[d] = canvas[pl.ds(pl.multiple_of((x * NC + 1 - core) * TR, 8), EXT), :TC].astype(BF)
 
 
 def place(shard, ids, rows, cols, masters):
     vm = pl.BlockSpec(memory_space=pltpu.VMEM)
     sm = pl.BlockSpec(memory_space=pltpu.SMEM)
     hbm = pl.BlockSpec(memory_space=pltpu.HBM)
-    bands = jax.ShapeDtypeStruct((NX, EXT, TC), F32)
+    bands = (NX, EXT, TC)
     return pl.pallas_call(
         place_kernel,
-        out_shape=(bands, bands, jax.ShapeDtypeStruct((1, INFO), jnp.int32)),
+        out_shape=(jax.ShapeDtypeStruct(bands, F32), jax.ShapeDtypeStruct(bands, BF), jax.ShapeDtypeStruct((1, INFO), jnp.int32)),
         in_specs=[sm] + [hbm] * 4,
         out_specs=(vm, vm, sm),
         scratch_shapes=[
@@ -257,6 +262,7 @@
         lay(down_ref, 1, k)
         lay(far_ref, 2, k)
     load.wait()
+    sub = lax.broadcasted_iota(jnp.int32, (P_SIZE // 8, 8, 128), 1)
     for k in range(NY):
 
         def one(i, carry, k=k):
@@ -267,8 +273,9 @@
                 r, c = lists[k, INST_DEV + i], lists[k, 2 * INST_DEV + i]
                 r0, c0 = (r // 8) * 8, (c // 128) * 128
                 full = canvas[k, pl.ds(pl.multiple_of(r0, 8), P_SIZE + 8), pl.ds(pl.multiple_of(c0, 128), 256)]
-                full = pltpu.roll(full, P_SIZE + 8 - (r - r0), 0)[:P_SIZE]
                 full = pltpu.roll(full, 256 - (c - c0), 1)[:, :128]
+                full = pltpu.roll(full.reshape(P_SIZE // 8 + 1, 8, 128), 8 - (r - r0), 1)
+                full = jnp.where(sub < 8 - (r - r0), full[:-1], full[1:]).reshape(P_SIZE, 128)
                 slot = (m // 16 - z + NZ) % NZ
                 sums[slot, m % 4] = sums[slot, m % 4] + full
 
@@ -305,10 +312,11 @@
     blocks, (out_ref, wide, sem) = refs[: len(places)], refs[n_in:]
     z, y = region_ref[0] // NY, region_ref[0] % NY
     copies = []
-    for n, (dz, ys) in enumerate(places):
-        wide[n] = blocks[n][...].astype(F32)
+    for block, (dz, ys) in zip(blocks, places):
         for j, k in enumerate(ys):
-            cp = pltpu.make_async_copy(wide.at[n, pl.ds(4 * j, 4)], out_ref.at[(z + dz + NZ) % NZ, (y - k + NY) % NY], sem.at[n, j])
+            at = len(copies)
+            wide[at] = block[4 * j : 4 * j + 4].astype(F32)
+            cp = pltpu.make_async_copy(wide.at[at], out_ref.at[(z + dz + NZ) % NZ, (y - k + NY) % NY], sem.at[at])
             cp.start()
             copies.append(cp)
     for cp in copies:
@@ -318,7 +326,7 @@
 def deposit(region, out, items):
     places = [item[1:] for item in items]
     blocks = [item[0] for item in items]
-    n = len(items)
+    n, total = len(items), sum(len(item[2]) for item in items)
     hbm = pl.BlockSpec(memory_space=pltpu.HBM)
     old = [] if out is None else [out]
     return pl.pallas_call(
@@ -327,9 +335,9 @@
         in_specs=[pl.BlockSpec(memory_space=pltpu.SMEM)] + [pl.BlockSpec(memory_space=pltpu.VMEM)] * n + [hbm] * len(old),
         out_specs=hbm,
         input_output_aliases={n + 1: 0} if old else {},
-        scratch_shapes=[pltpu.VMEM((n, 8, P_SIZE, P_SIZE), F32), pltpu.SemaphoreType.DMA((n, 2))],
+        scratch_shapes=[pltpu.VMEM((total, 4, P_SIZE, P_SIZE), F32), pltpu.SemaphoreType.DMA((total,))],
         compiler_params=pltpu.CompilerParams(vmem_limit_bytes=16 * 1024 * 1024),
-        cost_estimate=pl.CostEstimate(flops=500_000 * n, bytes_accessed=800_000 * n, transcendentals=0),
+        cost_estimate=pl.CostEstimate(flops=200_000 * total, bytes_accessed=400_000 * total, transcendentals=0),
         name="deposit",
     )(region, *blocks, *old)
 
@@ -354,26 +362,24 @@
 
 
 def spread(part, region):
-    before, after, across = shift(part, "y", 1), shift(part, "y", 3), shift(part, "y", 2)
-    chunks = (jnp.concatenate([part, before]), jnp.concatenate([after, across]))
-    backs = ((0, 1), (3, 2))
-    out = deposit(region, None, [(chunks[h], 0, backs[h]) for h in range(2)])
-    ups, downs = list(chunks), list(chunks)
-    got = []
-    for d in (1, 2, 3, 4):
-        if d > 1:
-            ups[0], downs[0], out = lax.optimization_barrier((ups[0], downs[0], out))
-        came, got = got, []
-        for h in range(2):
-            if d < 4 or h == 0:
-                ups[h] = shift(ups[h], "z", 1)
-                got.append((ups[h], -d, backs[h]))
-            if d < 4 or h == 1:
-                downs[h] = shift(downs[h], "z", -1)
-                got.append((downs[h], d, backs[h]))
-        if came:
-            out = deposit(region, out, came)
-    out = deposit(region, out, got)
+    own = jnp.concatenate([part, shift(part, "y", 2)])
+    ups, downs = shift(own, "z", 1), shift(own, "z", -1)
+    came = [(shift(own, "y", 1), 0, (1, 3))]
+    out = deposit(region, None, [(own, 0, (0, 2))])
+    for d in (1, 2, 3):
+        ups, downs, out = lax.optimization_barrier((ups, downs, out))
+        here = [(ups, -d, (0, 2)), (downs, d, (0, 2))]
+        if d < 3:
+            ups, downs = shift(ups, "z", 1), shift(downs, "z", -1)
+        else:
+            ups, downs = shift(ups[:4], "z", 1), shift(downs[4:], "z", -1)
+        side = [(shift(here[0][0], "y", 1), -d, (1, 3)), (shift(here[1][0], "y", -1), d, (3, 1))]
+        out = deposit(region, out, here + came)
+        came = side
+    ups, downs, out = lax.optimization_barrier((ups, downs, out))
+    side = [(shift(ups, "y", 1), -4, (1,)), (shift(ups, "y", -1), -4, (3,))]
+    out = deposit(region, out, [(ups, -4, (0,)), (downs, -4, (2,))] + came)
+    out = deposit(region, out, side)
     return out.reshape(MAS_DEV, P_SIZE, P_SIZE)
 
 
@@ -382,8 +388,8 @@
     region = lax.axis_index(("z", "y")).reshape(1)
     mine, theirs, info = place(shard, inst_master, inst_row, inst_col, masters)
     other = shift(theirs, "core", 1)
-    sums = [mine[d] + other[d] for d in range(NX)]
-    parts = [sums[0]] + [shift(sums[d], "x", d) for d in (2, 1, 3)]
+    sums = [mine[d] + other[d].astype(F32) for d in range(NX)]
+    parts = [sums[0]] + [shift(sums[d].astype(BF), "x", d) for d in (2, 1, 3)]
     tmid = target[0]
     tabove, tbelow = halo(tmid, ("x", "core"), 16)
     table = make_table(kernels)

time: 166 us -> 163 us (0.982)
  waiting for transfers between devices: 59 us -> 54.3 us
  starting transfers between devices: 61.2 us -> 64.2 us
    ppermute x34 -> x35, starting transfers between devices: 55.7 us -> 59.9 us  [shift(): return lax.ppermute(v, axis, [(i, (i + by) % n) for i in range(n)])]
    ppermute x34 -> x35, waiting for transfers between devices: 56.8 us -> 54.3 us  [shift(): return lax.ppermute(v, axis, [(i, (i + by) % n) for i in range(n)])]
    ppermute x1, waiting for transfers between devices: 2.25 us -> 0.01 us  [halo(): above = lax.ppermute(v[-width:], axis, [(i, i + 1) for i in range(n - 1)])]
    pallas_call x5 -> x6, Pallas kernels: 6.29 us -> 6.84 us  [deposit(): pl.pallas_call(functools.partial(deposit_kernel, places, n + len(old)), o...]
  transfers between devices with their start and end apart: 36 -> 37, of which waited for: 25 -> 18; matrix products, arithmetic and copies ran while one was open for 1% -> 0% of each run, Pallas kernels for 6% -> 7%
where the time goes in v1:
time: 163 us; the launch traced here: 162 us
  starting transfers between devices  64.2 us (39%)
  waiting for transfers between devices  54.3 us (33%)
  Pallas kernels  30.2 us (19%)
  blocking collectives  9.43 us (6%)
  between operations  1.84 us (1%)
  other arithmetic  1.66 us (1%)
    ppermute x35, starting transfers between devices, shift(): return lax.ppermute(v, axis, [(i, (i + by) % n) for i in range(n)])  59.9 us
    ppermute x35, waiting for transfers between devices, shift(): return lax.ppermute(v, axis, [(i, (i + by) % n) for i in range(n)])  54.3 us
    all_gather x4, blocking collectives, body(): bands = [lax.all_gather(v, 'core') for v in (own, up, down, far)]  9.43 us
    pallas_call x1, Pallas kernels, image(): pl.pallas_call(image_kernel, out_shape=(jax.ShapeDtypeStruct((TR, TC), BF...  9.12 us
    pallas_call x6, Pallas kernels, deposit(): pl.pallas_call(functools.partial(deposit_kernel, places, n + len(old)), o...  6.84 us
    pallas_call x1, Pallas kernels, make_table(): pl.pallas_call(table_kernel, out_shape=jax.ShapeDtypeStruct((K, 2 * KERN...  4.94 us
    pallas_call x1, Pallas kernels, place(): pl.pallas_call(place_kernel, out_shape=(jax.ShapeDtypeStruct(bands, F32),...  4.8 us
    pallas_call x1, Pallas kernels, cut(): pl.pallas_call(cut_kernel, out_shape=[jax.ShapeDtypeStruct(slot, F32)] +...  4.5 us
  transfers between devices with their start and end apart: 37, of which 18 were waited for; matrix products, arithmetic and copies ran while one was open for 0% of the time, Pallas kernels for 7%

profile of v1, /device:TPU:6, one launch (start us, length us, event | category | flops | bytes accessed | tf_op | source)
XLA Modules:
  0.0 162.5 jit_solution(3647096188233874079)
XLA Ops:
  0.7 4.8 %place.1 = (f32[4,80,1024]{2,1,0:T(8,128)}, bf16[4,80,1024]{2,1,0:T(8,128)(2,1)}, s32[1,128]{1,0:T(1,128)}) custom-call(s32[1]{0:T(128)} %bitcast.1.shard_ref, s32[8,1,16]{2,1,0:T(1,128)} %ids_hbm.1, s32[8,1,16]{2,1,0:T(1,128)} %rows_hbm.1, s32[8,1,16]{2,1,0:T(1,128)} %cols_hbm.1, f32[128,128,128]{2,1,0:T(8,128)} %masters_hbm.1), custom_call_target="tpu_custom_call" | custom-call | flops 1000000 | bytes 12000000 | tf_op jit(solution)/shard_map/place/pallas_call | solution.py:224
  5.6 2.3 %collective-permute-done = bf16[4,80,1024]{2,1,0:T(8,128)(2,1)S(1)} collective-permute-done((bf16[4,80,1024]{2,1,0:T(8,128)(2,1)}, bf16[4,80,1024]{2,1,0:T(8,128)(2,1)S(1)}, u32[]{:S(2)}, u32[]{:S(2)}) %collective-permute-start) | collective-permute-done | bytes 655392 | tf_op jit(solution)/shard_map/ppermute | solution.py:347
  7.9 1.4 fusion.2
  9.3 0.9 collective-permute-start.3
  10.2 2.4 %collective-permute-start.2 = (bf16[80,1024]{1,0:T(8,128)(2,1)S(1)}, bf16[80,1024]{1,0:T(8,128)(2,1)S(1)}, u32[]{:S(2)}, u32[]{:S(2)}) collective-permute-start(bf16[80,1024]{1,0:T(8,128)(2,1)S(1)} %get-tuple-element.53), channel_id=1, source_target_pairs={{0,64},{64,128},{128,192},{192,0},{1,65},{65,129},{129,193},{193,1... | collective-permute-start | bytes 491528 | tf_op jit(solution)/shard_map/ppermute | solution.py:347
  12.7 0.4 collective-permute-start.1
  13.1 2.2 %collective-permute-start.5 = (bf16[16,1024]{1,0:T(8,128)(2,1)S(1)}, bf16[16,1024]{1,0:T(8,128)(2,1)S(1)}, u32[]{:S(2)}, u32[]{:S(2)}) collective-permute-start(bf16[16,1024]{1,0:T(8,128)(2,1)S(1)} %get-tuple-element.56), channel_id=1, source_target_pairs={{32,0},{64,32},{96,64},{128,96},{160,128},{192,160},{224,192},{33,... | collective-permute-start | bytes 98312 | tf_op jit(solution)/shard_map/ppermute | solution.py:353
  15.3 2.1 %collective-permute-start.4 = (bf16[16,1024]{1,0:T(8,128)(2,1)S(1)}, bf16[16,1024]{1,0:T(8,128)(2,1)S(1)}, u32[]{:S(2)}, u32[]{:S(2)}) collective-permute-start(bf16[16,1024]{1,0:T(8,128)(2,1)S(1)} %get-tuple-element.57), channel_id=1, source_target_pairs={{0,32},{32,64},{64,96},{96,128},{128,160},{160,192},{192,224},{1,3... | collective-permute-start | bytes 98312 | tf_op jit(solution)/shard_map/ppermute | solution.py:352
  18.1 0.1 reshape.50
  18.2 0.1 copy.20
  18.4 0.1 rev.3
  18.6 0.1 pad.4.clone
  18.7 0.2 reshape.55.v_ref
  18.9 4.9 %taps_table.1.w_ref = bf16[768,3072]{1,0:T(8,128)(2,1)S(1)} custom-call(f32[24,1,512]{2,1,0:T(1,128)S(1)} %reshape.55.v_ref), custom_call_target="tpu_custom_call" | custom-call | flops 20000000 | bytes 10000000 | tf_op jit(solution)/shard_map/taps_table/pallas_call | solution.py:89
  23.9 9.1 %image.1 = (bf16[48,1024]{1,0:T(8,128)(2,1)}, bf16[64,1024]{1,0:T(8,128)(2,1)S(1)}) custom-call(s32[1]{0:T(128)S(6)} %copy.29.level_ref, s32[1]{0:T(128)} %bitcast.1.shard_ref, f32[8,12]{1,0:T(8,128)S(1)} %copy-done.1, f32[80,1024]{1,0:T(8,128)S(1)} %get-tuple-element.55.m0_ref, bf16[80,1024]{1,0:T(8,128)(2,1)S(1)} %collective-permute-done.1.m1_ref, ...), custom_call_target="tpu_custom_call" | custom-call | flops 5000000000 | bytes 8000000 | tf_op jit(solution)/shard_map/image/pallas_call | solution.py:155
  33.0 2.8 %collective-permute-start.8 = (bf16[64,1024]{1,0:T(8,128)(2,1)S(1)}, bf16[64,1024]{1,0:T(8,128)(2,1)S(1)}, u32[]{:S(2)}, u32[]{:S(2)}) collective-permute-start(bf16[64,1024]{1,0:T(8,128)(2,1)S(1)} %get-tuple-element.30.g0), channel_id=1, source_target_pairs={{0,3},{1,0},{2,1},{3,2},{4,7},{5,4},{6,5},{7,6},{8,11},{9,8},{10,9... | collective-permute-start | bytes 393224 | tf_op jit(solution)/shard_map/ppermute | solution.py:347
  35.8 0.6 collective-permute-start.7
  36.4 1.0 collective-permute-start.6
  37.4 3.5 %collective-permute-done.8.g3 = bf16[64,1024]{1,0:T(8,128)(2,1)S(1)} collective-permute-done((bf16[64,1024]{1,0:T(8,128)(2,1)S(1)}, bf16[64,1024]{1,0:T(8,128)(2,1)S(1)}, u32[]{:S(2)}, u32[]{:S(2)}) %collective-permute-start.8) | collective-permute-done | bytes 131104 | tf_op jit(solution)/shard_map/ppermute | solution.py:347
  41.0 2.3 %collective-permute-done.7.g2 = bf16[64,1024]{1,0:T(8,128)(2,1)S(1)} collective-permute-done((bf16[64,1024]{1,0:T(8,128)(2,1)S(1)}, bf16[64,1024]{1,0:T(8,128)(2,1)S(1)}, u32[]{:S(2)}, u32[]{:S(2)}) %collective-permute-start.7) | collective-permute-done | bytes 131104 | tf_op jit(solution)/shard_map/ppermute | solution.py:347
  43.3 1.3 collective-permute-done.6.g1
  44.7 4.6 %collective-permute-start.11 = (bf16[4,48,1024]{2,1,0:T(8,128)(2,1)S(1)}, bf16[4,48,1024]{2,1,0:T(8,128)(2,1)S(1)}, u32[]{:S(2)}, u32[]{:S(2)}) collective-permute-start(bf16[4,48,1024]{2,1,0:T(8,128)(2,1)S(1)} %pad_maximum_fusion), channel_id=1, source_target_pairs={{0,128},{64,192},{128,0},{192,64},{1,129},{65,193},{129,1},{193,65... | collective-permute-start | bytes 1179656 | tf_op jit(solution)/shard_map/ppermute | solution.py:347
  49.3 0.3 collective-permute-start.10
  49.6 2.9 %collective-permute-start.9 = (bf16[4,48,1024]{2,1,0:T(8,128)(2,1)S(1)}, bf16[4,48,1024]{2,1,0:T(8,128)(2,1)S(1)}, u32[]{:S(2)}, u32[]{:S(2)}) collective-permute-start(bf16[4,48,1024]{2,1,0:T(8,128)(2,1)S(1)} %pad_maximum_fusion), channel_id=1, source_target_pairs={{0,64},{64,128},{128,192},{192,0},{1,65},{65,129},{129,193},{193,1... | collective-permute-start | bytes 1179656 | tf_op jit(solution)/shard_map/ppermute | solution.py:347
  52.5 2.4 %all-gather = bf16[8,48,1024]{2,1,0:T(8,128)(2,1)S(1)} all-gather(bf16[4,48,1024]{2,1,0:T(8,128)(2,1)S(1)} %pad_maximum_fusion), channel_id=2, replica_groups=mesh['x'=4,'core'=2,'z'=8,'y'=4] {'core'}, dimensions={0}, use_global_device_ids=true | all-gather | bytes 1179648 | tf_op jit(solution)/shard_map/all_gather | solution.py:400
  54.9 4.4 %collective-permute-done.11 = bf16[4,48,1024]{2,1,0:T(8,128)(2,1)S(1)} collective-permute-done((bf16[4,48,1024]{2,1,0:T(8,128)(2,1)S(1)}, bf16[4,48,1024]{2,1,0:T(8,128)(2,1)S(1)}, u32[]{:S(2)}, u32[]{:S(2)}) %collective-permute-start.11) | collective-permute-done | bytes 393248 | tf_op jit(solution)/shard_map/ppermute | solution.py:347
  59.2 2.4 %all-gather.3 = bf16[8,48,1024]{2,1,0:T(8,128)(2,1)S(1)} all-gather(bf16[4,48,1024]{2,1,0:T(8,128)(2,1)S(1)} %collective-permute-done.11), channel_id=5, replica_groups=mesh['x'=4,'core'=2,'z'=8,'y'=4] {'core'}, dimensions={0}, use_global_device_ids=true | all-gather | bytes 1179648 | tf_op jit(solution)/shard_map/all_gather | solution.py:400
  61.6 5.4 %collective-permute-done.10 = bf16[4,48,1024]{2,1,0:T(8,128)(2,1)S(1)} collective-permute-done((bf16[4,48,1024]{2,1,0:T(8,128)(2,1)S(1)}, bf16[4,48,1024]{2,1,0:T(8,128)(2,1)S(1)}, u32[]{:S(2)}, u32[]{:S(2)}) %collective-permute-start.10) | collective-permute-done | bytes 393248 | tf_op jit(solution)/shard_map/ppermute | solution.py:347
  67.0 2.4 %all-gather.2 = bf16[8,48,1024]{2,1,0:T(8,128)(2,1)S(1)} all-gather(bf16[4,48,1024]{2,1,0:T(8,128)(2,1)S(1)} %collective-permute-done.10), channel_id=4, replica_groups=mesh['x'=4,'core'=2,'z'=8,'y'=4] {'core'}, dimensions={0}, use_global_device_ids=true | all-gather | bytes 1179648 | tf_op jit(solution)/shard_map/all_gather | solution.py:400
  69.4 2.4 %all-gather.1 = bf16[8,48,1024]{2,1,0:T(8,128)(2,1)S(1)} all-gather(bf16[4,48,1024]{2,1,0:T(8,128)(2,1)S(1)} %collective-permute-done.9), channel_id=3, replica_groups=mesh['x'=4,'core'=2,'z'=8,'y'=4] {'core'}, dimensions={0}, use_global_device_ids=true | all-gather | bytes 1179648 | tf_op jit(solution)/shard_map/all_gather | solution.py:400
  71.7 4.5 %cut.1 = (f32[4,128,128]{2,1,0:T(8,128)S(1)}, bf16[4,128,128]{2,1,0:T(8,128)(2,1)S(1)}, bf16[4,128,128]{2,1,0:T(8,128)(2,1)S(1)}, bf16[4,128,128]{2,1,0:T(8,128)...) custom-call(s32[1]{0:T(128)} %bitcast.1.shard_ref, ...), custom_call_target="tpu_custom_call" | custom-call | flops 1000000 | bytes 12000000 | tf_op jit(solution)/shard_map/cut/pallas_call | solution.py:293
  76.2 7.6 %collective-permute-start.12 = (bf16[4,128,128]{2,1,0:T(8,128)(2,1)S(1)}, bf16[4,128,128]{2,1,0:T(8,128)(2,1)S(1)}, u32[]{:S(2)}, u32[]{:S(2)}) collective-permute-start(bf16[4,128,128]{2,1,0:T(8,128)(2,1)S(1)} %get-tuple-element.32), channel_id=1, source_target_pairs={{0,16},{4,20},{8,24},{12,28},{16,0},{20,4},{24,8},{28,12},{1,17},{... | collective-permute-start | bytes 393224 | tf_op jit(solution)/shard_map/ppermute | solution.py:347
  83.8 1.5 collective-permute-start.13
  85.3 3.6 %collective-permute-start.14 = (bf16[4,128,128]{2,1,0:T(8,128)(2,1)S(1)}, bf16[4,128,128]{2,1,0:T(8,128)(2,1)S(1)}, u32[]{:S(2)}, u32[]{:S(2)}) collective-permute-start(bf16[4,128,128]{2,1,0:T(8,128)(2,1)S(1)} %get-tuple-element.34), channel_id=1, source_target_pairs={{0,20},{4,24},{8,28},{12,0},{16,4},{20,8},{24,12},{28,16},{1,21},{... | collective-permute-start | bytes 393224 | tf_op jit(solution)/shard_map/ppermute | solution.py:347
  88.9 0.9 collective-permute-start.15
  89.8 3.2 %collective-permute-start.16 = (bf16[4,128,128]{2,1,0:T(8,128)(2,1)S(1)}, bf16[4,128,128]{2,1,0:T(8,128)(2,1)S(1)}, u32[]{:S(2)}, u32[]{:S(2)}) collective-permute-start(bf16[4,128,128]{2,1,0:T(8,128)(2,1)S(1)} %get-tuple-element.36), channel_id=1, source_target_pairs={{0,24},{4,28},{8,0},{12,4},{16,8},{20,12},{24,16},{28,20},{1,25},{... | collective-permute-start | bytes 393224 | tf_op jit(solution)/shard_map/ppermute | solution.py:347
  93.0 2.7 %collective-permute-start.17 = (bf16[4,128,128]{2,1,0:T(8,128)(2,1)S(1)}, bf16[4,128,128]{2,1,0:T(8,128)(2,1)S(1)}, u32[]{:S(2)}, u32[]{:S(2)}) collective-permute-start(bf16[4,128,128]{2,1,0:T(8,128)(2,1)S(1)} %get-tuple-element.37), channel_id=1, source_target_pairs={{0,4},{4,8},{8,12},{12,16},{16,20},{20,24},{24,28},{28,0},{1,5},{5... | collective-permute-start | bytes 393224 | tf_op jit(solution)/shard_map/ppermute | solution.py:347
  95.7 6.2 %collective-permute-done.13 = bf16[4,128,128]{2,1,0:T(8,128)(2,1)S(1)} collective-permute-done((bf16[4,128,128]{2,1,0:T(8,128)(2,1)S(1)}, bf16[4,128,128]{2,1,0:T(8,128)(2,1)S(1)}, u32[]{:S(2)}, u32[]{:S(2)}) %collective-permute-start.13) | collective-permute-done | bytes 131104 | tf_op jit(solution)/shard_map/ppermute | solution.py:347
  101.9 0.9 collective-permute-done.15
  102.9 2.8 %collective-permute-done.16 = bf16[4,128,128]{2,1,0:T(8,128)(2,1)S(1)} collective-permute-done((bf16[4,128,128]{2,1,0:T(8,128)(2,1)S(1)}, bf16[4,128,128]{2,1,0:T(8,128)(2,1)S(1)}, u32[]{:S(2)}, u32[]{:S(2)}) %collective-permute-start.16) | collective-permute-done | bytes 131104 | tf_op jit(solution)/shard_map/ppermute | solution.py:347
  105.7 0.6 collective-permute-done.17
  106.3 2.3 %collective-permute-done.18 = bf16[4,128,128]{2,1,0:T(8,128)(2,1)S(1)} collective-permute-done((bf16[4,128,128]{2,1,0:T(8,128)(2,1)S(1)}, bf16[4,128,128]{2,1,0:T(8,128)(2,1)S(1)}, u32[]{:S(2)}, u32[]{:S(2)}) %collective-permute-start.18) | collective-permute-done | bytes 131104 | tf_op jit(solution)/shard_map/ppermute | solution.py:347
  108.6 0.1 add_convert_fusion.3
  108.9 6.8 %collective-permute-done.19 = bf16[4,128,128]{2,1,0:T(8,128)(2,1)S(1)} collective-permute-done((bf16[4,128,128]{2,1,0:T(8,128)(2,1)S(1)}, bf16[4,128,128]{2,1,0:T(8,128)(2,1)S(1)}, u32[]{:S(2)}, u32[]{:S(2)}) %collective-permute-start.19) | collective-permute-done | bytes 131104 | tf_op jit(solution)/shard_map/ppermute | solution.py:347
  115.7 3.0 %collective-permute-start.21 = (bf16[8,128,128]{2,1,0:T(8,128)(2,1)S(1)}, bf16[8,128,128]{2,1,0:T(8,128)(2,1)S(1)}, u32[]{:S(2)}, u32[]{:S(2)}) collective-permute-start(bf16[8,128,128]{2,1,0:T(8,128)(2,1)S(1)} %pad_maximum_fusion.1.refs_0_), channel_id=1, source_target_pairs={{0,28},{4,0},{8,4},{12,8},{16,12},{20,16},{24,20},{28,24},{1,29},{... | collective-permute-start | bytes 786440 | tf_op jit(solution)/shard_map/ppermute | solution.py:347
  118.7 0.8 deposit.6.refs_3_
  119.5 4.1 %collective-permute-done.21.refs_1_ = bf16[8,128,128]{2,1,0:T(8,128)(2,1)S(1)} collective-permute-done((bf16[8,128,128]{2,1,0:T(8,128)(2,1)S(1)}, bf16[8,128,128]{2,1,0:T(8,128)(2,1)S(1)}, u32[]{:S(2)}, u32[]{:S(2)}) %collective-permute-start.21) | collective-permute-done | bytes 262176 | tf_op jit(solution)/shard_map/ppermute | solution.py:347
  123.6 3.4 %collective-permute-done.20.refs_0_ = bf16[8,128,128]{2,1,0:T(8,128)(2,1)S(1)} collective-permute-done((bf16[8,128,128]{2,1,0:T(8,128)(2,1)S(1)}, bf16[8,128,128]{2,1,0:T(8,128)(2,1)S(1)}, u32[]{:S(2)}, u32[]{:S(2)}) %collective-permute-start.20) | collective-permute-done | bytes 262176 | tf_op jit(solution)/shard_map/ppermute | solution.py:347
  127.0 3.2 %collective-permute-start.23 = (bf16[8,128,128]{2,1,0:T(8,128)(2,1)S(1)}, bf16[8,128,128]{2,1,0:T(8,128)(2,1)S(1)}, u32[]{:S(2)}, u32[]{:S(2)}) collective-permute-start(bf16[8,128,128]{2,1,0:T(8,128)(2,1)S(1)} %collective-permute-done.21.refs_1_), channel_id=1, source_target_pairs={{0,28},{4,0},{8,4},{12,8},{16,12},{20,16},{24,20},{28,24},{1,29},{... | collective-permute-start | bytes 786440 | tf_op jit(solution)/shard_map/ppermute | solution.py:347
  130.2 3.2 %collective-permute-start.28 = (bf16[8,128,128]{2,1,0:T(8,128)(2,1)S(1)}, bf16[8,128,128]{2,1,0:T(8,128)(2,1)S(1)}, u32[]{:S(2)}, u32[]{:S(2)}) collective-permute-start(bf16[8,128,128]{2,1,0:T(8,128)(2,1)S(1)} %collective-permute-done.21.refs_1_), channel_id=1, source_target_pairs={{0,3},{1,0},{2,1},{3,2},{4,7},{5,4},{6,5},{7,6},{8,11},{9,8},{10,9... | collective-permute-start | bytes 786440 | tf_op jit(solution)/shard_map/ppermute | solution.py:347
  133.5 1.2 deposit.7.refs_4_
  134.8 3.2 %collective-permute-start.26 = (bf16[8,128,128]{2,1,0:T(8,128)(2,1)S(1)}, bf16[8,128,128]{2,1,0:T(8,128)(2,1)S(1)}, u32[]{:S(2)}, u32[]{:S(2)}) collective-permute-start(bf16[8,128,128]{2,1,0:T(8,128)(2,1)S(1)} %collective-permute-done.23.refs_1_), channel_id=1, source_target_pairs={{0,28},{4,0},{8,4},{12,8},{16,12},{20,16},{24,20},{28,24},{1,29},{... | collective-permute-start | bytes 786440 | tf_op jit(solution)/shard_map/ppermute | solution.py:347
  138.0 3.2 %collective-permute-start.32 = (bf16[8,128,128]{2,1,0:T(8,128)(2,1)S(1)}, bf16[8,128,128]{2,1,0:T(8,128)(2,1)S(1)}, u32[]{:S(2)}, u32[]{:S(2)}) collective-permute-start(bf16[8,128,128]{2,1,0:T(8,128)(2,1)S(1)} %collective-permute-done.23.refs_1_), channel_id=1, source_target_pairs={{0,3},{1,0},{2,1},{3,2},{4,7},{5,4},{6,5},{7,6},{8,11},{9,8},{10,9... | collective-permute-start | bytes 786440 | tf_op jit(solution)/shard_map/ppermute | solution.py:347
  141.2 1.4 deposit.8.refs_4_
  142.8 3.3 %collective-permute-start.36 = (bf16[8,128,128]{2,1,0:T(8,128)(2,1)S(1)}, bf16[8,128,128]{2,1,0:T(8,128)(2,1)S(1)}, u32[]{:S(2)}, u32[]{:S(2)}) collective-permute-start(bf16[8,128,128]{2,1,0:T(8,128)(2,1)S(1)} %collective-permute-done.26.refs_1_), channel_id=1, source_target_pairs={{0,3},{1,0},{2,1},{3,2},{4,7},{5,4},{6,5},{7,6},{8,11},{9,8},{10,9... | collective-permute-start | bytes 786440 | tf_op jit(solution)/shard_map/ppermute | solution.py:347
  146.1 2.9 %collective-permute-start.30 = (bf16[4,128,128]{2,1,0:T(8,128)(2,1)S(1)}, bf16[4,128,128]{2,1,0:T(8,128)(2,1)S(1)}, u32[]{:S(2)}, u32[]{:S(2)}) collective-permute-start(bf16[4,128,128]{2,1,0:T(8,128)(2,1)S(1)} %slice.71), channel_id=1, source_target_pairs={{0,28},{4,0},{8,4},{12,8},{16,12},{20,16},{24,20},{28,24},{1,29},{... | collective-permute-start | bytes 393224 | tf_op jit(solution)/shard_map/ppermute | solution.py:347
  149.0 1.4 deposit.9.refs_4_
  150.4 1.1 collective-permute-done.30.refs_1_
  151.5 3.7 %collective-permute-done.29.refs_0_ = bf16[4,128,128]{2,1,0:T(8,128)(2,1)S(1)} collective-permute-done((bf16[4,128,128]{2,1,0:T(8,128)(2,1)S(1)}, bf16[4,128,128]{2,1,0:T(8,128)(2,1)S(1)}, u32[]{:S(2)}, u32[]{:S(2)}) %collective-permute-start.29) | collective-permute-done | bytes 131104 | tf_op jit(solution)/shard_map/ppermute | solution.py:347
  155.3 1.9 %collective-permute-start.33 = (bf16[4,128,128]{2,1,0:T(8,128)(2,1)S(1)}, bf16[4,128,128]{2,1,0:T(8,128)(2,1)S(1)}, u32[]{:S(2)}, u32[]{:S(2)}) collective-permute-start(bf16[4,128,128]{2,1,0:T(8,128)(2,1)S(1)} %collective-permute-done.29.refs_0_), channel_id=1, source_target_pairs={{0,1},{1,2},{2,3},{3,0},{4,5},{5,6},{6,7},{7,4},{8,9},{9,10},{10,1... | collective-permute-start | bytes 393224 | tf_op jit(solution)/shard_map/ppermute | solution.py:347
  157.2 1.2 deposit.10.refs_2_
  158.4 1.7 %collective-permute-done.34.refs_1_ = bf16[4,128,128]{2,1,0:T(8,128)(2,1)S(1)} collective-permute-done((bf16[4,128,128]{2,1,0:T(8,128)(2,1)S(1)}, bf16[4,128,128]{2,1,0:T(8,128)(2,1)S(1)}, u32[]{:S(2)}, u32[]{:S(2)}) %collective-permute-start.34) | collective-permute-done | bytes 131104 | tf_op jit(solution)/shard_map/ppermute | solution.py:347
  160.2 1.3 collective-permute-done.33.refs_0_
  161.5 0.8 deposit.11
  (49 shorter events, 0.7 us)
Async XLA Ops:
  0.6 12.5 %copy-start = (bf16[1,48,1024]{2,1,0:T(8,128)(2,1)S(1)}, bf16[1,48,1024]{2,1,0:T(8,128)(2,1)}, u32[]{:S(2)}) copy-start(bf16[1,48,1024]{2,1,0:T(8,128)(2,1)} %param.15) | copy-start | bytes 294916
  0.6 17.5 %copy-start.3 = (bf16[24,225]{1,0:T(8,128)(2,1)S(1)}, bf16[24,225]{1,0:T(8,128)(2,1)}, u32[]{:S(2)}) copy-start(bf16[24,225]{1,0:T(8,128)(2,1)} %param.14) | copy-start | bytes 32404
  0.7 23.2 %copy-start.1 = (f32[8,12]{1,0:T(8,128)S(1)}, f32[8,12]{1,0:T(8,128)}, u32[]{:S(2)}) copy-start(f32[8,12]{1,0:T(8,128)} %wgt_ref.1) | copy-start | bytes 1156
  5.5 18.4 %copy-start.2 = (s32[1,128]{1,0:T(1,128)S(1)}, s32[1,128]{1,0:T(1,128)}, u32[]{:S(2)}) copy-start(s32[1,128]{1,0:T(1,128)} %get-tuple-element.29.info_ref) | copy-start | bytes 1540
  5.5 2.4 %collective-permute-start = (bf16[4,80,1024]{2,1,0:T(8,128)(2,1)}, bf16[4,80,1024]{2,1,0:T(8,128)(2,1)S(1)}, u32[]{:S(2)}, u32[]{:S(2)}) collective-permute-start(bf16[4,80,1024]{2,1,0:T(8,128)(2,1)} %get-tuple-element.28), channel_id=1, source_target_pairs={{0,32},{32,0},{1,33},{33,1},{2,34},{34,2},{3,35},{35,3},{4,36},{36... | collective-permute-start | bytes 1966088 | tf_op jit(solution)/shard_map/ppermute | solution.py:347
  9.3 14.5 %collective-permute-start.3 = (bf16[80,1024]{1,0:T(8,128)(2,1)S(1)}, bf16[80,1024]{1,0:T(8,128)(2,1)S(1)}, u32[]{:S(2)}, u32[]{:S(2)}) collective-permute-start(bf16[80,1024]{1,0:T(8,128)(2,1)S(1)} %get-tuple-element.52), channel_id=1, source_target_pairs={{0,192},{64,0},{128,64},{192,128},{1,193},{65,1},{129,65},{193,129... | collective-permute-start | bytes 491528 | tf_op jit(solution)/shard_map/ppermute | solution.py:347
  10.2 13.6 %collective-permute-start.2 = (bf16[80,1024]{1,0:T(8,128)(2,1)S(1)}, bf16[80,1024]{1,0:T(8,128)(2,1)S(1)}, u32[]{:S(2)}, u32[]{:S(2)}) collective-permute-start(bf16[80,1024]{1,0:T(8,128)(2,1)S(1)} %get-tuple-element.53), channel_id=1, source_target_pairs={{0,64},{64,128},{128,192},{192,0},{1,65},{65,129},{129,193},{193,1... | collective-permute-start | bytes 491528 | tf_op jit(solution)/shard_map/ppermute | solution.py:347
  12.7 11.2 %collective-permute-start.1 = (bf16[80,1024]{1,0:T(8,128)(2,1)S(1)}, bf16[80,1024]{1,0:T(8,128)(2,1)S(1)}, u32[]{:S(2)}, u32[]{:S(2)}) collective-permute-start(bf16[80,1024]{1,0:T(8,128)(2,1)S(1)} %get-tuple-element.54), channel_id=1, source_target_pairs={{0,128},{64,192},{128,0},{192,64},{1,129},{65,193},{129,1},{193,65... | collective-permute-start | bytes 491528 | tf_op jit(solution)/shard_map/ppermute | solution.py:347
  13.1 10.7 %collective-permute-start.5 = (bf16[16,1024]{1,0:T(8,128)(2,1)S(1)}, bf16[16,1024]{1,0:T(8,128)(2,1)S(1)}, u32[]{:S(2)}, u32[]{:S(2)}) collective-permute-start(bf16[16,1024]{1,0:T(8,128)(2,1)S(1)} %get-tuple-element.56), channel_id=1, source_target_pairs={{32,0},{64,32},{96,64},{128,96},{160,128},{192,160},{224,192},{33,... | collective-permute-start | bytes 98312 | tf_op jit(solution)/shard_map/ppermute | solution.py:353
  15.3 8.5 %collective-permute-start.4 = (bf16[16,1024]{1,0:T(8,128)(2,1)S(1)}, bf16[16,1024]{1,0:T(8,128)(2,1)S(1)}, u32[]{:S(2)}, u32[]{:S(2)}) collective-permute-start(bf16[16,1024]{1,0:T(8,128)(2,1)S(1)} %get-tuple-element.57), channel_id=1, source_target_pairs={{0,32},{32,64},{64,96},{96,128},{128,160},{160,192},{192,224},{1,3... | collective-permute-start | bytes 98312 | tf_op jit(solution)/shard_map/ppermute | solution.py:352
  33.0 7.9 %collective-permute-start.8 = (bf16[64,1024]{1,0:T(8,128)(2,1)S(1)}, bf16[64,1024]{1,0:T(8,128)(2,1)S(1)}, u32[]{:S(2)}, u32[]{:S(2)}) collective-permute-start(bf16[64,1024]{1,0:T(8,128)(2,1)S(1)} %get-tuple-element.30.g0), channel_id=1, source_target_pairs={{0,3},{1,0},{2,1},{3,2},{4,7},{5,4},{6,5},{7,6},{8,11},{9,8},{10,9... | collective-permute-start | bytes 393224 | tf_op jit(solution)/shard_map/ppermute | solution.py:347
  35.8 7.5 %collective-permute-start.7 = (bf16[64,1024]{1,0:T(8,128)(2,1)S(1)}, bf16[64,1024]{1,0:T(8,128)(2,1)S(1)}, u32[]{:S(2)}, u32[]{:S(2)}) collective-permute-start(bf16[64,1024]{1,0:T(8,128)(2,1)S(1)} %get-tuple-element.30.g0), channel_id=1, source_target_pairs={{0,2},{1,3},{2,0},{3,1},{4,6},{5,7},{6,4},{7,5},{8,10},{9,11},{10,... | collective-permute-start | bytes 393224 | tf_op jit(solution)/shard_map/ppermute | solution.py:347
  36.4 8.2 %collective-permute-start.6 = (bf16[64,1024]{1,0:T(8,128)(2,1)S(1)}, bf16[64,1024]{1,0:T(8,128)(2,1)S(1)}, u32[]{:S(2)}, u32[]{:S(2)}) collective-permute-start(bf16[64,1024]{1,0:T(8,128)(2,1)S(1)} %get-tuple-element.30.g0), channel_id=1, source_target_pairs={{0,1},{1,2},{2,3},{3,0},{4,5},{5,6},{6,7},{7,4},{8,9},{9,10},{10,1... | collective-permute-start | bytes 393224 | tf_op jit(solution)/shard_map/ppermute | solution.py:347
  44.7 14.5 %collective-permute-start.11 = (bf16[4,48,1024]{2,1,0:T(8,128)(2,1)S(1)}, bf16[4,48,1024]{2,1,0:T(8,128)(2,1)S(1)}, u32[]{:S(2)}, u32[]{:S(2)}) collective-permute-start(bf16[4,48,1024]{2,1,0:T(8,128)(2,1)S(1)} %pad_maximum_fusion), channel_id=1, source_target_pairs={{0,128},{64,192},{128,0},{192,64},{1,129},{65,193},{129,1},{193,65... | collective-permute-start | bytes 1179656 | tf_op jit(solution)/shard_map/ppermute | solution.py:347
  49.3 17.7 %collective-permute-start.10 = (bf16[4,48,1024]{2,1,0:T(8,128)(2,1)S(1)}, bf16[4,48,1024]{2,1,0:T(8,128)(2,1)S(1)}, u32[]{:S(2)}, u32[]{:S(2)}) collective-permute-start(bf16[4,48,1024]{2,1,0:T(8,128)(2,1)S(1)} %pad_maximum_fusion), channel_id=1, source_target_pairs={{0,192},{64,0},{128,64},{192,128},{1,193},{65,1},{129,65},{193,129... | collective-permute-start | bytes 1179656 | tf_op jit(solution)/shard_map/ppermute | solution.py:347
  49.6 19.7 %collective-permute-start.9 = (bf16[4,48,1024]{2,1,0:T(8,128)(2,1)S(1)}, bf16[4,48,1024]{2,1,0:T(8,128)(2,1)S(1)}, u32[]{:S(2)}, u32[]{:S(2)}) collective-permute-start(bf16[4,48,1024]{2,1,0:T(8,128)(2,1)S(1)} %pad_maximum_fusion), channel_id=1, source_target_pairs={{0,64},{64,128},{128,192},{192,0},{1,65},{65,129},{129,193},{193,1... | collective-permute-start | bytes 1179656 | tf_op jit(solution)/shard_map/ppermute | solution.py:347
  76.2 16.8 %collective-permute-start.12 = (bf16[4,128,128]{2,1,0:T(8,128)(2,1)S(1)}, bf16[4,128,128]{2,1,0:T(8,128)(2,1)S(1)}, u32[]{:S(2)}, u32[]{:S(2)}) collective-permute-start(bf16[4,128,128]{2,1,0:T(8,128)(2,1)S(1)} %get-tuple-element.32), channel_id=1, source_target_pairs={{0,16},{4,20},{8,24},{12,28},{16,0},{20,4},{24,8},{28,12},{1,17},{... | collective-permute-start | bytes 393224 | tf_op jit(solution)/shard_map/ppermute | solution.py:347
  83.8 18.1 %collective-permute-start.13 = (bf16[4,128,128]{2,1,0:T(8,128)(2,1)S(1)}, bf16[4,128,128]{2,1,0:T(8,128)(2,1)S(1)}, u32[]{:S(2)}, u32[]{:S(2)}) collective-permute-start(bf16[4,128,128]{2,1,0:T(8,128)(2,1)S(1)} %get-tuple-element.33), channel_id=1, source_target_pairs={{0,12},{4,16},{8,20},{12,24},{16,28},{20,0},{24,4},{28,8},{1,13},{... | collective-permute-start | bytes 393224 | tf_op jit(solution)/shard_map/ppermute | solution.py:347
  85.3 16.6 %collective-permute-start.14 = (bf16[4,128,128]{2,1,0:T(8,128)(2,1)S(1)}, bf16[4,128,128]{2,1,0:T(8,128)(2,1)S(1)}, u32[]{:S(2)}, u32[]{:S(2)}) collective-permute-start(bf16[4,128,128]{2,1,0:T(8,128)(2,1)S(1)} %get-tuple-element.34), channel_id=1, source_target_pairs={{0,20},{4,24},{8,28},{12,0},{16,4},{20,8},{24,12},{28,16},{1,21},{... | collective-permute-start | bytes 393224 | tf_op jit(solution)/shard_map/ppermute | solution.py:347
  88.9 14.0 %collective-permute-start.15 = (bf16[4,128,128]{2,1,0:T(8,128)(2,1)S(1)}, bf16[4,128,128]{2,1,0:T(8,128)(2,1)S(1)}, u32[]{:S(2)}, u32[]{:S(2)}) collective-permute-start(bf16[4,128,128]{2,1,0:T(8,128)(2,1)S(1)} %get-tuple-element.35), channel_id=1, source_target_pairs={{0,8},{4,12},{8,16},{12,20},{16,24},{20,28},{24,0},{28,4},{1,9},{5... | collective-permute-start | bytes 393224 | tf_op jit(solution)/shard_map/ppermute | solution.py:347
  89.8 15.9 %collective-permute-start.16 = (bf16[4,128,128]{2,1,0:T(8,128)(2,1)S(1)}, bf16[4,128,128]{2,1,0:T(8,128)(2,1)S(1)}, u32[]{:S(2)}, u32[]{:S(2)}) collective-permute-start(bf16[4,128,128]{2,1,0:T(8,128)(2,1)S(1)} %get-tuple-element.36), channel_id=1, source_target_pairs={{0,24},{4,28},{8,0},{12,4},{16,8},{20,12},{24,16},{28,20},{1,25},{... | collective-permute-start | bytes 393224 | tf_op jit(solution)/shard_map/ppermute | solution.py:347
  93.0 13.3 %collective-permute-start.17 = (bf16[4,128,128]{2,1,0:T(8,128)(2,1)S(1)}, bf16[4,128,128]{2,1,0:T(8,128)(2,1)S(1)}, u32[]{:S(2)}, u32[]{:S(2)}) collective-permute-start(bf16[4,128,128]{2,1,0:T(8,128)(2,1)S(1)} %get-tuple-element.37), channel_id=1, source_target_pairs={{0,4},{4,8},{8,12},{12,16},{16,20},{20,24},{24,28},{28,0},{1,5},{5... | collective-permute-start | bytes 393224 | tf_op jit(solution)/shard_map/ppermute | solution.py:347
  101.9 6.7 %collective-permute-start.18 = (bf16[4,128,128]{2,1,0:T(8,128)(2,1)S(1)}, bf16[4,128,128]{2,1,0:T(8,128)(2,1)S(1)}, u32[]{:S(2)}, u32[]{:S(2)}) collective-permute-start(bf16[4,128,128]{2,1,0:T(8,128)(2,1)S(1)} %get-tuple-element.38), channel_id=1, source_target_pairs={{0,28},{4,0},{8,4},{12,8},{16,12},{20,16},{24,20},{28,24},{1,29},{... | collective-permute-start | bytes 393224 | tf_op jit(solution)/shard_map/ppermute | solution.py:347
  108.8 6.9 %collective-permute-start.19 = (bf16[4,128,128]{2,1,0:T(8,128)(2,1)S(1)}, bf16[4,128,128]{2,1,0:T(8,128)(2,1)S(1)}, u32[]{:S(2)}, u32[]{:S(2)}) collective-permute-start(bf16[4,128,128]{2,1,0:T(8,128)(2,1)S(1)} %add_convert_fusion.3), channel_id=1, source_target_pairs={{0,2},{1,3},{2,0},{3,1},{4,6},{5,7},{6,4},{7,5},{8,10},{9,11},{10,... | collective-permute-start | bytes 393224 | tf_op jit(solution)/shard_map/ppermute | solution.py:347
  115.7 7.9 %collective-permute-start.21 = (bf16[8,128,128]{2,1,0:T(8,128)(2,1)S(1)}, bf16[8,128,128]{2,1,0:T(8,128)(2,1)S(1)}, u32[]{:S(2)}, u32[]{:S(2)}) collective-permute-start(bf16[8,128,128]{2,1,0:T(8,128)(2,1)S(1)} %pad_maximum_fusion.1.refs_0_), channel_id=1, source_target_pairs={{0,28},{4,0},{8,4},{12,8},{16,12},{20,16},{24,20},{28,24},{1,29},{... | collective-permute-start | bytes 786440 | tf_op jit(solution)/shard_map/ppermute | solution.py:347
  118.6 8.3 %collective-permute-start.20 = (bf16[8,128,128]{2,1,0:T(8,128)(2,1)S(1)}, bf16[8,128,128]{2,1,0:T(8,128)(2,1)S(1)}, u32[]{:S(2)}, u32[]{:S(2)}) collective-permute-start(bf16[8,128,128]{2,1,0:T(8,128)(2,1)S(1)} %pad_maximum_fusion.1.refs_0_), channel_id=1, source_target_pairs={{0,4},{4,8},{8,12},{12,16},{16,20},{20,24},{24,28},{28,0},{1,5},{5... | collective-permute-start | bytes 786440 | tf_op jit(solution)/shard_map/ppermute | solution.py:347
  118.6 14.8 %collective-permute-start.24 = (bf16[8,128,128]{2,1,0:T(8,128)(2,1)S(1)}, bf16[8,128,128]{2,1,0:T(8,128)(2,1)S(1)}, u32[]{:S(2)}, u32[]{:S(2)}) collective-permute-start(bf16[8,128,128]{2,1,0:T(8,128)(2,1)S(1)} %pad_maximum_fusion.1.refs_0_), channel_id=1, source_target_pairs={{0,1},{1,2},{2,3},{3,0},{4,5},{5,6},{6,7},{7,4},{8,9},{9,10},{10,1... | collective-permute-start | bytes 786440 | tf_op jit(solution)/shard_map/ppermute | solution.py:347
  127.0 7.7 %collective-permute-start.22 = (bf16[8,128,128]{2,1,0:T(8,128)(2,1)S(1)}, bf16[8,128,128]{2,1,0:T(8,128)(2,1)S(1)}, u32[]{:S(2)}, u32[]{:S(2)}) collective-permute-start(bf16[8,128,128]{2,1,0:T(8,128)(2,1)S(1)} %collective-permute-done.20.refs_0_), channel_id=1, source_target_pairs={{0,4},{4,8},{8,12},{12,16},{16,20},{20,24},{24,28},{28,0},{1,5},{5... | collective-permute-start | bytes 786440 | tf_op jit(solution)/shard_map/ppermute | solution.py:347
  127.0 7.7 %collective-permute-start.23 = (bf16[8,128,128]{2,1,0:T(8,128)(2,1)S(1)}, bf16[8,128,128]{2,1,0:T(8,128)(2,1)S(1)}, u32[]{:S(2)}, u32[]{:S(2)}) collective-permute-start(bf16[8,128,128]{2,1,0:T(8,128)(2,1)S(1)} %collective-permute-done.21.refs_1_), channel_id=1, source_target_pairs={{0,28},{4,0},{8,4},{12,8},{16,12},{20,16},{24,20},{28,24},{1,29},{... | collective-permute-start | bytes 786440 | tf_op jit(solution)/shard_map/ppermute | solution.py:347
  130.2 7.8 %collective-permute-start.27 = (bf16[8,128,128]{2,1,0:T(8,128)(2,1)S(1)}, bf16[8,128,128]{2,1,0:T(8,128)(2,1)S(1)}, u32[]{:S(2)}, u32[]{:S(2)}) collective-permute-start(bf16[8,128,128]{2,1,0:T(8,128)(2,1)S(1)} %collective-permute-done.20.refs_0_), channel_id=1, source_target_pairs={{0,1},{1,2},{2,3},{3,0},{4,5},{5,6},{6,7},{7,4},{8,9},{9,10},{10,1... | collective-permute-start | bytes 786440 | tf_op jit(solution)/shard_map/ppermute | solution.py:347
  130.2 11.0 %collective-permute-start.28 = (bf16[8,128,128]{2,1,0:T(8,128)(2,1)S(1)}, bf16[8,128,128]{2,1,0:T(8,128)(2,1)S(1)}, u32[]{:S(2)}, u32[]{:S(2)}) collective-permute-start(bf16[8,128,128]{2,1,0:T(8,128)(2,1)S(1)} %collective-permute-done.21.refs_1_), channel_id=1, source_target_pairs={{0,3},{1,0},{2,1},{3,2},{4,7},{5,4},{6,5},{7,6},{8,11},{9,8},{10,9... | collective-permute-start | bytes 786440 | tf_op jit(solution)/shard_map/ppermute | solution.py:347
  134.7 8.0 %collective-permute-start.25 = (bf16[8,128,128]{2,1,0:T(8,128)(2,1)S(1)}, bf16[8,128,128]{2,1,0:T(8,128)(2,1)S(1)}, u32[]{:S(2)}, u32[]{:S(2)}) collective-permute-start(bf16[8,128,128]{2,1,0:T(8,128)(2,1)S(1)} %collective-permute-done.22.refs_0_), channel_id=1, source_target_pairs={{0,4},{4,8},{8,12},{12,16},{16,20},{20,24},{24,28},{28,0},{1,5},{5... | collective-permute-start | bytes 786440 | tf_op jit(solution)/shard_map/ppermute | solution.py:347
  134.8 7.9 %collective-permute-start.26 = (bf16[8,128,128]{2,1,0:T(8,128)(2,1)S(1)}, bf16[8,128,128]{2,1,0:T(8,128)(2,1)S(1)}, u32[]{:S(2)}, u32[]{:S(2)}) collective-permute-start(bf16[8,128,128]{2,1,0:T(8,128)(2,1)S(1)} %collective-permute-done.23.refs_1_), channel_id=1, source_target_pairs={{0,28},{4,0},{8,4},{12,8},{16,12},{20,16},{24,20},{28,24},{1,29},{... | collective-permute-start | bytes 786440 | tf_op jit(solution)/shard_map/ppermute | solution.py:347
  138.0 11.0 %collective-permute-start.31 = (bf16[8,128,128]{2,1,0:T(8,128)(2,1)S(1)}, bf16[8,128,128]{2,1,0:T(8,128)(2,1)S(1)}, u32[]{:S(2)}, u32[]{:S(2)}) collective-permute-start(bf16[8,128,128]{2,1,0:T(8,128)(2,1)S(1)} %collective-permute-done.22.refs_0_), channel_id=1, source_target_pairs={{0,1},{1,2},{2,3},{3,0},{4,5},{5,6},{6,7},{7,4},{8,9},{9,10},{10,1... | collective-permute-start | bytes 786440 | tf_op jit(solution)/shard_map/ppermute | solution.py:347
  138.0 11.0 %collective-permute-start.32 = (bf16[8,128,128]{2,1,0:T(8,128)(2,1)S(1)}, bf16[8,128,128]{2,1,0:T(8,128)(2,1)S(1)}, u32[]{:S(2)}, u32[]{:S(2)}) collective-permute-start(bf16[8,128,128]{2,1,0:T(8,128)(2,1)S(1)} %collective-permute-done.23.refs_1_), channel_id=1, source_target_pairs={{0,3},{1,0},{2,1},{3,2},{4,7},{5,4},{6,5},{7,6},{8,11},{9,8},{10,9... | collective-permute-start | bytes 786440 | tf_op jit(solution)/shard_map/ppermute | solution.py:347
  142.7 14.5 %collective-permute-start.35 = (bf16[8,128,128]{2,1,0:T(8,128)(2,1)S(1)}, bf16[8,128,128]{2,1,0:T(8,128)(2,1)S(1)}, u32[]{:S(2)}, u32[]{:S(2)}) collective-permute-start(bf16[8,128,128]{2,1,0:T(8,128)(2,1)S(1)} %collective-permute-done.25.refs_0_), channel_id=1, source_target_pairs={{0,1},{1,2},{2,3},{3,0},{4,5},{5,6},{6,7},{7,4},{8,9},{9,10},{10,1... | collective-permute-start | bytes 786440 | tf_op jit(solution)/shard_map/ppermute | solution.py:347
  142.8 14.4 %collective-permute-start.36 = (bf16[8,128,128]{2,1,0:T(8,128)(2,1)S(1)}, bf16[8,128,128]{2,1,0:T(8,128)(2,1)S(1)}, u32[]{:S(2)}, u32[]{:S(2)}) collective-permute-start(bf16[8,128,128]{2,1,0:T(8,128)(2,1)S(1)} %collective-permute-done.26.refs_1_), channel_id=1, source_target_pairs={{0,3},{1,0},{2,1},{3,2},{4,7},{5,4},{6,5},{7,6},{8,11},{9,8},{10,9... | collective-permute-start | bytes 786440 | tf_op jit(solution)/shard_map/ppermute | solution.py:347
  146.1 5.4 %collective-permute-start.30 = (bf16[4,128,128]{2,1,0:T(8,128)(2,1)S(1)}, bf16[4,128,128]{2,1,0:T(8,128)(2,1)S(1)}, u32[]{:S(2)}, u32[]{:S(2)}) collective-permute-start(bf16[4,128,128]{2,1,0:T(8,128)(2,1)S(1)} %slice.71), channel_id=1, source_target_pairs={{0,28},{4,0},{8,4},{12,8},{16,12},{20,16},{24,20},{28,24},{1,29},{... | collective-permute-start | bytes 393224 | tf_op jit(solution)/shard_map/ppermute | solution.py:347
  149.0 6.2 %collective-permute-start.29 = (bf16[4,128,128]{2,1,0:T(8,128)(2,1)S(1)}, bf16[4,128,128]{2,1,0:T(8,128)(2,1)S(1)}, u32[]{:S(2)}, u32[]{:S(2)}) collective-permute-start(bf16[4,128,128]{2,1,0:T(8,128)(2,1)S(1)} %slice.70), channel_id=1, source_target_pairs={{0,4},{4,8},{8,12},{12,16},{16,20},{20,24},{24,28},{28,0},{1,5},{5... | collective-permute-start | bytes 393224 | tf_op jit(solution)/shard_map/ppermute | solution.py:347
  155.2 5.0 %collective-permute-start.34 = (bf16[4,128,128]{2,1,0:T(8,128)(2,1)S(1)}, bf16[4,128,128]{2,1,0:T(8,128)(2,1)S(1)}, u32[]{:S(2)}, u32[]{:S(2)}) collective-permute-start(bf16[4,128,128]{2,1,0:T(8,128)(2,1)S(1)} %collective-permute-done.29.refs_0_), channel_id=1, source_target_pairs={{0,3},{1,0},{2,1},{3,2},{4,7},{5,4},{6,5},{7,6},{8,11},{9,8},{10,9... | collective-permute-start | bytes 393224 | tf_op jit(solution)/shard_map/ppermute | solution.py:347
  155.3 6.2 %collective-permute-start.33 = (bf16[4,128,128]{2,1,0:T(8,128)(2,1)S(1)}, bf16[4,128,128]{2,1,0:T(8,128)(2,1)S(1)}, u32[]{:S(2)}, u32[]{:S(2)}) collective-permute-start(bf16[4,128,128]{2,1,0:T(8,128)(2,1)S(1)} %collective-permute-done.29.refs_0_), channel_id=1, source_target_pairs={{0,1},{1,2},{2,3},{3,0},{4,5},{5,6},{6,7},{7,4},{8,9},{9,10},{10,1... | collective-permute-start | bytes 393224 | tf_op jit(solution)/shard_map/ppermute | solution.py:347

commit v2 on v1

--- a/solution.py
+++ b/solution.py
@@ -60,11 +60,10 @@
         at = pl.ds(pl.multiple_of(c * 128, 128), 128)
         x = jnp.broadcast_to(v_ref[c], (16, 512))
         r = pltpu.roll(x, 1, 1, stride=1, stride_axis=0)
-        lo = jnp.where(low, r, 0.0)
-        hi = jnp.where(low, 0.0, r)
         for p in range(8):
-            lp = (pltpu.roll(lo, 512 - 16 * p, 1) if p else lo).astype(BF)
-            hp = (pltpu.roll(hi, 512 - 16 * p, 1) if p else hi).astype(BF)
+            rp = pltpu.roll(r, 512 - 16 * p, 1) if p else r
+            lp = jnp.where(low, rp, 0.0).astype(BF)
+            hp = jnp.where(low, 0.0, rp).astype(BF)
             for wy in range(24):
                 dy, yw = wy // 8, wy % 8
                 if (24 - wy) % 8 == p:
@@ -240,7 +239,7 @@
 
 
 def cut_kernel(shard_ref, region_ref, g0, g1, g2, g3, own_ref, up_ref, down_ref, far_ref, *rest):
-    outs, (canvas, sums, digits, lists, list_sem) = rest[:NZ], rest[NZ:]
+    outs, (canvas, sums, digits, lists, list_sem) = rest[: NZ + 1], rest[NZ + 1 :]
     digits[...] = jnp.zeros(digits.shape, jnp.int32)
     for k, g in enumerate((g0, g1, g2, g3)):
         tile = g[TR:, :128].astype(F32)
@@ -283,18 +282,23 @@
 
         lax.fori_loop(0, INST_DEV, one, 0)
     for d in range(NZ):
-        outs[d][...] = sums[d].astype(outs[d].dtype)
+        if d == 4:
+            outs[4][...] = sums[4, :2].astype(BF)
+            outs[NZ][...] = sums[4, 2:].astype(BF)
+        else:
+            outs[d][...] = sums[d].astype(outs[d].dtype)
 
 
 def cut(shard, region, grads, bands):
     vm = pl.BlockSpec(memory_space=pltpu.VMEM)
     sm = pl.BlockSpec(memory_space=pltpu.SMEM)
     slot = (4, P_SIZE, P_SIZE)
+    half = jax.ShapeDtypeStruct((2, P_SIZE, P_SIZE), BF)
     return pl.pallas_call(
         cut_kernel,
-        out_shape=[jax.ShapeDtypeStruct(slot, F32)] + [jax.ShapeDtypeStruct(slot, BF)] * (NZ - 1),
+        out_shape=[jax.ShapeDtypeStruct(slot, F32 if d in (0, 2, 6) else BF) if d != 4 else half for d in range(NZ)] + [half],
         in_specs=[sm] * 2 + [vm] * 8,
-        out_specs=[vm] * NZ,
+        out_specs=[vm] * (NZ + 1),
         scratch_shapes=[
             pltpu.VMEM((NY, 8 * TR + 8, WIDE), F32),
             pltpu.VMEM((NZ, 4, P_SIZE, P_SIZE), F32),
@@ -355,10 +359,15 @@
 
 
 def sum_along_z(slots):
-    total = slots[0]
-    for d in (4, 3, 5, 2, 6, 1, 7):
-        total = total + shift(slots[d], "z", d).astype(F32)
-    return total
+    own, one, two, three, low, five, six, seven, high = slots
+    three, five = shift(three, "z", 1), shift(five, "z", -1)
+    low, high = shift(low, "z", 2).astype(F32), shift(high, "z", -2).astype(F32)
+    three, one, seven = lax.optimization_barrier((three, one, seven))
+    two, six = two + three.astype(F32), six + five.astype(F32)
+    two = jnp.concatenate([two[:2] + low, two[2:]])
+    six = jnp.concatenate([six[:2], six[2:] + high])
+    near = shift(one, "z", 1).astype(F32) + shift(seven, "z", -1).astype(F32)
+    return own + near + shift(two.astype(BF), "z", 2).astype(F32) + shift(six.astype(BF), "z", -2).astype(F32)
 
 
 def spread(part, region):
@@ -369,17 +378,16 @@
     for d in (1, 2, 3):
         ups, downs, out = lax.optimization_barrier((ups, downs, out))
         here = [(ups, -d, (0, 2)), (downs, d, (0, 2))]
+        ups = shift(ups, "z", 1)
         if d < 3:
-            ups, downs = shift(ups, "z", 1), shift(downs, "z", -1)
-        else:
-            ups, downs = shift(ups[:4], "z", 1), shift(downs[4:], "z", -1)
+            downs = shift(downs, "z", -1)
         side = [(shift(here[0][0], "y", 1), -d, (1, 3)), (shift(here[1][0], "y", -1), d, (3, 1))]
         out = deposit(region, out, here + came)
         came = side
-    ups, downs, out = lax.optimization_barrier((ups, downs, out))
-    side = [(shift(ups, "y", 1), -4, (1,)), (shift(ups, "y", -1), -4, (3,))]
-    out = deposit(region, out, [(ups, -4, (0,)), (downs, -4, (2,))] + came)
-    out = deposit(region, out, side)
+    ups, out = lax.optimization_barrier((ups, out))
+    side = shift(ups, "y", 1)
+    out = deposit(region, out, [(ups, -4, (0, 2))] + came)
+    out = deposit(region, out, [(side, -4, (1, 3))])
     return out.reshape(MAS_DEV, P_SIZE, P_SIZE)
 
 
@@ -388,11 +396,11 @@
     region = lax.axis_index(("z", "y")).reshape(1)
     mine, theirs, info = place(shard, inst_master, inst_row, inst_col, masters)
     other = shift(theirs, "core", 1)
+    table = make_table(kernels)
     sums = [mine[d] + other[d].astype(F32) for d in range(NX)]
     parts = [sums[0]] + [shift(sums[d].astype(BF), "x", d) for d in (2, 1, 3)]
     tmid = target[0]
     tabove, tbelow = halo(tmid, ("x", "core"), 16)
-    table = make_table(kernels)
     resist, grad = image(def_index, shard, def_weights, parts, tabove, tmid, tbelow, info, table)
     grads = [grad] + [shift(grad, "y", k) for k in (1, 2, 3)]
     own = jnp.stack([g[:TR] for g in grads])

time: 163 us -> 154 us (0.945)
  starting transfers between devices: 64.2 us -> 56.9 us
    ppermute x35 -> x34, starting transfers between devices: 59.9 us -> 52.6 us  [shift(): return lax.ppermute(v, axis, [(i, (i + by) % n) for i in range(n)])]
    ppermute x35 -> x34, waiting for transfers between devices: 54.3 us -> 53.6 us  [shift(): return lax.ppermute(v, axis, [(i, (i + by) % n) for i in range(n)])]
  transfers between devices with their start and end apart: 37 -> 36, of which waited for: 18 -> 20; matrix products, arithmetic and copies ran while one was open for 0% -> 1% of each run, Pallas kernels for 7% -> 7%
where the time goes in v2:
time: 154 us
  starting transfers between devices  56.9 us (37%)
  waiting for transfers between devices  53.6 us (35%)
  Pallas kernels  30.1 us (20%)
  blocking collectives  9.43 us (6%)
  between operations  1.83 us (1%)
  other arithmetic  1.73 us (1%)
    ppermute x34, waiting for transfers between devices, shift(): return lax.ppermute(v, axis, [(i, (i + by) % n) for i in range(n)])  53.6 us
    ppermute x34, starting transfers between devices, shift(): return lax.ppermute(v, axis, [(i, (i + by) % n) for i in range(n)])  52.6 us
    all_gather x4, blocking collectives, body(): bands = [lax.all_gather(v, 'core') for v in (own, up, down, far)]  9.43 us
    pallas_call x1, Pallas kernels, image(): pl.pallas_call(image_kernel, out_shape=(jax.ShapeDtypeStruct((TR, TC), BF...  9.12 us
    pallas_call x6, Pallas kernels, deposit(): pl.pallas_call(functools.partial(deposit_kernel, places, n + len(old)), o...  6.84 us
    pallas_call x1, Pallas kernels, place(): pl.pallas_call(place_kernel, out_shape=(jax.ShapeDtypeStruct(bands, F32),...  4.8 us
    pallas_call x1, Pallas kernels, make_table(): pl.pallas_call(table_kernel, out_shape=jax.ShapeDtypeStruct((K, 2 * KERN...  4.74 us
    pallas_call x1, Pallas kernels, cut(): pl.pallas_call(cut_kernel, out_shape=[jax.ShapeDtypeStruct(slot, F32 if d...  4.62 us
  transfers between devices with their start and end apart: 36, of which 20 were waited for; matrix products, arithmetic and copies ran while one was open for 1% of the time, Pallas kernels for 7%

profile of v2, /device:TPU:6, one launch (start us, length us, event | category | flops | bytes accessed | tf_op | source)
XLA Modules:
  0.0 154.4 jit_solution(9598688723404769153)
XLA Ops:
  0.7 4.8 %place.1 = (f32[4,80,1024]{2,1,0:T(8,128)}, bf16[4,80,1024]{2,1,0:T(8,128)(2,1)}, s32[1,128]{1,0:T(1,128)}) custom-call(s32[1]{0:T(128)} %bitcast.1.shard_ref, s32[8,1,16]{2,1,0:T(1,128)} %ids_hbm.1, s32[8,1,16]{2,1,0:T(1,128)} %rows_hbm.1, s32[8,1,16]{2,1,0:T(1,128)} %cols_hbm.1, f32[128,128,128]{2,1,0:T(8,128)} %masters_hbm.1), custom_call_target="tpu_custom_call" | custom-call | flops 1000000 | bytes 12000000 | tf_op jit(solution)/shard_map/place/pallas_call | solution.py:223
  5.6 2.3 %collective-permute-done = bf16[4,80,1024]{2,1,0:T(8,128)(2,1)S(1)} collective-permute-done((bf16[4,80,1024]{2,1,0:T(8,128)(2,1)}, bf16[4,80,1024]{2,1,0:T(8,128)(2,1)S(1)}, u32[]{:S(2)}, u32[]{:S(2)}) %collective-permute-start) | collective-permute-done | bytes 655392 | tf_op jit(solution)/shard_map/ppermute | solution.py:351
  7.9 1.4 fusion.2
  9.3 0.9 collective-permute-start.3
  10.3 2.4 %collective-permute-start.2 = (bf16[80,1024]{1,0:T(8,128)(2,1)S(1)}, bf16[80,1024]{1,0:T(8,128)(2,1)S(1)}, u32[]{:S(2)}, u32[]{:S(2)}) collective-permute-start(bf16[80,1024]{1,0:T(8,128)(2,1)S(1)} %get-tuple-element.59), channel_id=1, source_target_pairs={{0,64},{64,128},{128,192},{192,0},{1,65},{65,129},{129,193},{193,1... | collective-permute-start | bytes 491528 | tf_op jit(solution)/shard_map/ppermute | solution.py:351
  12.7 0.4 collective-permute-start.1
  13.1 2.2 %collective-permute-start.5 = (bf16[16,1024]{1,0:T(8,128)(2,1)S(1)}, bf16[16,1024]{1,0:T(8,128)(2,1)S(1)}, u32[]{:S(2)}, u32[]{:S(2)}) collective-permute-start(bf16[16,1024]{1,0:T(8,128)(2,1)S(1)} %get-tuple-element.62), channel_id=1, source_target_pairs={{32,0},{64,32},{96,64},{128,96},{160,128},{192,160},{224,192},{33,... | collective-permute-start | bytes 98312 | tf_op jit(solution)/shard_map/ppermute | solution.py:357
  15.3 2.1 %collective-permute-start.4 = (bf16[16,1024]{1,0:T(8,128)(2,1)S(1)}, bf16[16,1024]{1,0:T(8,128)(2,1)S(1)}, u32[]{:S(2)}, u32[]{:S(2)}) collective-permute-start(bf16[16,1024]{1,0:T(8,128)(2,1)S(1)} %get-tuple-element.63), channel_id=1, source_target_pairs={{0,32},{32,64},{64,96},{96,128},{128,160},{160,192},{192,224},{1,3... | collective-permute-start | bytes 98312 | tf_op jit(solution)/shard_map/ppermute | solution.py:356
  18.2 0.1 copy.20
  18.6 0.1 pad.4.clone
  18.7 0.2 reshape.55.v_ref
  18.9 4.7 %taps_table.1.w_ref = bf16[768,3072]{1,0:T(8,128)(2,1)S(1)} custom-call(f32[24,1,512]{2,1,0:T(1,128)S(1)} %reshape.55.v_ref), custom_call_target="tpu_custom_call" | custom-call | flops 20000000 | bytes 10000000 | tf_op jit(solution)/shard_map/taps_table/pallas_call | solution.py:88
  23.7 9.1 %image.1 = (bf16[48,1024]{1,0:T(8,128)(2,1)}, bf16[64,1024]{1,0:T(8,128)(2,1)S(1)}) custom-call(s32[1]{0:T(128)S(6)} %copy.29.level_ref, s32[1]{0:T(128)} %bitcast.1.shard_ref, f32[8,12]{1,0:T(8,128)S(1)} %copy-done.1, f32[80,1024]{1,0:T(8,128)S(1)} %get-tuple-element.61.m0_ref, bf16[80,1024]{1,0:T(8,128)(2,1)S(1)} %collective-permute-done.1.m1_ref, ...), custom_call_target="tpu_custom_call" | custom-call | flops 5000000000 | bytes 8000000 | tf_op jit(solution)/shard_map/image/pallas_call | solution.py:154
  32.8 2.8 %collective-permute-start.8 = (bf16[64,1024]{1,0:T(8,128)(2,1)S(1)}, bf16[64,1024]{1,0:T(8,128)(2,1)S(1)}, u32[]{:S(2)}, u32[]{:S(2)}) collective-permute-start(bf16[64,1024]{1,0:T(8,128)(2,1)S(1)} %get-tuple-element.33.g0), channel_id=1, source_target_pairs={{0,3},{1,0},{2,1},{3,2},{4,7},{5,4},{6,5},{7,6},{8,11},{9,8},{10,9... | collective-permute-start | bytes 393224 | tf_op jit(solution)/shard_map/ppermute | solution.py:351
  35.6 0.6 collective-permute-start.7
  36.2 1.0 collective-permute-start.6
  37.2 3.5 %collective-permute-done.8.g3 = bf16[64,1024]{1,0:T(8,128)(2,1)S(1)} collective-permute-done((bf16[64,1024]{1,0:T(8,128)(2,1)S(1)}, bf16[64,1024]{1,0:T(8,128)(2,1)S(1)}, u32[]{:S(2)}, u32[]{:S(2)}) %collective-permute-start.8) | collective-permute-done | bytes 131104 | tf_op jit(solution)/shard_map/ppermute | solution.py:351
  40.8 2.3 %collective-permute-done.7.g2 = bf16[64,1024]{1,0:T(8,128)(2,1)S(1)} collective-permute-done((bf16[64,1024]{1,0:T(8,128)(2,1)S(1)}, bf16[64,1024]{1,0:T(8,128)(2,1)S(1)}, u32[]{:S(2)}, u32[]{:S(2)}) %collective-permute-start.7) | collective-permute-done | bytes 131104 | tf_op jit(solution)/shard_map/ppermute | solution.py:351
  43.1 1.3 collective-permute-done.6.g1
  44.5 4.6 %collective-permute-start.11 = (bf16[4,48,1024]{2,1,0:T(8,128)(2,1)S(1)}, bf16[4,48,1024]{2,1,0:T(8,128)(2,1)S(1)}, u32[]{:S(2)}, u32[]{:S(2)}) collective-permute-start(bf16[4,48,1024]{2,1,0:T(8,128)(2,1)S(1)} %pad_maximum_fusion), channel_id=1, source_target_pairs={{0,128},{64,192},{128,0},{192,64},{1,129},{65,193},{129,1},{193,65... | collective-permute-start | bytes 1179656 | tf_op jit(solution)/shard_map/ppermute | solution.py:351
  49.1 0.3 collective-permute-start.10
  49.4 2.9 %collective-permute-start.9 = (bf16[4,48,1024]{2,1,0:T(8,128)(2,1)S(1)}, bf16[4,48,1024]{2,1,0:T(8,128)(2,1)S(1)}, u32[]{:S(2)}, u32[]{:S(2)}) collective-permute-start(bf16[4,48,1024]{2,1,0:T(8,128)(2,1)S(1)} %pad_maximum_fusion), channel_id=1, source_target_pairs={{0,64},{64,128},{128,192},{192,0},{1,65},{65,129},{129,193},{193,1... | collective-permute-start | bytes 1179656 | tf_op jit(solution)/shard_map/ppermute | solution.py:351
  52.3 2.4 %all-gather = bf16[8,48,1024]{2,1,0:T(8,128)(2,1)S(1)} all-gather(bf16[4,48,1024]{2,1,0:T(8,128)(2,1)S(1)} %pad_maximum_fusion), channel_id=2, replica_groups=mesh['x'=4,'core'=2,'z'=8,'y'=4] {'core'}, dimensions={0}, use_global_device_ids=true | all-gather | bytes 1179648 | tf_op jit(solution)/shard_map/all_gather | solution.py:408
  54.7 4.4 %collective-permute-done.11 = bf16[4,48,1024]{2,1,0:T(8,128)(2,1)S(1)} collective-permute-done((bf16[4,48,1024]{2,1,0:T(8,128)(2,1)S(1)}, bf16[4,48,1024]{2,1,0:T(8,128)(2,1)S(1)}, u32[]{:S(2)}, u32[]{:S(2)}) %collective-permute-start.11) | collective-permute-done | bytes 393248 | tf_op jit(solution)/shard_map/ppermute | solution.py:351
  59.0 2.4 %all-gather.3 = bf16[8,48,1024]{2,1,0:T(8,128)(2,1)S(1)} all-gather(bf16[4,48,1024]{2,1,0:T(8,128)(2,1)S(1)} %collective-permute-done.11), channel_id=5, replica_groups=mesh['x'=4,'core'=2,'z'=8,'y'=4] {'core'}, dimensions={0}, use_global_device_ids=true | all-gather | bytes 1179648 | tf_op jit(solution)/shard_map/all_gather | solution.py:408
  61.4 5.4 %collective-permute-done.10 = bf16[4,48,1024]{2,1,0:T(8,128)(2,1)S(1)} collective-permute-done((bf16[4,48,1024]{2,1,0:T(8,128)(2,1)S(1)}, bf16[4,48,1024]{2,1,0:T(8,128)(2,1)S(1)}, u32[]{:S(2)}, u32[]{:S(2)}) %collective-permute-start.10) | collective-permute-done | bytes 393248 | tf_op jit(solution)/shard_map/ppermute | solution.py:351
  66.8 2.4 %all-gather.2 = bf16[8,48,1024]{2,1,0:T(8,128)(2,1)S(1)} all-gather(bf16[4,48,1024]{2,1,0:T(8,128)(2,1)S(1)} %collective-permute-done.10), channel_id=4, replica_groups=mesh['x'=4,'core'=2,'z'=8,'y'=4] {'core'}, dimensions={0}, use_global_device_ids=true | all-gather | bytes 1179648 | tf_op jit(solution)/shard_map/all_gather | solution.py:408
  69.2 2.4 %all-gather.1 = bf16[8,48,1024]{2,1,0:T(8,128)(2,1)S(1)} all-gather(bf16[4,48,1024]{2,1,0:T(8,128)(2,1)S(1)} %collective-permute-done.9), channel_id=3, replica_groups=mesh['x'=4,'core'=2,'z'=8,'y'=4] {'core'}, dimensions={0}, use_global_device_ids=true | all-gather | bytes 1179648 | tf_op jit(solution)/shard_map/all_gather | solution.py:408
  71.5 4.6 %cut.1 = (f32[4,128,128]{2,1,0:T(8,128)S(1)}, bf16[4,128,128]{2,1,0:T(8,128)(2,1)S(1)}, f32[4,128,128]{2,1,0:T(8,128)S(1)}, bf16[4,128,128]{2,1,0:T(8,128)(2,1)S...) custom-call(s32[1]{0:T(128)} %bitcast.1.shard_ref, ...), custom_call_target="tpu_custom_call" | custom-call | flops 1000000 | bytes 12000000 | tf_op jit(solution)/shard_map/cut/pallas_call | solution.py:297
  76.1 2.2 %collective-permute-start.12 = (bf16[4,128,128]{2,1,0:T(8,128)(2,1)S(1)}, bf16[4,128,128]{2,1,0:T(8,128)(2,1)S(1)}, u32[]{:S(2)}, u32[]{:S(2)}) collective-permute-start(bf16[4,128,128]{2,1,0:T(8,128)(2,1)S(1)} %get-tuple-element.35), channel_id=1, source_target_pairs={{0,4},{4,8},{8,12},{12,16},{16,20},{20,24},{24,28},{28,0},{1,5},{5... | collective-permute-start | bytes 393224 | tf_op jit(solution)/shard_map/ppermute | solution.py:351
  78.4 3.6 %collective-permute-start.15 = (bf16[2,128,128]{2,1,0:T(8,128)(2,1)S(1)}, bf16[2,128,128]{2,1,0:T(8,128)(2,1)S(1)}, u32[]{:S(2)}, u32[]{:S(2)}) collective-permute-start(bf16[2,128,128]{2,1,0:T(8,128)(2,1)S(1)} %get-tuple-element.42), channel_id=1, source_target_pairs={{0,8},{4,12},{8,16},{12,20},{16,24},{20,28},{24,0},{28,4},{1,9},{5... | collective-permute-start | bytes 196616 | tf_op jit(solution)/shard_map/ppermute | solution.py:351
  82.0 1.6 %collective-permute-start.18 = (bf16[2,128,128]{2,1,0:T(8,128)(2,1)S(1)}, bf16[2,128,128]{2,1,0:T(8,128)(2,1)S(1)}, u32[]{:S(2)}, u32[]{:S(2)}) collective-permute-start(bf16[2,128,128]{2,1,0:T(8,128)(2,1)S(1)} %get-tuple-element.45), channel_id=1, source_target_pairs={{0,24},{4,28},{8,0},{12,4},{16,8},{20,12},{24,16},{28,20},{1,25},{... | collective-permute-start | bytes 196616 | tf_op jit(solution)/shard_map/ppermute | solution.py:351
  83.6 1.8 %collective-permute-start.17 = (bf16[4,128,128]{2,1,0:T(8,128)(2,1)S(1)}, bf16[4,128,128]{2,1,0:T(8,128)(2,1)S(1)}, u32[]{:S(2)}, u32[]{:S(2)}) collective-permute-start(bf16[4,128,128]{2,1,0:T(8,128)(2,1)S(1)} %get-tuple-element.44), channel_id=1, source_target_pairs={{0,28},{4,0},{8,4},{12,8},{16,12},{20,16},{24,20},{28,24},{1,29},{... | collective-permute-start | bytes 393224 | tf_op jit(solution)/shard_map/ppermute | solution.py:351
  85.5 0.6 collective-permute-done.12
  86.1 3.2 %collective-permute-start.14 = (bf16[4,128,128]{2,1,0:T(8,128)(2,1)S(1)}, bf16[4,128,128]{2,1,0:T(8,128)(2,1)S(1)}, u32[]{:S(2)}, u32[]{:S(2)}) collective-permute-start(bf16[4,128,128]{2,1,0:T(8,128)(2,1)S(1)} %get-tuple-element.39), channel_id=1, source_target_pairs={{0,28},{4,0},{8,4},{12,8},{16,12},{20,16},{24,20},{28,24},{1,29},{... | collective-permute-start | bytes 393224 | tf_op jit(solution)/shard_map/ppermute | solution.py:351
  89.4 0.2 collective-permute-start.16
  89.6 1.5 collective-permute-done.17
  91.2 2.6 %collective-permute-start.19 = (bf16[4,128,128]{2,1,0:T(8,128)(2,1)S(1)}, bf16[4,128,128]{2,1,0:T(8,128)(2,1)S(1)}, u32[]{:S(2)}, u32[]{:S(2)}) collective-permute-start(bf16[4,128,128]{2,1,0:T(8,128)(2,1)S(1)} %pad_maximum_fusion.3), channel_id=1, source_target_pairs={{0,24},{4,28},{8,0},{12,4},{16,8},{20,12},{24,16},{28,20},{1,25},{... | collective-permute-start | bytes 393224 | tf_op jit(solution)/shard_map/ppermute | solution.py:351
  93.8 3.7 %collective-permute-done.16 = bf16[4,128,128]{2,1,0:T(8,128)(2,1)S(1)} collective-permute-done((bf16[4,128,128]{2,1,0:T(8,128)(2,1)S(1)}, bf16[4,128,128]{2,1,0:T(8,128)(2,1)S(1)}, u32[]{:S(2)}, u32[]{:S(2)}) %collective-permute-start.16) | collective-permute-done | bytes 131104 | tf_op jit(solution)/shard_map/ppermute | solution.py:351
  97.6 2.5 %collective-permute-done.19 = bf16[4,128,128]{2,1,0:T(8,128)(2,1)S(1)} collective-permute-done((bf16[4,128,128]{2,1,0:T(8,128)(2,1)S(1)}, bf16[4,128,128]{2,1,0:T(8,128)(2,1)S(1)}, u32[]{:S(2)}, u32[]{:S(2)}) %collective-permute-start.19) | collective-permute-done | bytes 131104 | tf_op jit(solution)/shard_map/ppermute | solution.py:351
  100.2 1.6 %collective-permute-start.20 = (bf16[4,128,128]{2,1,0:T(8,128)(2,1)S(1)}, bf16[4,128,128]{2,1,0:T(8,128)(2,1)S(1)}, u32[]{:S(2)}, u32[]{:S(2)}) collective-permute-start(bf16[4,128,128]{2,1,0:T(8,128)(2,1)S(1)} %add_convert_fusion.3), channel_id=1, source_target_pairs={{0,2},{1,3},{2,0},{3,1},{4,6},{5,7},{6,4},{7,5},{8,10},{9,11},{10,... | collective-permute-start | bytes 393224 | tf_op jit(solution)/shard_map/ppermute | solution.py:351
  101.8 4.9 %collective-permute-done.20 = bf16[4,128,128]{2,1,0:T(8,128)(2,1)S(1)} collective-permute-done((bf16[4,128,128]{2,1,0:T(8,128)(2,1)S(1)}, bf16[4,128,128]{2,1,0:T(8,128)(2,1)S(1)}, u32[]{:S(2)}, u32[]{:S(2)}) %collective-permute-start.20) | collective-permute-done | bytes 131104 | tf_op jit(solution)/shard_map/ppermute | solution.py:351
  106.7 2.8 %collective-permute-start.22 = (bf16[8,128,128]{2,1,0:T(8,128)(2,1)S(1)}, bf16[8,128,128]{2,1,0:T(8,128)(2,1)S(1)}, u32[]{:S(2)}, u32[]{:S(2)}) collective-permute-start(bf16[8,128,128]{2,1,0:T(8,128)(2,1)S(1)} %pad_maximum_fusion.1.refs_0_), channel_id=1, source_target_pairs={{0,28},{4,0},{8,4},{12,8},{16,12},{20,16},{24,20},{28,24},{1,29},{... | collective-permute-start | bytes 786440 | tf_op jit(solution)/shard_map/ppermute | solution.py:351
  109.5 0.8 deposit.6.refs_3_
  110.3 3.1 %collective-permute-done.22.refs_1_ = bf16[8,128,128]{2,1,0:T(8,128)(2,1)S(1)} collective-permute-done((bf16[8,128,128]{2,1,0:T(8,128)(2,1)S(1)}, bf16[8,128,128]{2,1,0:T(8,128)(2,1)S(1)}, u32[]{:S(2)}, u32[]{:S(2)}) %collective-permute-start.22) | collective-permute-done | bytes 262176 | tf_op jit(solution)/shard_map/ppermute | solution.py:351
  113.4 4.8 %collective-permute-done.21.refs_0_ = bf16[8,128,128]{2,1,0:T(8,128)(2,1)S(1)} collective-permute-done((bf16[8,128,128]{2,1,0:T(8,128)(2,1)S(1)}, bf16[8,128,128]{2,1,0:T(8,128)(2,1)S(1)}, u32[]{:S(2)}, u32[]{:S(2)}) %collective-permute-start.21) | collective-permute-done | bytes 262176 | tf_op jit(solution)/shard_map/ppermute | solution.py:351
  118.2 3.2 %collective-permute-start.24 = (bf16[8,128,128]{2,1,0:T(8,128)(2,1)S(1)}, bf16[8,128,128]{2,1,0:T(8,128)(2,1)S(1)}, u32[]{:S(2)}, u32[]{:S(2)}) collective-permute-start(bf16[8,128,128]{2,1,0:T(8,128)(2,1)S(1)} %collective-permute-done.22.refs_1_), channel_id=1, source_target_pairs={{0,28},{4,0},{8,4},{12,8},{16,12},{20,16},{24,20},{28,24},{1,29},{... | collective-permute-start | bytes 786440 | tf_op jit(solution)/shard_map/ppermute | solution.py:351
  121.5 3.2 %collective-permute-start.29 = (bf16[8,128,128]{2,1,0:T(8,128)(2,1)S(1)}, bf16[8,128,128]{2,1,0:T(8,128)(2,1)S(1)}, u32[]{:S(2)}, u32[]{:S(2)}) collective-permute-start(bf16[8,128,128]{2,1,0:T(8,128)(2,1)S(1)} %collective-permute-done.22.refs_1_), channel_id=1, source_target_pairs={{0,3},{1,0},{2,1},{3,2},{4,7},{5,4},{6,5},{7,6},{8,11},{9,8},{10,9... | collective-permute-start | bytes 786440 | tf_op jit(solution)/shard_map/ppermute | solution.py:351
  124.7 1.2 deposit.7.refs_4_
  125.9 2.3 %collective-permute-done.23.refs_0_ = bf16[8,128,128]{2,1,0:T(8,128)(2,1)S(1)} collective-permute-done((bf16[8,128,128]{2,1,0:T(8,128)(2,1)S(1)}, bf16[8,128,128]{2,1,0:T(8,128)(2,1)S(1)}, u32[]{:S(2)}, u32[]{:S(2)}) %collective-permute-start.23) | collective-permute-done | bytes 262176 | tf_op jit(solution)/shard_map/ppermute | solution.py:351
  128.2 1.6 %collective-permute-start.26 = (bf16[8,128,128]{2,1,0:T(8,128)(2,1)S(1)}, bf16[8,128,128]{2,1,0:T(8,128)(2,1)S(1)}, u32[]{:S(2)}, u32[]{:S(2)}) collective-permute-start(bf16[8,128,128]{2,1,0:T(8,128)(2,1)S(1)} %collective-permute-done.23.refs_0_), channel_id=1, source_target_pairs={{0,4},{4,8},{8,12},{12,16},{16,20},{20,24},{24,28},{28,0},{1,5},{5... | collective-permute-start | bytes 786440 | tf_op jit(solution)/shard_map/ppermute | solution.py:351
  129.8 1.8 %collective-permute-start.27 = (bf16[8,128,128]{2,1,0:T(8,128)(2,1)S(1)}, bf16[8,128,128]{2,1,0:T(8,128)(2,1)S(1)}, u32[]{:S(2)}, u32[]{:S(2)}) collective-permute-start(bf16[8,128,128]{2,1,0:T(8,128)(2,1)S(1)} %collective-permute-done.24.refs_1_), channel_id=1, source_target_pairs={{0,28},{4,0},{8,4},{12,8},{16,12},{20,16},{24,20},{28,24},{1,29},{... | collective-permute-start | bytes 786440 | tf_op jit(solution)/shard_map/ppermute | solution.py:351
  131.6 0.2 collective-permute-done.28.refs_2_
  131.8 3.0 %collective-permute-start.32 = (bf16[8,128,128]{2,1,0:T(8,128)(2,1)S(1)}, bf16[8,128,128]{2,1,0:T(8,128)(2,1)S(1)}, u32[]{:S(2)}, u32[]{:S(2)}) collective-permute-start(bf16[8,128,128]{2,1,0:T(8,128)(2,1)S(1)} %collective-permute-done.24.refs_1_), channel_id=1, source_target_pairs={{0,3},{1,0},{2,1},{3,2},{4,7},{5,4},{6,5},{7,6},{8,11},{9,8},{10,9... | collective-permute-start | bytes 786440 | tf_op jit(solution)/shard_map/ppermute | solution.py:351
  134.9 1.4 deposit.8.refs_4_
  136.3 1.9 %collective-permute-done.26.refs_0_ = bf16[8,128,128]{2,1,0:T(8,128)(2,1)S(1)} collective-permute-done((bf16[8,128,128]{2,1,0:T(8,128)(2,1)S(1)}, bf16[8,128,128]{2,1,0:T(8,128)(2,1)S(1)}, u32[]{:S(2)}, u32[]{:S(2)}) %collective-permute-start.26) | collective-permute-done | bytes 262176 | tf_op jit(solution)/shard_map/ppermute | solution.py:351
  138.2 0.6 collective-permute-start.30
  138.8 3.2 %collective-permute-start.35 = (bf16[8,128,128]{2,1,0:T(8,128)(2,1)S(1)}, bf16[8,128,128]{2,1,0:T(8,128)(2,1)S(1)}, u32[]{:S(2)}, u32[]{:S(2)}) collective-permute-start(bf16[8,128,128]{2,1,0:T(8,128)(2,1)S(1)} %collective-permute-done.27.refs_1_), channel_id=1, source_target_pairs={{0,3},{1,0},{2,1},{3,2},{4,7},{5,4},{6,5},{7,6},{8,11},{9,8},{10,9... | collective-permute-start | bytes 786440 | tf_op jit(solution)/shard_map/ppermute | solution.py:351
  142.0 1.4 deposit.9.refs_3_
  143.4 2.4 %collective-permute-done.30.refs_0_ = bf16[8,128,128]{2,1,0:T(8,128)(2,1)S(1)} collective-permute-done((bf16[8,128,128]{2,1,0:T(8,128)(2,1)S(1)}, bf16[8,128,128]{2,1,0:T(8,128)(2,1)S(1)}, u32[]{:S(2)}, u32[]{:S(2)}) %collective-permute-start.30) | collective-permute-done | bytes 262176 | tf_op jit(solution)/shard_map/ppermute | solution.py:351
  145.9 1.3 collective-permute-done.34.refs_1_
  147.2 1.2 deposit.10.refs_1_
  148.4 4.9 %collective-permute-done.33.refs_0_ = bf16[8,128,128]{2,1,0:T(8,128)(2,1)S(1)} collective-permute-done((bf16[8,128,128]{2,1,0:T(8,128)(2,1)S(1)}, bf16[8,128,128]{2,1,0:T(8,128)(2,1)S(1)}, u32[]{:S(2)}, u32[]{:S(2)}) %collective-permute-start.33) | collective-permute-done | bytes 262176 | tf_op jit(solution)/shard_map/ppermute | solution.py:351
  153.4 0.8 deposit.11
  (53 shorter events, 0.9 us)
Async XLA Ops:
  0.6 12.5 %copy-start = (bf16[1,48,1024]{2,1,0:T(8,128)(2,1)S(1)}, bf16[1,48,1024]{2,1,0:T(8,128)(2,1)}, u32[]{:S(2)}) copy-start(bf16[1,48,1024]{2,1,0:T(8,128)(2,1)} %param.15) | copy-start | bytes 294916
  0.6 17.5 %copy-start.3 = (bf16[24,225]{1,0:T(8,128)(2,1)S(1)}, bf16[24,225]{1,0:T(8,128)(2,1)}, u32[]{:S(2)}) copy-start(bf16[24,225]{1,0:T(8,128)(2,1)} %param.14) | copy-start | bytes 32404
  0.7 23.0 %copy-start.1 = (f32[8,12]{1,0:T(8,128)S(1)}, f32[8,12]{1,0:T(8,128)}, u32[]{:S(2)}) copy-start(f32[8,12]{1,0:T(8,128)} %wgt_ref.1) | copy-start | bytes 1156
  5.5 18.2 %copy-start.2 = (s32[1,128]{1,0:T(1,128)S(1)}, s32[1,128]{1,0:T(1,128)}, u32[]{:S(2)}) copy-start(s32[1,128]{1,0:T(1,128)} %get-tuple-element.32.info_ref) | copy-start | bytes 1540
  5.5 2.4 %collective-permute-start = (bf16[4,80,1024]{2,1,0:T(8,128)(2,1)}, bf16[4,80,1024]{2,1,0:T(8,128)(2,1)S(1)}, u32[]{:S(2)}, u32[]{:S(2)}) collective-permute-start(bf16[4,80,1024]{2,1,0:T(8,128)(2,1)} %get-tuple-element.31), channel_id=1, source_target_pairs={{0,32},{32,0},{1,33},{33,1},{2,34},{34,2},{3,35},{35,3},{4,36},{36... | collective-permute-start | bytes 1966088 | tf_op jit(solution)/shard_map/ppermute | solution.py:351
  9.3 14.3 %collective-permute-start.3 = (bf16[80,1024]{1,0:T(8,128)(2,1)S(1)}, bf16[80,1024]{1,0:T(8,128)(2,1)S(1)}, u32[]{:S(2)}, u32[]{:S(2)}) collective-permute-start(bf16[80,1024]{1,0:T(8,128)(2,1)S(1)} %get-tuple-element.58), channel_id=1, source_target_pairs={{0,192},{64,0},{128,64},{192,128},{1,193},{65,1},{129,65},{193,129... | collective-permute-start | bytes 491528 | tf_op jit(solution)/shard_map/ppermute | solution.py:351
  10.3 13.4 %collective-permute-start.2 = (bf16[80,1024]{1,0:T(8,128)(2,1)S(1)}, bf16[80,1024]{1,0:T(8,128)(2,1)S(1)}, u32[]{:S(2)}, u32[]{:S(2)}) collective-permute-start(bf16[80,1024]{1,0:T(8,128)(2,1)S(1)} %get-tuple-element.59), channel_id=1, source_target_pairs={{0,64},{64,128},{128,192},{192,0},{1,65},{65,129},{129,193},{193,1... | collective-permute-start | bytes 491528 | tf_op jit(solution)/shard_map/ppermute | solution.py:351
  12.7 11.0 %collective-permute-start.1 = (bf16[80,1024]{1,0:T(8,128)(2,1)S(1)}, bf16[80,1024]{1,0:T(8,128)(2,1)S(1)}, u32[]{:S(2)}, u32[]{:S(2)}) collective-permute-start(bf16[80,1024]{1,0:T(8,128)(2,1)S(1)} %get-tuple-element.60), channel_id=1, source_target_pairs={{0,128},{64,192},{128,0},{192,64},{1,129},{65,193},{129,1},{193,65... | collective-permute-start | bytes 491528 | tf_op jit(solution)/shard_map/ppermute | solution.py:351
  13.1 10.5 %collective-permute-start.5 = (bf16[16,1024]{1,0:T(8,128)(2,1)S(1)}, bf16[16,1024]{1,0:T(8,128)(2,1)S(1)}, u32[]{:S(2)}, u32[]{:S(2)}) collective-permute-start(bf16[16,1024]{1,0:T(8,128)(2,1)S(1)} %get-tuple-element.62), channel_id=1, source_target_pairs={{32,0},{64,32},{96,64},{128,96},{160,128},{192,160},{224,192},{33,... | collective-permute-start | bytes 98312 | tf_op jit(solution)/shard_map/ppermute | solution.py:357
  15.3 8.3 %collective-permute-start.4 = (bf16[16,1024]{1,0:T(8,128)(2,1)S(1)}, bf16[16,1024]{1,0:T(8,128)(2,1)S(1)}, u32[]{:S(2)}, u32[]{:S(2)}) collective-permute-start(bf16[16,1024]{1,0:T(8,128)(2,1)S(1)} %get-tuple-element.63), channel_id=1, source_target_pairs={{0,32},{32,64},{64,96},{96,128},{128,160},{160,192},{192,224},{1,3... | collective-permute-start | bytes 98312 | tf_op jit(solution)/shard_map/ppermute | solution.py:356
  32.8 7.9 %collective-permute-start.8 = (bf16[64,1024]{1,0:T(8,128)(2,1)S(1)}, bf16[64,1024]{1,0:T(8,128)(2,1)S(1)}, u32[]{:S(2)}, u32[]{:S(2)}) collective-permute-start(bf16[64,1024]{1,0:T(8,128)(2,1)S(1)} %get-tuple-element.33.g0), channel_id=1, source_target_pairs={{0,3},{1,0},{2,1},{3,2},{4,7},{5,4},{6,5},{7,6},{8,11},{9,8},{10,9... | collective-permute-start | bytes 393224 | tf_op jit(solution)/shard_map/ppermute | solution.py:351
  35.6 7.5 %collective-permute-start.7 = (bf16[64,1024]{1,0:T(8,128)(2,1)S(1)}, bf16[64,1024]{1,0:T(8,128)(2,1)S(1)}, u32[]{:S(2)}, u32[]{:S(2)}) collective-permute-start(bf16[64,1024]{1,0:T(8,128)(2,1)S(1)} %get-tuple-element.33.g0), channel_id=1, source_target_pairs={{0,2},{1,3},{2,0},{3,1},{4,6},{5,7},{6,4},{7,5},{8,10},{9,11},{10,... | collective-permute-start | bytes 393224 | tf_op jit(solution)/shard_map/ppermute | solution.py:351
  36.2 8.2 %collective-permute-start.6 = (bf16[64,1024]{1,0:T(8,128)(2,1)S(1)}, bf16[64,1024]{1,0:T(8,128)(2,1)S(1)}, u32[]{:S(2)}, u32[]{:S(2)}) collective-permute-start(bf16[64,1024]{1,0:T(8,128)(2,1)S(1)} %get-tuple-element.33.g0), channel_id=1, source_target_pairs={{0,1},{1,2},{2,3},{3,0},{4,5},{5,6},{6,7},{7,4},{8,9},{9,10},{10,1... | collective-permute-start | bytes 393224 | tf_op jit(solution)/shard_map/ppermute | solution.py:351
  44.5 14.5 %collective-permute-start.11 = (bf16[4,48,1024]{2,1,0:T(8,128)(2,1)S(1)}, bf16[4,48,1024]{2,1,0:T(8,128)(2,1)S(1)}, u32[]{:S(2)}, u32[]{:S(2)}) collective-permute-start(bf16[4,48,1024]{2,1,0:T(8,128)(2,1)S(1)} %pad_maximum_fusion), channel_id=1, source_target_pairs={{0,128},{64,192},{128,0},{192,64},{1,129},{65,193},{129,1},{193,65... | collective-permute-start | bytes 1179656 | tf_op jit(solution)/shard_map/ppermute | solution.py:351
  49.1 17.7 %collective-permute-start.10 = (bf16[4,48,1024]{2,1,0:T(8,128)(2,1)S(1)}, bf16[4,48,1024]{2,1,0:T(8,128)(2,1)S(1)}, u32[]{:S(2)}, u32[]{:S(2)}) collective-permute-start(bf16[4,48,1024]{2,1,0:T(8,128)(2,1)S(1)} %pad_maximum_fusion), channel_id=1, source_target_pairs={{0,192},{64,0},{128,64},{192,128},{1,193},{65,1},{129,65},{193,129... | collective-permute-start | bytes 1179656 | tf_op jit(solution)/shard_map/ppermute | solution.py:351
  49.4 19.7 %collective-permute-start.9 = (bf16[4,48,1024]{2,1,0:T(8,128)(2,1)S(1)}, bf16[4,48,1024]{2,1,0:T(8,128)(2,1)S(1)}, u32[]{:S(2)}, u32[]{:S(2)}) collective-permute-start(bf16[4,48,1024]{2,1,0:T(8,128)(2,1)S(1)} %pad_maximum_fusion), channel_id=1, source_target_pairs={{0,64},{64,128},{128,192},{192,0},{1,65},{65,129},{129,193},{193,1... | collective-permute-start | bytes 1179656 | tf_op jit(solution)/shard_map/ppermute | solution.py:351
  76.1 9.9 %collective-permute-start.12 = (bf16[4,128,128]{2,1,0:T(8,128)(2,1)S(1)}, bf16[4,128,128]{2,1,0:T(8,128)(2,1)S(1)}, u32[]{:S(2)}, u32[]{:S(2)}) collective-permute-start(bf16[4,128,128]{2,1,0:T(8,128)(2,1)S(1)} %get-tuple-element.35), channel_id=1, source_target_pairs={{0,4},{4,8},{8,12},{12,16},{16,20},{20,24},{24,28},{28,0},{1,5},{5... | collective-permute-start | bytes 393224 | tf_op jit(solution)/shard_map/ppermute | solution.py:351
  78.4 11.0 %collective-permute-start.15 = (bf16[2,128,128]{2,1,0:T(8,128)(2,1)S(1)}, bf16[2,128,128]{2,1,0:T(8,128)(2,1)S(1)}, u32[]{:S(2)}, u32[]{:S(2)}) collective-permute-start(bf16[2,128,128]{2,1,0:T(8,128)(2,1)S(1)} %get-tuple-element.42), channel_id=1, source_target_pairs={{0,8},{4,12},{8,16},{12,20},{16,24},{20,28},{24,0},{28,4},{1,9},{5... | collective-permute-start | bytes 196616 | tf_op jit(solution)/shard_map/ppermute | solution.py:351
  82.0 9.2 %collective-permute-start.18 = (bf16[2,128,128]{2,1,0:T(8,128)(2,1)S(1)}, bf16[2,128,128]{2,1,0:T(8,128)(2,1)S(1)}, u32[]{:S(2)}, u32[]{:S(2)}) collective-permute-start(bf16[2,128,128]{2,1,0:T(8,128)(2,1)S(1)} %get-tuple-element.45), channel_id=1, source_target_pairs={{0,24},{4,28},{8,0},{12,4},{16,8},{20,12},{24,16},{28,20},{1,25},{... | collective-permute-start | bytes 196616 | tf_op jit(solution)/shard_map/ppermute | solution.py:351
  83.6 7.5 %collective-permute-start.17 = (bf16[4,128,128]{2,1,0:T(8,128)(2,1)S(1)}, bf16[4,128,128]{2,1,0:T(8,128)(2,1)S(1)}, u32[]{:S(2)}, u32[]{:S(2)}) collective-permute-start(bf16[4,128,128]{2,1,0:T(8,128)(2,1)S(1)} %get-tuple-element.44), channel_id=1, source_target_pairs={{0,28},{4,0},{8,4},{12,8},{16,12},{20,16},{24,20},{28,24},{1,29},{... | collective-permute-start | bytes 393224 | tf_op jit(solution)/shard_map/ppermute | solution.py:351
  86.1 7.7 %collective-permute-start.13 = (bf16[4,128,128]{2,1,0:T(8,128)(2,1)S(1)}, bf16[4,128,128]{2,1,0:T(8,128)(2,1)S(1)}, u32[]{:S(2)}, u32[]{:S(2)}) collective-permute-start(bf16[4,128,128]{2,1,0:T(8,128)(2,1)S(1)} %get-tuple-element.38), channel_id=1, source_target_pairs={{0,4},{4,8},{8,12},{12,16},{16,20},{20,24},{24,28},{28,0},{1,5},{5... | collective-permute-start | bytes 393224 | tf_op jit(solution)/shard_map/ppermute | solution.py:351
  86.1 7.7 %collective-permute-start.14 = (bf16[4,128,128]{2,1,0:T(8,128)(2,1)S(1)}, bf16[4,128,128]{2,1,0:T(8,128)(2,1)S(1)}, u32[]{:S(2)}, u32[]{:S(2)}) collective-permute-start(bf16[4,128,128]{2,1,0:T(8,128)(2,1)S(1)} %get-tuple-element.39), channel_id=1, source_target_pairs={{0,28},{4,0},{8,4},{12,8},{16,12},{20,16},{24,20},{28,24},{1,29},{... | collective-permute-start | bytes 393224 | tf_op jit(solution)/shard_map/ppermute | solution.py:351
  89.4 8.1 %collective-permute-start.16 = (bf16[4,128,128]{2,1,0:T(8,128)(2,1)S(1)}, bf16[4,128,128]{2,1,0:T(8,128)(2,1)S(1)}, u32[]{:S(2)}, u32[]{:S(2)}) collective-permute-start(bf16[4,128,128]{2,1,0:T(8,128)(2,1)S(1)} %pad_maximum_fusion.2), channel_id=1, source_target_pairs={{0,8},{4,12},{8,16},{12,20},{16,24},{20,28},{24,0},{28,4},{1,9},{5... | collective-permute-start | bytes 393224 | tf_op jit(solution)/shard_map/ppermute | solution.py:351
  91.2 8.8 %collective-permute-start.19 = (bf16[4,128,128]{2,1,0:T(8,128)(2,1)S(1)}, bf16[4,128,128]{2,1,0:T(8,128)(2,1)S(1)}, u32[]{:S(2)}, u32[]{:S(2)}) collective-permute-start(bf16[4,128,128]{2,1,0:T(8,128)(2,1)S(1)} %pad_maximum_fusion.3), channel_id=1, source_target_pairs={{0,24},{4,28},{8,0},{12,4},{16,8},{20,12},{24,16},{28,20},{1,25},{... | collective-permute-start | bytes 393224 | tf_op jit(solution)/shard_map/ppermute | solution.py:351
  100.2 6.6 %collective-permute-start.20 = (bf16[4,128,128]{2,1,0:T(8,128)(2,1)S(1)}, bf16[4,128,128]{2,1,0:T(8,128)(2,1)S(1)}, u32[]{:S(2)}, u32[]{:S(2)}) collective-permute-start(bf16[4,128,128]{2,1,0:T(8,128)(2,1)S(1)} %add_convert_fusion.3), channel_id=1, source_target_pairs={{0,2},{1,3},{2,0},{3,1},{4,6},{5,7},{6,4},{7,5},{8,10},{9,11},{10,... | collective-permute-start | bytes 393224 | tf_op jit(solution)/shard_map/ppermute | solution.py:351
  106.7 6.7 %collective-permute-start.22 = (bf16[8,128,128]{2,1,0:T(8,128)(2,1)S(1)}, bf16[8,128,128]{2,1,0:T(8,128)(2,1)S(1)}, u32[]{:S(2)}, u32[]{:S(2)}) collective-permute-start(bf16[8,128,128]{2,1,0:T(8,128)(2,1)S(1)} %pad_maximum_fusion.1.refs_0_), channel_id=1, source_target_pairs={{0,28},{4,0},{8,4},{12,8},{16,12},{20,16},{24,20},{28,24},{1,29},{... | collective-permute-start | bytes 786440 | tf_op jit(solution)/shard_map/ppermute | solution.py:351
  109.5 8.7 %collective-permute-start.21 = (bf16[8,128,128]{2,1,0:T(8,128)(2,1)S(1)}, bf16[8,128,128]{2,1,0:T(8,128)(2,1)S(1)}, u32[]{:S(2)}, u32[]{:S(2)}) collective-permute-start(bf16[8,128,128]{2,1,0:T(8,128)(2,1)S(1)} %pad_maximum_fusion.1.refs_0_), channel_id=1, source_target_pairs={{0,4},{4,8},{8,12},{12,16},{16,20},{20,24},{24,28},{28,0},{1,5},{5... | collective-permute-start | bytes 786440 | tf_op jit(solution)/shard_map/ppermute | solution.py:351
  109.5 15.2 %collective-permute-start.25 = (bf16[8,128,128]{2,1,0:T(8,128)(2,1)S(1)}, bf16[8,128,128]{2,1,0:T(8,128)(2,1)S(1)}, u32[]{:S(2)}, u32[]{:S(2)}) collective-permute-start(bf16[8,128,128]{2,1,0:T(8,128)(2,1)S(1)} %pad_maximum_fusion.1.refs_0_), channel_id=1, source_target_pairs={{0,1},{1,2},{2,3},{3,0},{4,5},{5,6},{6,7},{7,4},{8,9},{9,10},{10,1... | collective-permute-start | bytes 786440 | tf_op jit(solution)/shard_map/ppermute | solution.py:351
  118.2 9.9 %collective-permute-start.23 = (bf16[8,128,128]{2,1,0:T(8,128)(2,1)S(1)}, bf16[8,128,128]{2,1,0:T(8,128)(2,1)S(1)}, u32[]{:S(2)}, u32[]{:S(2)}) collective-permute-start(bf16[8,128,128]{2,1,0:T(8,128)(2,1)S(1)} %collective-permute-done.21.refs_0_), channel_id=1, source_target_pairs={{0,4},{4,8},{8,12},{12,16},{16,20},{20,24},{24,28},{28,0},{1,5},{5... | collective-permute-start | bytes 786440 | tf_op jit(solution)/shard_map/ppermute | solution.py:351
  118.2 9.9 %collective-permute-start.24 = (bf16[8,128,128]{2,1,0:T(8,128)(2,1)S(1)}, bf16[8,128,128]{2,1,0:T(8,128)(2,1)S(1)}, u32[]{:S(2)}, u32[]{:S(2)}) collective-permute-start(bf16[8,128,128]{2,1,0:T(8,128)(2,1)S(1)} %collective-permute-done.22.refs_1_), channel_id=1, source_target_pairs={{0,28},{4,0},{8,4},{12,8},{16,12},{20,16},{24,20},{28,24},{1,29},{... | collective-permute-start | bytes 786440 | tf_op jit(solution)/shard_map/ppermute | solution.py:351
  121.5 10.3 %collective-permute-start.28 = (bf16[8,128,128]{2,1,0:T(8,128)(2,1)S(1)}, bf16[8,128,128]{2,1,0:T(8,128)(2,1)S(1)}, u32[]{:S(2)}, u32[]{:S(2)}) collective-permute-start(bf16[8,128,128]{2,1,0:T(8,128)(2,1)S(1)} %collective-permute-done.21.refs_0_), channel_id=1, source_target_pairs={{0,1},{1,2},{2,3},{3,0},{4,5},{5,6},{6,7},{7,4},{8,9},{9,10},{10,1... | collective-permute-start | bytes 786440 | tf_op jit(solution)/shard_map/ppermute | solution.py:351
  121.5 13.4 %collective-permute-start.29 = (bf16[8,128,128]{2,1,0:T(8,128)(2,1)S(1)}, bf16[8,128,128]{2,1,0:T(8,128)(2,1)S(1)}, u32[]{:S(2)}, u32[]{:S(2)}) collective-permute-start(bf16[8,128,128]{2,1,0:T(8,128)(2,1)S(1)} %collective-permute-done.22.refs_1_), channel_id=1, source_target_pairs={{0,3},{1,0},{2,1},{3,2},{4,7},{5,4},{6,5},{7,6},{8,11},{9,8},{10,9... | collective-permute-start | bytes 786440 | tf_op jit(solution)/shard_map/ppermute | solution.py:351
  128.2 10.0 %collective-permute-start.26 = (bf16[8,128,128]{2,1,0:T(8,128)(2,1)S(1)}, bf16[8,128,128]{2,1,0:T(8,128)(2,1)S(1)}, u32[]{:S(2)}, u32[]{:S(2)}) collective-permute-start(bf16[8,128,128]{2,1,0:T(8,128)(2,1)S(1)} %collective-permute-done.23.refs_0_), channel_id=1, source_target_pairs={{0,4},{4,8},{8,12},{12,16},{16,20},{20,24},{24,28},{28,0},{1,5},{5... | collective-permute-start | bytes 786440 | tf_op jit(solution)/shard_map/ppermute | solution.py:351
  129.8 8.4 %collective-permute-start.27 = (bf16[8,128,128]{2,1,0:T(8,128)(2,1)S(1)}, bf16[8,128,128]{2,1,0:T(8,128)(2,1)S(1)}, u32[]{:S(2)}, u32[]{:S(2)}) collective-permute-start(bf16[8,128,128]{2,1,0:T(8,128)(2,1)S(1)} %collective-permute-done.24.refs_1_), channel_id=1, source_target_pairs={{0,28},{4,0},{8,4},{12,8},{16,12},{20,16},{24,20},{28,24},{1,29},{... | collective-permute-start | bytes 786440 | tf_op jit(solution)/shard_map/ppermute | solution.py:351
  131.6 10.4 %collective-permute-start.31 = (bf16[8,128,128]{2,1,0:T(8,128)(2,1)S(1)}, bf16[8,128,128]{2,1,0:T(8,128)(2,1)S(1)}, u32[]{:S(2)}, u32[]{:S(2)}) collective-permute-start(bf16[8,128,128]{2,1,0:T(8,128)(2,1)S(1)} %collective-permute-done.23.refs_0_), channel_id=1, source_target_pairs={{0,1},{1,2},{2,3},{3,0},{4,5},{5,6},{6,7},{7,4},{8,9},{9,10},{10,1... | collective-permute-start | bytes 786440 | tf_op jit(solution)/shard_map/ppermute | solution.py:351
  131.8 10.2 %collective-permute-start.32 = (bf16[8,128,128]{2,1,0:T(8,128)(2,1)S(1)}, bf16[8,128,128]{2,1,0:T(8,128)(2,1)S(1)}, u32[]{:S(2)}, u32[]{:S(2)}) collective-permute-start(bf16[8,128,128]{2,1,0:T(8,128)(2,1)S(1)} %collective-permute-done.24.refs_1_), channel_id=1, source_target_pairs={{0,3},{1,0},{2,1},{3,2},{4,7},{5,4},{6,5},{7,6},{8,11},{9,8},{10,9... | collective-permute-start | bytes 786440 | tf_op jit(solution)/shard_map/ppermute | solution.py:351
  138.2 7.6 %collective-permute-start.30 = (bf16[8,128,128]{2,1,0:T(8,128)(2,1)S(1)}, bf16[8,128,128]{2,1,0:T(8,128)(2,1)S(1)}, u32[]{:S(2)}, u32[]{:S(2)}) collective-permute-start(bf16[8,128,128]{2,1,0:T(8,128)(2,1)S(1)} %collective-permute-done.26.refs_0_), channel_id=1, source_target_pairs={{0,4},{4,8},{8,12},{12,16},{16,20},{20,24},{24,28},{28,0},{1,5},{5... | collective-permute-start | bytes 786440 | tf_op jit(solution)/shard_map/ppermute | solution.py:351
  138.8 8.4 %collective-permute-start.34 = (bf16[8,128,128]{2,1,0:T(8,128)(2,1)S(1)}, bf16[8,128,128]{2,1,0:T(8,128)(2,1)S(1)}, u32[]{:S(2)}, u32[]{:S(2)}) collective-permute-start(bf16[8,128,128]{2,1,0:T(8,128)(2,1)S(1)} %collective-permute-done.26.refs_0_), channel_id=1, source_target_pairs={{0,1},{1,2},{2,3},{3,0},{4,5},{5,6},{6,7},{7,4},{8,9},{9,10},{10,1... | collective-permute-start | bytes 786440 | tf_op jit(solution)/shard_map/ppermute | solution.py:351
  138.8 7.1 %collective-permute-start.35 = (bf16[8,128,128]{2,1,0:T(8,128)(2,1)S(1)}, bf16[8,128,128]{2,1,0:T(8,128)(2,1)S(1)}, u32[]{:S(2)}, u32[]{:S(2)}) collective-permute-start(bf16[8,128,128]{2,1,0:T(8,128)(2,1)S(1)} %collective-permute-done.27.refs_1_), channel_id=1, source_target_pairs={{0,3},{1,0},{2,1},{3,2},{4,7},{5,4},{6,5},{7,6},{8,11},{9,8},{10,9... | collective-permute-start | bytes 786440 | tf_op jit(solution)/shard_map/ppermute | solution.py:351
  145.8 7.6 %collective-permute-start.33 = (bf16[8,128,128]{2,1,0:T(8,128)(2,1)S(1)}, bf16[8,128,128]{2,1,0:T(8,128)(2,1)S(1)}, u32[]{:S(2)}, u32[]{:S(2)}) collective-permute-start(bf16[8,128,128]{2,1,0:T(8,128)(2,1)S(1)} %collective-permute-done.30.refs_0_), channel_id=1, source_target_pairs={{0,1},{1,2},{2,3},{3,0},{4,5},{5,6},{6,7},{7,4},{8,9},{9,10},{10,1... | collective-permute-start | bytes 786440 | tf_op jit(solution)/shard_map/ppermute | solution.py:351

commit v3 on v2

--- a/solution.py
+++ b/solution.py
@@ -15,6 +15,9 @@
 M = ROWB * COLB
 K = 6 * 128
 F32, BF = jnp.float32, jnp.bfloat16
+NX, NC, NY, NZ = 4, 2, 4, 8
+LEAD = 16
+EXT = TR + 2 * LEAD
 
 
 def swap_chunks(x):
@@ -96,10 +99,11 @@
     )(taps_rows(kernels))
 
 
-def image_kernel(level_ref, shard_ref, wgt_ref, m0_ref, m1_ref, m2_ref, m3_ref, tabove_ref, tmid_ref, tbelow_ref, info_ref, w_ref,
+def image_kernel(level_ref, shard_ref, wgt_ref, m0_ref, m1_ref, m2_ref, m3_ref, rims_ref, tmid_ref, info_ref, w_ref,
                  resist_ref, grad_ref, lhs_ref, fields_ref, cot_ref):
     level_at = level_ref[0]
-    x = m0_ref[...] + m1_ref[...].astype(F32) + m2_ref[...].astype(F32) + m3_ref[...].astype(F32)
+    m1, m3 = m1_ref[...].astype(F32), m3_ref[...].astype(F32)
+    x = m0_ref[...] + m1[:EXT] + m2_ref[...].astype(F32) + m3[:EXT]
     x = x.astype(BF).astype(F32)
     x = pltpu.roll(x, 8 * MROWB - 1, 0)
     x = jnp.concatenate([x, jnp.zeros((8 * MROWB, 128), F32)], axis=1)
@@ -117,7 +121,11 @@
         intensity = intensity + wgt_ref[level_at, c] * (f[:, :128] + f[:, 128:])
     level = 1.0 / (1.0 + jnp.exp(-STEEP * (intensity - THRESH)))
     resist_ref[...] = from_blocks(level, ROWB, 8)[8 : 8 + TR].astype(BF)
-    goal = jnp.concatenate([tabove_ref[...].astype(F32)[8:], tmid_ref[...].astype(F32), tbelow_ref[...].astype(F32)[:8]], axis=0)
+    rims = rims_ref[...].astype(F32)
+    first = shard_ref[0] % NC == 0
+    above = jnp.where(first, m1[EXT + 8 :], rims[8:])
+    below = jnp.where(first, rims[:8], m3[EXT : EXT + 8])
+    goal = jnp.concatenate([above, tmid_ref[...].astype(F32), below], axis=0)
     goal = to_blocks(goal)
     slope = STEEP * (level - goal) * level * (1.0 - level)
     row_block = lax.broadcasted_iota(jnp.int32, (M, 128), 0) // COLB
@@ -148,30 +156,27 @@
     grad_ref[TR:] = jnp.concatenate([digits, jnp.zeros((16, TC - 128), F32)], axis=1).astype(BF)
 
 
-def image(level, shard, weights, parts, tabove, tmid, tbelow, info, table):
+def image(level, shard, weights, parts, rims, tmid, info, table):
     vm = pl.BlockSpec(memory_space=pltpu.VMEM)
     sm = pl.BlockSpec(memory_space=pltpu.SMEM)
     return pl.pallas_call(
         image_kernel,
         out_shape=(jax.ShapeDtypeStruct((TR, TC), BF), jax.ShapeDtypeStruct((TR + 16, TC), BF)),
-        in_specs=[sm] * 3 + [vm] * 9,
+        in_specs=[sm] * 3 + [vm] * 8,
         out_specs=(vm, vm),
         scratch_shapes=[pltpu.VMEM((M, K), BF), pltpu.VMEM((KERN, M, 256), F32), pltpu.VMEM((M, 2 * KERN * 128), BF)],
         compiler_params=pltpu.CompilerParams(vmem_limit_bytes=28 * 1024 * 1024),
         cost_estimate=pl.CostEstimate(flops=5_000_000_000, bytes_accessed=8_000_000, transcendentals=65536),
         name="image",
-    )(level, shard, weights, *parts, tabove, tmid, tbelow, info, table)
-
-
-NX, NC, NY, NZ = 4, 2, 4, 8
+    )(level, shard, weights, *parts, rims, tmid, info, table)
+
+
 WIDE = TC + 128
-LEAD = 16
-EXT = TR + 2 * LEAD
 INFO = 128
 PLACE_GRANT = 56
 
 
-def place_kernel(shard_ref, ids_hbm, rows_hbm, cols_hbm, masters_hbm, mine_ref, theirs_ref, info_ref, scalars, panels, canvas, sem, info_sem):
+def place_kernel(shard_ref, ids_hbm, rows_hbm, cols_hbm, masters_hbm, target_ref, mine_ref, theirs_ref, info_ref, scalars, panels, canvas, sem, info_sem):
     shard = shard_ref[0]
     loads = [pltpu.make_async_copy(ref.at[shard], scalars.at[j], info_sem.at[j]) for j, ref in enumerate((ids_hbm, rows_hbm, cols_hbm))]
     for cp in loads:
@@ -212,18 +217,20 @@
     for d in range(NX):
         x = (shard // NC + d) % NX
         mine_ref[d] = canvas[pl.ds(pl.multiple_of((x * NC + core) * TR, 8), EXT), :TC]
-        theirs_ref[d] = canvas[pl.ds(pl.multiple_of((x * NC + 1 - core) * TR, 8), EXT), :TC].astype(BF)
-
-
-def place(shard, ids, rows, cols, masters):
+        theirs_ref[EXT * d : EXT * d + EXT] = canvas[pl.ds(pl.multiple_of((x * NC + 1 - core) * TR, 8), EXT), :TC].astype(BF)
+    goal = target_ref[...].astype(F32)
+    theirs_ref[EXT * NX :] = jnp.concatenate([goal[:8], goal[TR - 8 :]], axis=0).astype(BF)
+
+
+def place(shard, ids, rows, cols, masters, target):
     vm = pl.BlockSpec(memory_space=pltpu.VMEM)
     sm = pl.BlockSpec(memory_space=pltpu.SMEM)
     hbm = pl.BlockSpec(memory_space=pltpu.HBM)
     bands = (NX, EXT, TC)
     return pl.pallas_call(
         place_kernel,
-        out_shape=(jax.ShapeDtypeStruct(bands, F32), jax.ShapeDtypeStruct(bands, BF), jax.ShapeDtypeStruct((1, INFO), jnp.int32)),
-        in_specs=[sm] + [hbm] * 4,
+        out_shape=(jax.ShapeDtypeStruct(bands, F32), jax.ShapeDtypeStruct((NX * EXT + 16, TC), BF), jax.ShapeDtypeStruct((1, INFO), jnp.int32)),
+        in_specs=[sm] + [hbm] * 4 + [vm],
         out_specs=(vm, vm, sm),
         scratch_shapes=[
             pltpu.SMEM((3, 1, INST_DEV), jnp.int32),
@@ -235,7 +242,7 @@
         compiler_params=pltpu.CompilerParams(vmem_limit_bytes=PLACE_GRANT * 1024 * 1024),
         cost_estimate=pl.CostEstimate(flops=1_000_000, bytes_accessed=12_000_000, transcendentals=0),
         name="place",
-    )(shard, ids, rows, cols, masters)
+    )(shard, ids, rows, cols, masters, target)
 
 
 def cut_kernel(shard_ref, region_ref, g0, g1, g2, g3, own_ref, up_ref, down_ref, far_ref, *rest):
@@ -351,13 +358,6 @@
     return lax.ppermute(v, axis, [(i, (i + by) % n) for i in range(n)])
 
 
-def halo(v, axis, width):
-    n = lax.axis_size(axis)
-    above = lax.ppermute(v[-width:], axis, [(i, i + 1) for i in range(n - 1)])
-    below = lax.ppermute(v[:width], axis, [(i + 1, i) for i in range(n - 1)])
-    return above, below
-
-
 def sum_along_z(slots):
     own, one, two, three, low, five, six, seven, high = slots
     three, five = shift(three, "z", 1), shift(five, "z", -1)
@@ -394,14 +394,16 @@
 def body(masters, inst_master, inst_row, inst_col, def_index, def_weights, kernels, target):
     shard = lax.axis_index(("x", "core")).reshape(1)
     region = lax.axis_index(("z", "y")).reshape(1)
-    mine, theirs, info = place(shard, inst_master, inst_row, inst_col, masters)
+    tmid = target[0]
+    mine, theirs, info = place(shard, inst_master, inst_row, inst_col, masters, tmid)
     other = shift(theirs, "core", 1)
+    rims = other[NX * EXT :]
+    sums = [mine[d] + other[EXT * d : EXT * d + EXT].astype(F32) for d in range(NX)]
+    sends = [jnp.concatenate([sums[d].astype(BF), rims]) if d != 2 else sums[d].astype(BF) for d in range(NX)]
+    parts = [sums[0]] + [shift(sends[d], "x", d) for d in (1, 2, 3)]
     table = make_table(kernels)
-    sums = [mine[d] + other[d].astype(F32) for d in range(NX)]
-    parts = [sums[0]] + [shift(sums[d].astype(BF), "x", d) for d in (2, 1, 3)]
     tmid = target[0]
-    tabove, tbelow = halo(tmid, ("x", "core"), 16)
-    resist, grad = image(def_index, shard, def_weights, parts, tabove, tmid, tbelow, info, table)
+    resist, grad = image(def_index, shard, def_weights, parts, rims, tmid, info, table)
     grads = [grad] + [shift(grad, "y", k) for k in (1, 2, 3)]
     own = jnp.stack([g[:TR] for g in grads])
     up, down, far = [shift(own, "x", by) for by in (1, 3, 2)]

time: 154 us -> 150 us (0.974)
  starting transfers between devices: 56.9 us -> 48.9 us
  waiting for transfers between devices: 53.6 us -> 55.9 us
    ppermute x2 -> x0, starting transfers between devices: 4.32 us -> none  [the longest x1 2.23 us: halo(): below = lax.ppermute(v[:width], axis, [(i + 1, i) for i in range(n - 1)])]
    ppermute x34, starting transfers between devices: 52.6 us -> 48.9 us  [shift(): return lax.ppermute(v, axis, [(i, (i + by) % n) for i in range(n)])]
    ppermute x34, waiting for transfers between devices: 53.6 us -> 55.9 us  [shift(): return lax.ppermute(v, axis, [(i, (i + by) % n) for i in range(n)])]
  transfers between devices with their start and end apart: 36 -> 34, of which waited for: 20 -> 22; matrix products, arithmetic and copies ran while one was open for 1% -> 1% of each run, Pallas kernels for 7% -> 7%
where the time goes in v3:
time: 150 us; the launch traced here: 149 us
  waiting for transfers between devices  55.9 us (37%)
  starting transfers between devices  48.9 us (33%)
  Pallas kernels  30.7 us (20%)
  blocking collectives  9.43 us (6%)
  between operations  1.8 us (1%)
  other arithmetic  1.75 us (1%)
    ppermute x34, waiting for transfers between devices, shift(): return lax.ppermute(v, axis, [(i, (i + by) % n) for i in range(n)])  55.9 us
    ppermute x34, starting transfers between devices, shift(): return lax.ppermute(v, axis, [(i, (i + by) % n) for i in range(n)])  48.9 us
    all_gather x4, blocking collectives, body(): bands = [lax.all_gather(v, 'core') for v in (own, up, down, far)]  9.43 us
    pallas_call x1, Pallas kernels, image(): pl.pallas_call(image_kernel, out_shape=(jax.ShapeDtypeStruct((TR, TC), BF...  9.07 us
    pallas_call x6, Pallas kernels, deposit(): pl.pallas_call(functools.partial(deposit_kernel, places, n + len(old)), o...  6.84 us
    pallas_call x1, Pallas kernels, place(): pl.pallas_call(place_kernel, out_shape=(jax.ShapeDtypeStruct(bands, F32),...  5.63 us
    pallas_call x1, Pallas kernels, make_table(): pl.pallas_call(table_kernel, out_shape=jax.ShapeDtypeStruct((K, 2 * KERN...  4.74 us
    pallas_call x1, Pallas kernels, cut(): pl.pallas_call(cut_kernel, out_shape=[jax.ShapeDtypeStruct(slot, F32 if d...  4.38 us
  transfers between devices with their start and end apart: 34, of which 22 were waited for; matrix products, arithmetic and copies ran while one was open for 1% of the time, Pallas kernels for 7%

profile of v3, /device:TPU:6, one launch (start us, length us, event | category | flops | bytes accessed | tf_op | source)
XLA Modules:
  0.0 149.3 jit_solution(14167555480387451803)
XLA Ops:
  0.7 5.6 %place.1 = (f32[4,80,1024]{2,1,0:T(8,128)}, bf16[336,1024]{1,0:T(8,128)(2,1)}, s32[1,128]{1,0:T(1,128)}) custom-call(s32[1]{0:T(128)} %bitcast.1.shard_ref, s32[8,1,16]{2,1,0:T(1,128)} %ids_hbm.1, s32[8,1,16]{2,1,0:T(1,128)} %rows_hbm.1, s32[8,1,16]{2,1,0:T(1,128)} %cols_hbm.1, f32[128,128,128]{2,1,0:T(8,128)} %masters_hbm.1, bf16[48,1024]{1,0:T(8,128)(2,1)} %bitcast.37), custom_call_target="tpu_custom_call" | custom-call | flops 1000000 | bytes 12000000 | tf_op jit(solution)/shard_map/place/pallas_call | solution.py:230
  6.4 2.3 %collective-permute-done = bf16[336,1024]{1,0:T(8,128)(2,1)S(1)} collective-permute-done((bf16[336,1024]{1,0:T(8,128)(2,1)}, bf16[336,1024]{1,0:T(8,128)(2,1)S(1)}, u32[]{:S(2)}, u32[]{:S(2)}) %collective-permute-start) | collective-permute-done | bytes 688160 | tf_op jit(solution)/shard_map/ppermute | solution.py:358
  8.8 1.4 fusion
  10.3 0.9 collective-permute-start.3
  11.2 2.4 %collective-permute-start.1 = (bf16[96,1024]{1,0:T(8,128)(2,1)S(1)}, bf16[96,1024]{1,0:T(8,128)(2,1)S(1)}, u32[]{:S(2)}, u32[]{:S(2)}) collective-permute-start(bf16[96,1024]{1,0:T(8,128)(2,1)S(1)} %get-tuple-element.63), channel_id=1, source_target_pairs={{0,64},{64,128},{128,192},{192,0},{1,65},{65,129},{129,193},{193,1... | collective-permute-start | bytes 589832 | tf_op jit(solution)/shard_map/ppermute | solution.py:358
  13.6 0.4 collective-permute-start.2
  15.3 0.2 reshape.42.v_ref
  15.5 4.7 %taps_table.1.w_ref = bf16[768,3072]{1,0:T(8,128)(2,1)S(1)} custom-call(f32[24,1,512]{2,1,0:T(1,128)S(1)} %reshape.42.v_ref), custom_call_target="tpu_custom_call" | custom-call | flops 20000000 | bytes 10000000 | tf_op jit(solution)/shard_map/taps_table/pallas_call | solution.py:91
  20.2 2.2 %collective-permute-done.2.m2_ref = bf16[80,1024]{1,0:T(8,128)(2,1)S(1)} collective-permute-done((bf16[80,1024]{1,0:T(8,128)(2,1)S(1)}, bf16[80,1024]{1,0:T(8,128)(2,1)S(1)}, u32[]{:S(2)}, u32[]{:S(2)}) %collective-permute-start.2) | collective-permute-done | bytes 163872 | tf_op jit(solution)/shard_map/ppermute | solution.py:358
  22.5 9.1 %image.1 = (bf16[48,1024]{1,0:T(8,128)(2,1)}, bf16[64,1024]{1,0:T(8,128)(2,1)S(1)}) custom-call(s32[1]{0:T(128)S(6)} %copy.29.level_ref, s32[1]{0:T(128)} %bitcast.1.shard_ref, f32[8,12]{1,0:T(8,128)S(1)} %copy-done.1, f32[80,1024]{1,0:T(8,128)S(1)} %get-tuple-element.61.m0_ref, bf16[96,1024]{1,0:T(8,128)(2,1)S(1)} %collective-permute-done.1.m1_ref, ...), custom_call_target="tpu_custom_call" | custom-call | flops 5000000000 | bytes 8000000 | tf_op jit(solution)/shard_map/image/pallas_call | solution.py:162
  31.5 2.6 %collective-permute-start.6 = (bf16[64,1024]{1,0:T(8,128)(2,1)S(1)}, bf16[64,1024]{1,0:T(8,128)(2,1)S(1)}, u32[]{:S(2)}, u32[]{:S(2)}) collective-permute-start(bf16[64,1024]{1,0:T(8,128)(2,1)S(1)} %get-tuple-element.33.g0), channel_id=1, source_target_pairs={{0,3},{1,0},{2,1},{3,2},{4,7},{5,4},{6,5},{7,6},{8,11},{9,8},{10,9... | collective-permute-start | bytes 393224 | tf_op jit(solution)/shard_map/ppermute | solution.py:358
  34.1 0.6 collective-permute-start.5
  34.7 1.0 collective-permute-start.4
  35.7 3.5 %collective-permute-done.6.g3 = bf16[64,1024]{1,0:T(8,128)(2,1)S(1)} collective-permute-done((bf16[64,1024]{1,0:T(8,128)(2,1)S(1)}, bf16[64,1024]{1,0:T(8,128)(2,1)S(1)}, u32[]{:S(2)}, u32[]{:S(2)}) %collective-permute-start.6) | collective-permute-done | bytes 131104 | tf_op jit(solution)/shard_map/ppermute | solution.py:358
  39.2 2.3 %collective-permute-done.5.g2 = bf16[64,1024]{1,0:T(8,128)(2,1)S(1)} collective-permute-done((bf16[64,1024]{1,0:T(8,128)(2,1)S(1)}, bf16[64,1024]{1,0:T(8,128)(2,1)S(1)}, u32[]{:S(2)}, u32[]{:S(2)}) %collective-permute-start.5) | collective-permute-done | bytes 131104 | tf_op jit(solution)/shard_map/ppermute | solution.py:358
  41.5 1.3 collective-permute-done.4.g1
  42.9 1.4 collective-permute-start.9
  44.3 1.6 %collective-permute-start.8 = (bf16[4,48,1024]{2,1,0:T(8,128)(2,1)S(1)}, bf16[4,48,1024]{2,1,0:T(8,128)(2,1)S(1)}, u32[]{:S(2)}, u32[]{:S(2)}) collective-permute-start(bf16[4,48,1024]{2,1,0:T(8,128)(2,1)S(1)} %pad_maximum_fusion), channel_id=1, source_target_pairs={{0,192},{64,0},{128,64},{192,128},{1,193},{65,1},{129,65},{193,129... | collective-permute-start | bytes 1179656 | tf_op jit(solution)/shard_map/ppermute | solution.py:358
  45.9 1.6 %collective-permute-start.7 = (bf16[4,48,1024]{2,1,0:T(8,128)(2,1)S(1)}, bf16[4,48,1024]{2,1,0:T(8,128)(2,1)S(1)}, u32[]{:S(2)}, u32[]{:S(2)}) collective-permute-start(bf16[4,48,1024]{2,1,0:T(8,128)(2,1)S(1)} %pad_maximum_fusion), channel_id=1, source_target_pairs={{0,64},{64,128},{128,192},{192,0},{1,65},{65,129},{129,193},{193,1... | collective-permute-start | bytes 1179656 | tf_op jit(solution)/shard_map/ppermute | solution.py:358
  47.6 2.4 %all-gather = bf16[8,48,1024]{2,1,0:T(8,128)(2,1)S(1)} all-gather(bf16[4,48,1024]{2,1,0:T(8,128)(2,1)S(1)} %pad_maximum_fusion), channel_id=2, replica_groups=mesh['x'=4,'core'=2,'z'=8,'y'=4] {'core'}, dimensions={0}, use_global_device_ids=true | all-gather | bytes 1179648 | tf_op jit(solution)/shard_map/all_gather | solution.py:410
  49.9 6.7 %collective-permute-done.9 = bf16[4,48,1024]{2,1,0:T(8,128)(2,1)S(1)} collective-permute-done((bf16[4,48,1024]{2,1,0:T(8,128)(2,1)S(1)}, bf16[4,48,1024]{2,1,0:T(8,128)(2,1)S(1)}, u32[]{:S(2)}, u32[]{:S(2)}) %collective-permute-start.9) | collective-permute-done | bytes 393248 | tf_op jit(solution)/shard_map/ppermute | solution.py:358
  56.6 2.4 %all-gather.3 = bf16[8,48,1024]{2,1,0:T(8,128)(2,1)S(1)} all-gather(bf16[4,48,1024]{2,1,0:T(8,128)(2,1)S(1)} %collective-permute-done.9), channel_id=5, replica_groups=mesh['x'=4,'core'=2,'z'=8,'y'=4] {'core'}, dimensions={0}, use_global_device_ids=true | all-gather | bytes 1179648 | tf_op jit(solution)/shard_map/all_gather | solution.py:410
  59.0 4.3 %collective-permute-done.8 = bf16[4,48,1024]{2,1,0:T(8,128)(2,1)S(1)} collective-permute-done((bf16[4,48,1024]{2,1,0:T(8,128)(2,1)S(1)}, bf16[4,48,1024]{2,1,0:T(8,128)(2,1)S(1)}, u32[]{:S(2)}, u32[]{:S(2)}) %collective-permute-start.8) | collective-permute-done | bytes 393248 | tf_op jit(solution)/shard_map/ppermute | solution.py:358
  63.3 2.4 %all-gather.2 = bf16[8,48,1024]{2,1,0:T(8,128)(2,1)S(1)} all-gather(bf16[4,48,1024]{2,1,0:T(8,128)(2,1)S(1)} %collective-permute-done.8), channel_id=4, replica_groups=mesh['x'=4,'core'=2,'z'=8,'y'=4] {'core'}, dimensions={0}, use_global_device_ids=true | all-gather | bytes 1179648 | tf_op jit(solution)/shard_map/all_gather | solution.py:410
  65.6 2.4 %all-gather.1 = bf16[8,48,1024]{2,1,0:T(8,128)(2,1)S(1)} all-gather(bf16[4,48,1024]{2,1,0:T(8,128)(2,1)S(1)} %collective-permute-done.7), channel_id=3, replica_groups=mesh['x'=4,'core'=2,'z'=8,'y'=4] {'core'}, dimensions={0}, use_global_device_ids=true | all-gather | bytes 1179648 | tf_op jit(solution)/shard_map/all_gather | solution.py:410
  68.0 4.4 %cut.1 = (f32[4,128,128]{2,1,0:T(8,128)S(1)}, bf16[4,128,128]{2,1,0:T(8,128)(2,1)S(1)}, f32[4,128,128]{2,1,0:T(8,128)S(1)}, bf16[4,128,128]{2,1,0:T(8,128)(2,1)S...) custom-call(s32[1]{0:T(128)} %bitcast.1.shard_ref, ...), custom_call_target="tpu_custom_call" | custom-call | flops 1000000 | bytes 12000000 | tf_op jit(solution)/shard_map/cut/pallas_call | solution.py:304
  72.4 2.5 %collective-permute-start.10 = (bf16[4,128,128]{2,1,0:T(8,128)(2,1)S(1)}, bf16[4,128,128]{2,1,0:T(8,128)(2,1)S(1)}, u32[]{:S(2)}, u32[]{:S(2)}) collective-permute-start(bf16[4,128,128]{2,1,0:T(8,128)(2,1)S(1)} %get-tuple-element.35), channel_id=1, source_target_pairs={{0,4},{4,8},{8,12},{12,16},{16,20},{20,24},{24,28},{28,0},{1,5},{5... | collective-permute-start | bytes 393224 | tf_op jit(solution)/shard_map/ppermute | solution.py:358
  74.8 2.8 %collective-permute-start.13 = (bf16[2,128,128]{2,1,0:T(8,128)(2,1)S(1)}, bf16[2,128,128]{2,1,0:T(8,128)(2,1)S(1)}, u32[]{:S(2)}, u32[]{:S(2)}) collective-permute-start(bf16[2,128,128]{2,1,0:T(8,128)(2,1)S(1)} %get-tuple-element.42), channel_id=1, source_target_pairs={{0,8},{4,12},{8,16},{12,20},{16,24},{20,28},{24,0},{28,4},{1,9},{5... | collective-permute-start | bytes 196616 | tf_op jit(solution)/shard_map/ppermute | solution.py:358
  77.6 2.8 %collective-permute-start.16 = (bf16[2,128,128]{2,1,0:T(8,128)(2,1)S(1)}, bf16[2,128,128]{2,1,0:T(8,128)(2,1)S(1)}, u32[]{:S(2)}, u32[]{:S(2)}) collective-permute-start(bf16[2,128,128]{2,1,0:T(8,128)(2,1)S(1)} %get-tuple-element.45), channel_id=1, source_target_pairs={{0,24},{4,28},{8,0},{12,4},{16,8},{20,12},{24,16},{28,20},{1,25},{... | collective-permute-start | bytes 196616 | tf_op jit(solution)/shard_map/ppermute | solution.py:358
  80.4 1.8 %collective-permute-start.15 = (bf16[4,128,128]{2,1,0:T(8,128)(2,1)S(1)}, bf16[4,128,128]{2,1,0:T(8,128)(2,1)S(1)}, u32[]{:S(2)}, u32[]{:S(2)}) collective-permute-start(bf16[4,128,128]{2,1,0:T(8,128)(2,1)S(1)} %get-tuple-element.44), channel_id=1, source_target_pairs={{0,28},{4,0},{8,4},{12,8},{16,12},{20,16},{24,20},{28,24},{1,29},{... | collective-permute-start | bytes 393224 | tf_op jit(solution)/shard_map/ppermute | solution.py:358
  82.3 0.7 collective-permute-done.10
  83.0 3.2 %collective-permute-start.12 = (bf16[4,128,128]{2,1,0:T(8,128)(2,1)S(1)}, bf16[4,128,128]{2,1,0:T(8,128)(2,1)S(1)}, u32[]{:S(2)}, u32[]{:S(2)}) collective-permute-start(bf16[4,128,128]{2,1,0:T(8,128)(2,1)S(1)} %get-tuple-element.39), channel_id=1, source_target_pairs={{0,28},{4,0},{8,4},{12,8},{16,12},{20,16},{24,20},{28,24},{1,29},{... | collective-permute-start | bytes 393224 | tf_op jit(solution)/shard_map/ppermute | solution.py:358
  86.3 0.3 collective-permute-start.14
  86.6 1.2 collective-permute-done.15
  88.0 2.8 %collective-permute-start.17 = (bf16[4,128,128]{2,1,0:T(8,128)(2,1)S(1)}, bf16[4,128,128]{2,1,0:T(8,128)(2,1)S(1)}, u32[]{:S(2)}, u32[]{:S(2)}) collective-permute-start(bf16[4,128,128]{2,1,0:T(8,128)(2,1)S(1)} %pad_maximum_fusion.5), channel_id=1, source_target_pairs={{0,24},{4,28},{8,0},{12,4},{16,8},{20,12},{24,16},{28,20},{1,25},{... | collective-permute-start | bytes 393224 | tf_op jit(solution)/shard_map/ppermute | solution.py:358
  90.7 0.3 collective-permute-done.11
  91.0 3.4 %collective-permute-done.14 = bf16[4,128,128]{2,1,0:T(8,128)(2,1)S(1)} collective-permute-done((bf16[4,128,128]{2,1,0:T(8,128)(2,1)S(1)}, bf16[4,128,128]{2,1,0:T(8,128)(2,1)S(1)}, u32[]{:S(2)}, u32[]{:S(2)}) %collective-permute-start.14) | collective-permute-done | bytes 131104 | tf_op jit(solution)/shard_map/ppermute | solution.py:358
  94.4 3.0 %collective-permute-done.17 = bf16[4,128,128]{2,1,0:T(8,128)(2,1)S(1)} collective-permute-done((bf16[4,128,128]{2,1,0:T(8,128)(2,1)S(1)}, bf16[4,128,128]{2,1,0:T(8,128)(2,1)S(1)}, u32[]{:S(2)}, u32[]{:S(2)}) %collective-permute-start.17) | collective-permute-done | bytes 131104 | tf_op jit(solution)/shard_map/ppermute | solution.py:358
  97.5 6.5 %collective-permute-done.18 = bf16[4,128,128]{2,1,0:T(8,128)(2,1)S(1)} collective-permute-done((bf16[4,128,128]{2,1,0:T(8,128)(2,1)S(1)}, bf16[4,128,128]{2,1,0:T(8,128)(2,1)S(1)}, u32[]{:S(2)}, u32[]{:S(2)}) %collective-permute-start.18) | collective-permute-done | bytes 131104 | tf_op jit(solution)/shard_map/ppermute | solution.py:358
  104.0 0.8 collective-permute-start.20
  104.8 1.3 collective-permute-start.19
  106.1 0.8 deposit.6.refs_3_
  107.0 3.5 %collective-permute-done.20.refs_1_ = bf16[8,128,128]{2,1,0:T(8,128)(2,1)S(1)} collective-permute-done((bf16[8,128,128]{2,1,0:T(8,128)(2,1)S(1)}, bf16[8,128,128]{2,1,0:T(8,128)(2,1)S(1)}, u32[]{:S(2)}, u32[]{:S(2)}) %collective-permute-start.20) | collective-permute-done | bytes 262176 | tf_op jit(solution)/shard_map/ppermute | solution.py:358
  110.5 2.4 %collective-permute-done.19.refs_0_ = bf16[8,128,128]{2,1,0:T(8,128)(2,1)S(1)} collective-permute-done((bf16[8,128,128]{2,1,0:T(8,128)(2,1)S(1)}, bf16[8,128,128]{2,1,0:T(8,128)(2,1)S(1)}, u32[]{:S(2)}, u32[]{:S(2)}) %collective-permute-start.19) | collective-permute-done | bytes 262176 | tf_op jit(solution)/shard_map/ppermute | solution.py:358
  112.9 1.1 collective-permute-start.21
  114.1 2.2 %collective-permute-start.22 = (bf16[8,128,128]{2,1,0:T(8,128)(2,1)S(1)}, bf16[8,128,128]{2,1,0:T(8,128)(2,1)S(1)}, u32[]{:S(2)}, u32[]{:S(2)}) collective-permute-start(bf16[8,128,128]{2,1,0:T(8,128)(2,1)S(1)} %collective-permute-done.20.refs_1_), channel_id=1, source_target_pairs={{0,28},{4,0},{8,4},{12,8},{16,12},{20,16},{24,20},{28,24},{1,29},{... | collective-permute-start | bytes 786440 | tf_op jit(solution)/shard_map/ppermute | solution.py:358
  116.2 3.2 %collective-permute-start.27 = (bf16[8,128,128]{2,1,0:T(8,128)(2,1)S(1)}, bf16[8,128,128]{2,1,0:T(8,128)(2,1)S(1)}, u32[]{:S(2)}, u32[]{:S(2)}) collective-permute-start(bf16[8,128,128]{2,1,0:T(8,128)(2,1)S(1)} %collective-permute-done.20.refs_1_), channel_id=1, source_target_pairs={{0,3},{1,0},{2,1},{3,2},{4,7},{5,4},{6,5},{7,6},{8,11},{9,8},{10,9... | collective-permute-start | bytes 786440 | tf_op jit(solution)/shard_map/ppermute | solution.py:358
  119.5 1.2 deposit.7.refs_4_
  120.7 0.6 collective-permute-done.21.refs_0_
  121.3 1.5 collective-permute-done.22.refs_1_
  122.8 1.8 %collective-permute-start.24 = (bf16[8,128,128]{2,1,0:T(8,128)(2,1)S(1)}, bf16[8,128,128]{2,1,0:T(8,128)(2,1)S(1)}, u32[]{:S(2)}, u32[]{:S(2)}) collective-permute-start(bf16[8,128,128]{2,1,0:T(8,128)(2,1)S(1)} %collective-permute-done.21.refs_0_), channel_id=1, source_target_pairs={{0,4},{4,8},{8,12},{12,16},{16,20},{20,24},{24,28},{28,0},{1,5},{5... | collective-permute-start | bytes 786440 | tf_op jit(solution)/shard_map/ppermute | solution.py:358
  124.6 1.4 collective-permute-start.25
  126.0 3.2 %collective-permute-start.30 = (bf16[8,128,128]{2,1,0:T(8,128)(2,1)S(1)}, bf16[8,128,128]{2,1,0:T(8,128)(2,1)S(1)}, u32[]{:S(2)}, u32[]{:S(2)}) collective-permute-start(bf16[8,128,128]{2,1,0:T(8,128)(2,1)S(1)} %collective-permute-done.22.refs_1_), channel_id=1, source_target_pairs={{0,3},{1,0},{2,1},{3,2},{4,7},{5,4},{6,5},{7,6},{8,11},{9,8},{10,9... | collective-permute-start | bytes 786440 | tf_op jit(solution)/shard_map/ppermute | solution.py:358
  129.3 1.4 deposit.8.refs_4_
  130.7 2.4 %collective-permute-done.24.refs_0_ = bf16[8,128,128]{2,1,0:T(8,128)(2,1)S(1)} collective-permute-done((bf16[8,128,128]{2,1,0:T(8,128)(2,1)S(1)}, bf16[8,128,128]{2,1,0:T(8,128)(2,1)S(1)}, u32[]{:S(2)}, u32[]{:S(2)}) %collective-permute-start.24) | collective-permute-done | bytes 262176 | tf_op jit(solution)/shard_map/ppermute | solution.py:358
  133.1 1.6 %collective-permute-start.28 = (bf16[8,128,128]{2,1,0:T(8,128)(2,1)S(1)}, bf16[8,128,128]{2,1,0:T(8,128)(2,1)S(1)}, u32[]{:S(2)}, u32[]{:S(2)}) collective-permute-start(bf16[8,128,128]{2,1,0:T(8,128)(2,1)S(1)} %collective-permute-done.24.refs_0_), channel_id=1, source_target_pairs={{0,4},{4,8},{8,12},{12,16},{16,20},{20,24},{24,28},{28,0},{1,5},{5... | collective-permute-start | bytes 786440 | tf_op jit(solution)/shard_map/ppermute | solution.py:358
  134.7 3.2 %collective-permute-start.33 = (bf16[8,128,128]{2,1,0:T(8,128)(2,1)S(1)}, bf16[8,128,128]{2,1,0:T(8,128)(2,1)S(1)}, u32[]{:S(2)}, u32[]{:S(2)}) collective-permute-start(bf16[8,128,128]{2,1,0:T(8,128)(2,1)S(1)} %collective-permute-done.25.refs_1_), channel_id=1, source_target_pairs={{0,3},{1,0},{2,1},{3,2},{4,7},{5,4},{6,5},{7,6},{8,11},{9,8},{10,9... | collective-permute-start | bytes 786440 | tf_op jit(solution)/shard_map/ppermute | solution.py:358
  137.9 1.4 deposit.9.refs_3_
  139.3 1.4 collective-permute-done.28.refs_0_
  140.7 1.1 collective-permute-done.33.refs_2_
  141.8 0.9 collective-permute-done.32.refs_1_
  142.7 1.2 deposit.10.refs_1_
  143.9 4.4 %collective-permute-done.31.refs_0_ = bf16[8,128,128]{2,1,0:T(8,128)(2,1)S(1)} collective-permute-done((bf16[8,128,128]{2,1,0:T(8,128)(2,1)S(1)}, bf16[8,128,128]{2,1,0:T(8,128)(2,1)S(1)}, u32[]{:S(2)}, u32[]{:S(2)}) %collective-permute-start.31) | collective-permute-done | bytes 262176 | tf_op jit(solution)/shard_map/ppermute | solution.py:358
  148.3 0.8 deposit.11
  (50 shorter events, 1.2 us)
Async XLA Ops:
  0.6 14.0 %copy-start.3 = (bf16[24,225]{1,0:T(8,128)(2,1)S(1)}, bf16[24,225]{1,0:T(8,128)(2,1)}, u32[]{:S(2)}) copy-start(bf16[24,225]{1,0:T(8,128)(2,1)} %param.14) | copy-start | bytes 32404
  0.6 21.8 %copy-start = (bf16[1,48,1024]{2,1,0:T(8,128)(2,1)S(1)}, bf16[1,48,1024]{2,1,0:T(8,128)(2,1)}, u32[]{:S(2)}) copy-start(bf16[1,48,1024]{2,1,0:T(8,128)(2,1)} %param.15) | copy-start | bytes 294916
  0.7 21.8 %copy-start.1 = (f32[8,12]{1,0:T(8,128)S(1)}, f32[8,12]{1,0:T(8,128)}, u32[]{:S(2)}) copy-start(f32[8,12]{1,0:T(8,128)} %wgt_ref.1) | copy-start | bytes 1156
  6.3 16.2 %copy-start.2 = (s32[1,128]{1,0:T(1,128)S(1)}, s32[1,128]{1,0:T(1,128)}, u32[]{:S(2)}) copy-start(s32[1,128]{1,0:T(1,128)} %get-tuple-element.32.info_ref) | copy-start | bytes 1540
  6.3 2.4 %collective-permute-start = (bf16[336,1024]{1,0:T(8,128)(2,1)}, bf16[336,1024]{1,0:T(8,128)(2,1)S(1)}, u32[]{:S(2)}, u32[]{:S(2)}) collective-permute-start(bf16[336,1024]{1,0:T(8,128)(2,1)} %get-tuple-element.31), channel_id=1, source_target_pairs={{0,32},{32,0},{1,33},{33,1},{2,34},{34,2},{3,35},{35,3},{4,36},{36... | collective-permute-start | bytes 2064392 | tf_op jit(solution)/shard_map/ppermute | solution.py:358
  10.3 12.2 %collective-permute-start.3 = (bf16[96,1024]{1,0:T(8,128)(2,1)S(1)}, bf16[96,1024]{1,0:T(8,128)(2,1)S(1)}, u32[]{:S(2)}, u32[]{:S(2)}) collective-permute-start(bf16[96,1024]{1,0:T(8,128)(2,1)S(1)} %get-tuple-element.62), channel_id=1, source_target_pairs={{0,192},{64,0},{128,64},{192,128},{1,193},{65,1},{129,65},{193,129... | collective-permute-start | bytes 589832 | tf_op jit(solution)/shard_map/ppermute | solution.py:358
  11.2 11.3 %collective-permute-start.1 = (bf16[96,1024]{1,0:T(8,128)(2,1)S(1)}, bf16[96,1024]{1,0:T(8,128)(2,1)S(1)}, u32[]{:S(2)}, u32[]{:S(2)}) collective-permute-start(bf16[96,1024]{1,0:T(8,128)(2,1)S(1)} %get-tuple-element.63), channel_id=1, source_target_pairs={{0,64},{64,128},{128,192},{192,0},{1,65},{65,129},{129,193},{193,1... | collective-permute-start | bytes 589832 | tf_op jit(solution)/shard_map/ppermute | solution.py:358
  13.6 8.9 %collective-permute-start.2 = (bf16[80,1024]{1,0:T(8,128)(2,1)S(1)}, bf16[80,1024]{1,0:T(8,128)(2,1)S(1)}, u32[]{:S(2)}, u32[]{:S(2)}) collective-permute-start(bf16[80,1024]{1,0:T(8,128)(2,1)S(1)} %get-tuple-element.59), channel_id=1, source_target_pairs={{0,128},{64,192},{128,0},{192,64},{1,129},{65,193},{129,1},{193,65... | collective-permute-start | bytes 491528 | tf_op jit(solution)/shard_map/ppermute | solution.py:358
  31.5 7.6 %collective-permute-start.6 = (bf16[64,1024]{1,0:T(8,128)(2,1)S(1)}, bf16[64,1024]{1,0:T(8,128)(2,1)S(1)}, u32[]{:S(2)}, u32[]{:S(2)}) collective-permute-start(bf16[64,1024]{1,0:T(8,128)(2,1)S(1)} %get-tuple-element.33.g0), channel_id=1, source_target_pairs={{0,3},{1,0},{2,1},{3,2},{4,7},{5,4},{6,5},{7,6},{8,11},{9,8},{10,9... | collective-permute-start | bytes 393224 | tf_op jit(solution)/shard_map/ppermute | solution.py:358
  34.1 7.4 %collective-permute-start.5 = (bf16[64,1024]{1,0:T(8,128)(2,1)S(1)}, bf16[64,1024]{1,0:T(8,128)(2,1)S(1)}, u32[]{:S(2)}, u32[]{:S(2)}) collective-permute-start(bf16[64,1024]{1,0:T(8,128)(2,1)S(1)} %get-tuple-element.33.g0), channel_id=1, source_target_pairs={{0,2},{1,3},{2,0},{3,1},{4,6},{5,7},{6,4},{7,5},{8,10},{9,11},{10,... | collective-permute-start | bytes 393224 | tf_op jit(solution)/shard_map/ppermute | solution.py:358
  34.7 8.1 %collective-permute-start.4 = (bf16[64,1024]{1,0:T(8,128)(2,1)S(1)}, bf16[64,1024]{1,0:T(8,128)(2,1)S(1)}, u32[]{:S(2)}, u32[]{:S(2)}) collective-permute-start(bf16[64,1024]{1,0:T(8,128)(2,1)S(1)} %get-tuple-element.33.g0), channel_id=1, source_target_pairs={{0,1},{1,2},{2,3},{3,0},{4,5},{5,6},{6,7},{7,4},{8,9},{9,10},{10,1... | collective-permute-start | bytes 393224 | tf_op jit(solution)/shard_map/ppermute | solution.py:358
  42.9 13.7 %collective-permute-start.9 = (bf16[4,48,1024]{2,1,0:T(8,128)(2,1)S(1)}, bf16[4,48,1024]{2,1,0:T(8,128)(2,1)S(1)}, u32[]{:S(2)}, u32[]{:S(2)}) collective-permute-start(bf16[4,48,1024]{2,1,0:T(8,128)(2,1)S(1)} %pad_maximum_fusion), channel_id=1, source_target_pairs={{0,128},{64,192},{128,0},{192,64},{1,129},{65,193},{129,1},{193,65... | collective-permute-start | bytes 1179656 | tf_op jit(solution)/shard_map/ppermute | solution.py:358
  44.3 18.9 %collective-permute-start.8 = (bf16[4,48,1024]{2,1,0:T(8,128)(2,1)S(1)}, bf16[4,48,1024]{2,1,0:T(8,128)(2,1)S(1)}, u32[]{:S(2)}, u32[]{:S(2)}) collective-permute-start(bf16[4,48,1024]{2,1,0:T(8,128)(2,1)S(1)} %pad_maximum_fusion), channel_id=1, source_target_pairs={{0,192},{64,0},{128,64},{192,128},{1,193},{65,1},{129,65},{193,129... | collective-permute-start | bytes 1179656 | tf_op jit(solution)/shard_map/ppermute | solution.py:358
  45.9 19.7 %collective-permute-start.7 = (bf16[4,48,1024]{2,1,0:T(8,128)(2,1)S(1)}, bf16[4,48,1024]{2,1,0:T(8,128)(2,1)S(1)}, u32[]{:S(2)}, u32[]{:S(2)}) collective-permute-start(bf16[4,48,1024]{2,1,0:T(8,128)(2,1)S(1)} %pad_maximum_fusion), channel_id=1, source_target_pairs={{0,64},{64,128},{128,192},{192,0},{1,65},{65,129},{129,193},{193,1... | collective-permute-start | bytes 1179656 | tf_op jit(solution)/shard_map/ppermute | solution.py:358
  72.4 10.6 %collective-permute-start.10 = (bf16[4,128,128]{2,1,0:T(8,128)(2,1)S(1)}, bf16[4,128,128]{2,1,0:T(8,128)(2,1)S(1)}, u32[]{:S(2)}, u32[]{:S(2)}) collective-permute-start(bf16[4,128,128]{2,1,0:T(8,128)(2,1)S(1)} %get-tuple-element.35), channel_id=1, source_target_pairs={{0,4},{4,8},{8,12},{12,16},{16,20},{20,24},{24,28},{28,0},{1,5},{5... | collective-permute-start | bytes 393224 | tf_op jit(solution)/shard_map/ppermute | solution.py:358
  74.8 11.4 %collective-permute-start.13 = (bf16[2,128,128]{2,1,0:T(8,128)(2,1)S(1)}, bf16[2,128,128]{2,1,0:T(8,128)(2,1)S(1)}, u32[]{:S(2)}, u32[]{:S(2)}) collective-permute-start(bf16[2,128,128]{2,1,0:T(8,128)(2,1)S(1)} %get-tuple-element.42), channel_id=1, source_target_pairs={{0,8},{4,12},{8,16},{12,20},{16,24},{20,28},{24,0},{28,4},{1,9},{5... | collective-permute-start | bytes 196616 | tf_op jit(solution)/shard_map/ppermute | solution.py:358
  77.6 10.3 %collective-permute-start.16 = (bf16[2,128,128]{2,1,0:T(8,128)(2,1)S(1)}, bf16[2,128,128]{2,1,0:T(8,128)(2,1)S(1)}, u32[]{:S(2)}, u32[]{:S(2)}) collective-permute-start(bf16[2,128,128]{2,1,0:T(8,128)(2,1)S(1)} %get-tuple-element.45), channel_id=1, source_target_pairs={{0,24},{4,28},{8,0},{12,4},{16,8},{20,12},{24,16},{28,20},{1,25},{... | collective-permute-start | bytes 196616 | tf_op jit(solution)/shard_map/ppermute | solution.py:358
  80.4 7.4 %collective-permute-start.15 = (bf16[4,128,128]{2,1,0:T(8,128)(2,1)S(1)}, bf16[4,128,128]{2,1,0:T(8,128)(2,1)S(1)}, u32[]{:S(2)}, u32[]{:S(2)}) collective-permute-start(bf16[4,128,128]{2,1,0:T(8,128)(2,1)S(1)} %get-tuple-element.44), channel_id=1, source_target_pairs={{0,28},{4,0},{8,4},{12,8},{16,12},{20,16},{24,20},{28,24},{1,29},{... | collective-permute-start | bytes 393224 | tf_op jit(solution)/shard_map/ppermute | solution.py:358
  83.0 8.0 %collective-permute-start.11 = (bf16[4,128,128]{2,1,0:T(8,128)(2,1)S(1)}, bf16[4,128,128]{2,1,0:T(8,128)(2,1)S(1)}, u32[]{:S(2)}, u32[]{:S(2)}) collective-permute-start(bf16[4,128,128]{2,1,0:T(8,128)(2,1)S(1)} %get-tuple-element.38), channel_id=1, source_target_pairs={{0,4},{4,8},{8,12},{12,16},{16,20},{20,24},{24,28},{28,0},{1,5},{5... | collective-permute-start | bytes 393224 | tf_op jit(solution)/shard_map/ppermute | solution.py:358
  83.0 8.0 %collective-permute-start.12 = (bf16[4,128,128]{2,1,0:T(8,128)(2,1)S(1)}, bf16[4,128,128]{2,1,0:T(8,128)(2,1)S(1)}, u32[]{:S(2)}, u32[]{:S(2)}) collective-permute-start(bf16[4,128,128]{2,1,0:T(8,128)(2,1)S(1)} %get-tuple-element.39), channel_id=1, source_target_pairs={{0,28},{4,0},{8,4},{12,8},{16,12},{20,16},{24,20},{28,24},{1,29},{... | collective-permute-start | bytes 393224 | tf_op jit(solution)/shard_map/ppermute | solution.py:358
  86.3 8.1 %collective-permute-start.14 = (bf16[4,128,128]{2,1,0:T(8,128)(2,1)S(1)}, bf16[4,128,128]{2,1,0:T(8,128)(2,1)S(1)}, u32[]{:S(2)}, u32[]{:S(2)}) collective-permute-start(bf16[4,128,128]{2,1,0:T(8,128)(2,1)S(1)} %pad_maximum_fusion.4), channel_id=1, source_target_pairs={{0,8},{4,12},{8,16},{12,20},{16,24},{20,28},{24,0},{28,4},{1,9},{5... | collective-permute-start | bytes 393224 | tf_op jit(solution)/shard_map/ppermute | solution.py:358
  88.0 9.4 %collective-permute-start.17 = (bf16[4,128,128]{2,1,0:T(8,128)(2,1)S(1)}, bf16[4,128,128]{2,1,0:T(8,128)(2,1)S(1)}, u32[]{:S(2)}, u32[]{:S(2)}) collective-permute-start(bf16[4,128,128]{2,1,0:T(8,128)(2,1)S(1)} %pad_maximum_fusion.5), channel_id=1, source_target_pairs={{0,24},{4,28},{8,0},{12,4},{16,8},{20,12},{24,16},{28,20},{1,25},{... | collective-permute-start | bytes 393224 | tf_op jit(solution)/shard_map/ppermute | solution.py:358
  97.4 6.6 %collective-permute-start.18 = (bf16[4,128,128]{2,1,0:T(8,128)(2,1)S(1)}, bf16[4,128,128]{2,1,0:T(8,128)(2,1)S(1)}, u32[]{:S(2)}, u32[]{:S(2)}) collective-permute-start(bf16[4,128,128]{2,1,0:T(8,128)(2,1)S(1)} %add_convert_fusion), channel_id=1, source_target_pairs={{0,2},{1,3},{2,0},{3,1},{4,6},{5,7},{6,4},{7,5},{8,10},{9,11},{10,... | collective-permute-start | bytes 393224 | tf_op jit(solution)/shard_map/ppermute | solution.py:358
  104.0 6.5 %collective-permute-start.20 = (bf16[8,128,128]{2,1,0:T(8,128)(2,1)S(1)}, bf16[8,128,128]{2,1,0:T(8,128)(2,1)S(1)}, u32[]{:S(2)}, u32[]{:S(2)}) collective-permute-start(bf16[8,128,128]{2,1,0:T(8,128)(2,1)S(1)} %pad_maximum_fusion.1.refs_0_), channel_id=1, source_target_pairs={{0,28},{4,0},{8,4},{12,8},{16,12},{20,16},{24,20},{28,24},{1,29},{... | collective-permute-start | bytes 786440 | tf_op jit(solution)/shard_map/ppermute | solution.py:358
  104.8 8.1 %collective-permute-start.19 = (bf16[8,128,128]{2,1,0:T(8,128)(2,1)S(1)}, bf16[8,128,128]{2,1,0:T(8,128)(2,1)S(1)}, u32[]{:S(2)}, u32[]{:S(2)}) collective-permute-start(bf16[8,128,128]{2,1,0:T(8,128)(2,1)S(1)} %pad_maximum_fusion.1.refs_0_), channel_id=1, source_target_pairs={{0,4},{4,8},{8,12},{12,16},{16,20},{20,24},{24,28},{28,0},{1,5},{5... | collective-permute-start | bytes 786440 | tf_op jit(solution)/shard_map/ppermute | solution.py:358
  106.1 13.3 %collective-permute-start.23 = (bf16[8,128,128]{2,1,0:T(8,128)(2,1)S(1)}, bf16[8,128,128]{2,1,0:T(8,128)(2,1)S(1)}, u32[]{:S(2)}, u32[]{:S(2)}) collective-permute-start(bf16[8,128,128]{2,1,0:T(8,128)(2,1)S(1)} %pad_maximum_fusion.1.refs_0_), channel_id=1, source_target_pairs={{0,1},{1,2},{2,3},{3,0},{4,5},{5,6},{6,7},{7,4},{8,9},{9,10},{10,1... | collective-permute-start | bytes 786440 | tf_op jit(solution)/shard_map/ppermute | solution.py:358
  112.9 8.4 %collective-permute-start.21 = (bf16[8,128,128]{2,1,0:T(8,128)(2,1)S(1)}, bf16[8,128,128]{2,1,0:T(8,128)(2,1)S(1)}, u32[]{:S(2)}, u32[]{:S(2)}) collective-permute-start(bf16[8,128,128]{2,1,0:T(8,128)(2,1)S(1)} %collective-permute-done.19.refs_0_), channel_id=1, source_target_pairs={{0,4},{4,8},{8,12},{12,16},{16,20},{20,24},{24,28},{28,0},{1,5},{5... | collective-permute-start | bytes 786440 | tf_op jit(solution)/shard_map/ppermute | solution.py:358
  114.1 8.7 %collective-permute-start.22 = (bf16[8,128,128]{2,1,0:T(8,128)(2,1)S(1)}, bf16[8,128,128]{2,1,0:T(8,128)(2,1)S(1)}, u32[]{:S(2)}, u32[]{:S(2)}) collective-permute-start(bf16[8,128,128]{2,1,0:T(8,128)(2,1)S(1)} %collective-permute-done.20.refs_1_), channel_id=1, source_target_pairs={{0,28},{4,0},{8,4},{12,8},{16,12},{20,16},{24,20},{28,24},{1,29},{... | collective-permute-start | bytes 786440 | tf_op jit(solution)/shard_map/ppermute | solution.py:358
  116.2 9.8 %collective-permute-start.26 = (bf16[8,128,128]{2,1,0:T(8,128)(2,1)S(1)}, bf16[8,128,128]{2,1,0:T(8,128)(2,1)S(1)}, u32[]{:S(2)}, u32[]{:S(2)}) collective-permute-start(bf16[8,128,128]{2,1,0:T(8,128)(2,1)S(1)} %collective-permute-done.19.refs_0_), channel_id=1, source_target_pairs={{0,1},{1,2},{2,3},{3,0},{4,5},{5,6},{6,7},{7,4},{8,9},{9,10},{10,1... | collective-permute-start | bytes 786440 | tf_op jit(solution)/shard_map/ppermute | solution.py:358
  116.2 13.0 %collective-permute-start.27 = (bf16[8,128,128]{2,1,0:T(8,128)(2,1)S(1)}, bf16[8,128,128]{2,1,0:T(8,128)(2,1)S(1)}, u32[]{:S(2)}, u32[]{:S(2)}) collective-permute-start(bf16[8,128,128]{2,1,0:T(8,128)(2,1)S(1)} %collective-permute-done.20.refs_1_), channel_id=1, source_target_pairs={{0,3},{1,0},{2,1},{3,2},{4,7},{5,4},{6,5},{7,6},{8,11},{9,8},{10,9... | collective-permute-start | bytes 786440 | tf_op jit(solution)/shard_map/ppermute | solution.py:358
  122.8 10.3 %collective-permute-start.24 = (bf16[8,128,128]{2,1,0:T(8,128)(2,1)S(1)}, bf16[8,128,128]{2,1,0:T(8,128)(2,1)S(1)}, u32[]{:S(2)}, u32[]{:S(2)}) collective-permute-start(bf16[8,128,128]{2,1,0:T(8,128)(2,1)S(1)} %collective-permute-done.21.refs_0_), channel_id=1, source_target_pairs={{0,4},{4,8},{8,12},{12,16},{16,20},{20,24},{24,28},{28,0},{1,5},{5... | collective-permute-start | bytes 786440 | tf_op jit(solution)/shard_map/ppermute | solution.py:358
  124.6 8.5 %collective-permute-start.25 = (bf16[8,128,128]{2,1,0:T(8,128)(2,1)S(1)}, bf16[8,128,128]{2,1,0:T(8,128)(2,1)S(1)}, u32[]{:S(2)}, u32[]{:S(2)}) collective-permute-start(bf16[8,128,128]{2,1,0:T(8,128)(2,1)S(1)} %collective-permute-done.22.refs_1_), channel_id=1, source_target_pairs={{0,28},{4,0},{8,4},{12,8},{16,12},{20,16},{24,20},{28,24},{1,29},{... | collective-permute-start | bytes 786440 | tf_op jit(solution)/shard_map/ppermute | solution.py:358
  126.0 11.9 %collective-permute-start.29 = (bf16[8,128,128]{2,1,0:T(8,128)(2,1)S(1)}, bf16[8,128,128]{2,1,0:T(8,128)(2,1)S(1)}, u32[]{:S(2)}, u32[]{:S(2)}) collective-permute-start(bf16[8,128,128]{2,1,0:T(8,128)(2,1)S(1)} %collective-permute-done.21.refs_0_), channel_id=1, source_target_pairs={{0,1},{1,2},{2,3},{3,0},{4,5},{5,6},{6,7},{7,4},{8,9},{9,10},{10,1... | collective-permute-start | bytes 786440 | tf_op jit(solution)/shard_map/ppermute | solution.py:358
  126.0 11.9 %collective-permute-start.30 = (bf16[8,128,128]{2,1,0:T(8,128)(2,1)S(1)}, bf16[8,128,128]{2,1,0:T(8,128)(2,1)S(1)}, u32[]{:S(2)}, u32[]{:S(2)}) collective-permute-start(bf16[8,128,128]{2,1,0:T(8,128)(2,1)S(1)} %collective-permute-done.22.refs_1_), channel_id=1, source_target_pairs={{0,3},{1,0},{2,1},{3,2},{4,7},{5,4},{6,5},{7,6},{8,11},{9,8},{10,9... | collective-permute-start | bytes 786440 | tf_op jit(solution)/shard_map/ppermute | solution.py:358
  133.1 7.6 %collective-permute-start.28 = (bf16[8,128,128]{2,1,0:T(8,128)(2,1)S(1)}, bf16[8,128,128]{2,1,0:T(8,128)(2,1)S(1)}, u32[]{:S(2)}, u32[]{:S(2)}) collective-permute-start(bf16[8,128,128]{2,1,0:T(8,128)(2,1)S(1)} %collective-permute-done.24.refs_0_), channel_id=1, source_target_pairs={{0,4},{4,8},{8,12},{12,16},{16,20},{20,24},{24,28},{28,0},{1,5},{5... | collective-permute-start | bytes 786440 | tf_op jit(solution)/shard_map/ppermute | solution.py:358
  134.7 8.0 %collective-permute-start.32 = (bf16[8,128,128]{2,1,0:T(8,128)(2,1)S(1)}, bf16[8,128,128]{2,1,0:T(8,128)(2,1)S(1)}, u32[]{:S(2)}, u32[]{:S(2)}) collective-permute-start(bf16[8,128,128]{2,1,0:T(8,128)(2,1)S(1)} %collective-permute-done.24.refs_0_), channel_id=1, source_target_pairs={{0,1},{1,2},{2,3},{3,0},{4,5},{5,6},{6,7},{7,4},{8,9},{9,10},{10,1... | collective-permute-start | bytes 786440 | tf_op jit(solution)/shard_map/ppermute | solution.py:358
  134.7 7.1 %collective-permute-start.33 = (bf16[8,128,128]{2,1,0:T(8,128)(2,1)S(1)}, bf16[8,128,128]{2,1,0:T(8,128)(2,1)S(1)}, u32[]{:S(2)}, u32[]{:S(2)}) collective-permute-start(bf16[8,128,128]{2,1,0:T(8,128)(2,1)S(1)} %collective-permute-done.25.refs_1_), channel_id=1, source_target_pairs={{0,3},{1,0},{2,1},{3,2},{4,7},{5,4},{6,5},{7,6},{8,11},{9,8},{10,9... | collective-permute-start | bytes 786440 | tf_op jit(solution)/shard_map/ppermute | solution.py:358
  140.7 7.6 %collective-permute-start.31 = (bf16[8,128,128]{2,1,0:T(8,128)(2,1)S(1)}, bf16[8,128,128]{2,1,0:T(8,128)(2,1)S(1)}, u32[]{:S(2)}, u32[]{:S(2)}) collective-permute-start(bf16[8,128,128]{2,1,0:T(8,128)(2,1)S(1)} %collective-permute-done.28.refs_0_), channel_id=1, source_target_pairs={{0,1},{1,2},{2,3},{3,0},{4,5},{5,6},{6,7},{7,4},{8,9},{9,10},{10,1... | collective-permute-start | bytes 786440 | tf_op jit(solution)/shard_map/ppermute | solution.py:358

commit v4 on v3

--- a/solution.py
+++ b/solution.py
@@ -102,8 +102,8 @@
 def image_kernel(level_ref, shard_ref, wgt_ref, m0_ref, m1_ref, m2_ref, m3_ref, rims_ref, tmid_ref, info_ref, w_ref,
                  resist_ref, grad_ref, lhs_ref, fields_ref, cot_ref):
     level_at = level_ref[0]
-    m1, m3 = m1_ref[...].astype(F32), m3_ref[...].astype(F32)
-    x = m0_ref[...] + m1[:EXT] + m2_ref[...].astype(F32) + m3[:EXT]
+    m1 = m1_ref[...].astype(F32)
+    x = m0_ref[...] + m1[:EXT] + m2_ref[...].astype(F32) + m3_ref[...].astype(F32)
     x = x.astype(BF).astype(F32)
     x = pltpu.roll(x, 8 * MROWB - 1, 0)
     x = jnp.concatenate([x, jnp.zeros((8 * MROWB, 128), F32)], axis=1)
@@ -124,7 +124,7 @@
     rims = rims_ref[...].astype(F32)
     first = shard_ref[0] % NC == 0
     above = jnp.where(first, m1[EXT + 8 :], rims[8:])
-    below = jnp.where(first, rims[:8], m3[EXT : EXT + 8])
+    below = jnp.where(first, rims[:8], m1[EXT : EXT + 8])
     goal = jnp.concatenate([above, tmid_ref[...].astype(F32), below], axis=0)
     goal = to_blocks(goal)
     slope = STEEP * (level - goal) * level * (1.0 - level)
@@ -173,13 +173,20 @@
 
 WIDE = TC + 128
 INFO = 128
+
+
+def direction(shard):
+    return 1 - 2 * (shard % NC)
+
+
 PLACE_GRANT = 56
 
 
-def place_kernel(shard_ref, ids_hbm, rows_hbm, cols_hbm, masters_hbm, target_ref, mine_ref, theirs_ref, info_ref, scalars, panels, canvas, sem, info_sem):
+def place_kernel(shard_ref, ids_hbm, rows_hbm, cols_hbm, masters_hbm, target_hbm, mine_ref, theirs_ref, info_ref, scalars, panels, canvas, goal_buf, sem, info_sem, rim_sem):
     shard = shard_ref[0]
     loads = [pltpu.make_async_copy(ref.at[shard], scalars.at[j], info_sem.at[j]) for j, ref in enumerate((ids_hbm, rows_hbm, cols_hbm))]
-    for cp in loads:
+    rim_load = pltpu.make_async_copy(target_hbm, goal_buf, rim_sem)
+    for cp in loads + [rim_load]:
         cp.start()
     for cp in loads:
         cp.wait()
@@ -214,11 +221,14 @@
         at = (pl.ds(pl.multiple_of(r0, 8), P_SIZE + 8), pl.ds(pl.multiple_of(c0, 128), 256))
         canvas[at] = canvas[at] + full
     core = shard % NC
+    way = direction(shard)
     for d in range(NX):
-        x = (shard // NC + d) % NX
+        x = (shard // NC + way * d + NX) % NX
         mine_ref[d] = canvas[pl.ds(pl.multiple_of((x * NC + core) * TR, 8), EXT), :TC]
+        x = (shard // NC - way * d + NX) % NX
         theirs_ref[EXT * d : EXT * d + EXT] = canvas[pl.ds(pl.multiple_of((x * NC + 1 - core) * TR, 8), EXT), :TC].astype(BF)
-    goal = target_ref[...].astype(F32)
+    rim_load.wait()
+    goal = goal_buf[...].astype(F32)
     theirs_ref[EXT * NX :] = jnp.concatenate([goal[:8], goal[TR - 8 :]], axis=0).astype(BF)
 
 
@@ -230,14 +240,16 @@
     return pl.pallas_call(
         place_kernel,
         out_shape=(jax.ShapeDtypeStruct(bands, F32), jax.ShapeDtypeStruct((NX * EXT + 16, TC), BF), jax.ShapeDtypeStruct((1, INFO), jnp.int32)),
-        in_specs=[sm] + [hbm] * 4 + [vm],
+        in_specs=[sm] + [hbm] * 5,
         out_specs=(vm, vm, sm),
         scratch_shapes=[
             pltpu.SMEM((3, 1, INST_DEV), jnp.int32),
             pltpu.VMEM((INST_DEV, P_SIZE, P_SIZE), F32),
             pltpu.VMEM((LEAD + 8 * TR + LEAD, WIDE), F32),
+            pltpu.VMEM((TR, TC), BF),
             pltpu.SemaphoreType.DMA((INST_DEV,)),
             pltpu.SemaphoreType.DMA((3,)),
+            pltpu.SemaphoreType.DMA,
         ],
         compiler_params=pltpu.CompilerParams(vmem_limit_bytes=PLACE_GRANT * 1024 * 1024),
         cost_estimate=pl.CostEstimate(flops=1_000_000, bytes_accessed=12_000_000, transcendentals=0),
@@ -253,36 +265,34 @@
         digits[k : k + 1] = (tile[0:1] * 128.0 + tile[1:2]).astype(jnp.int32)
     load = pltpu.make_async_copy(digits, lists, list_sem)
     load.start()
-    x = shard_ref[0] // NC
+    x = shard_ref[0] // NC + NX
     z, y = region_ref[0] // NY, region_ref[0] % NY
     sums[...] = jnp.zeros(sums.shape, F32)
 
-    def lay(ref, n, at):
-        for core in range(NC):
-            row = ((x + n) % NX * NC + core) * TR
-            canvas[at, pl.ds(pl.multiple_of(row, 8), TR), :TC] = ref[core, at].astype(F32)
-
-    for k in range(NY):
-        lay(own_ref, 0, k)
-        lay(up_ref, 3, k)
-        lay(down_ref, 1, k)
-        lay(far_ref, 2, k)
+    for core in range(NC):
+        way = 1 - 2 * core
+        for ref, n in ((own_ref, 0), (up_ref, -way), (down_ref, way), (far_ref, 2)):
+            row = pl.multiple_of(((x + n) % NX * NC + core) * TR, 8)
+            for k in range(NY):
+                canvas[-way * k % NY, pl.ds(row, TR), :TC] = ref[core, k].astype(F32)
     load.wait()
     sub = lax.broadcasted_iota(jnp.int32, (P_SIZE // 8, 8, 128), 1)
+    way = direction(shard_ref[0])
     for k in range(NY):
-
-        def one(i, carry, k=k):
+        tile = (NY - way * k) % NY
+
+        def one(i, carry, k=k, tile=tile):
             m = lists[k, i]
 
             @pl.when((m // 4) % NY == y)
             def _():
                 r, c = lists[k, INST_DEV + i], lists[k, 2 * INST_DEV + i]
                 r0, c0 = (r // 8) * 8, (c // 128) * 128
-                full = canvas[k, pl.ds(pl.multiple_of(r0, 8), P_SIZE + 8), pl.ds(pl.multiple_of(c0, 128), 256)]
+                full = canvas[tile, pl.ds(pl.multiple_of(r0, 8), P_SIZE + 8), pl.ds(pl.multiple_of(c0, 128), 256)]
                 full = pltpu.roll(full, 256 - (c - c0), 1)[:, :128]
                 full = pltpu.roll(full.reshape(P_SIZE // 8 + 1, 8, 128), 8 - (r - r0), 1)
                 full = jnp.where(sub < 8 - (r - r0), full[:-1], full[1:]).reshape(P_SIZE, 128)
-                slot = (m // 16 - z + NZ) % NZ
+                slot = (way * (m // 16 - z) + NZ) % NZ
                 sums[slot, m % 4] = sums[slot, m % 4] + full
 
             return carry
@@ -319,7 +329,8 @@
     )(shard, region, *grads, *bands)
 
 
-def deposit_kernel(places, n_in, region_ref, *refs):
+def deposit_kernel(places, n_in, shard_ref, region_ref, *refs):
+    way = direction(shard_ref[0])
     blocks, (out_ref, wide, sem) = refs[: len(places)], refs[n_in:]
     z, y = region_ref[0] // NY, region_ref[0] % NY
     copies = []
@@ -327,14 +338,14 @@
         for j, k in enumerate(ys):
             at = len(copies)
             wide[at] = block[4 * j : 4 * j + 4].astype(F32)
-            cp = pltpu.make_async_copy(wide.at[at], out_ref.at[(z + dz + NZ) % NZ, (y - k + NY) % NY], sem.at[at])
+            cp = pltpu.make_async_copy(wide.at[at], out_ref.at[(z + way * dz + NZ) % NZ, (y - way * k + NY) % NY], sem.at[at])
             cp.start()
             copies.append(cp)
     for cp in copies:
         cp.wait()
 
 
-def deposit(region, out, items):
+def deposit(shard, region, out, items):
     places = [item[1:] for item in items]
     blocks = [item[0] for item in items]
     n, total = len(items), sum(len(item[2]) for item in items)
@@ -343,19 +354,22 @@
     return pl.pallas_call(
         functools.partial(deposit_kernel, places, n + len(old)),
         out_shape=jax.ShapeDtypeStruct((NZ, NY, 4, P_SIZE, P_SIZE), F32),
-        in_specs=[pl.BlockSpec(memory_space=pltpu.SMEM)] + [pl.BlockSpec(memory_space=pltpu.VMEM)] * n + [hbm] * len(old),
+        in_specs=[pl.BlockSpec(memory_space=pltpu.SMEM)] * 2 + [pl.BlockSpec(memory_space=pltpu.VMEM)] * n + [hbm] * len(old),
         out_specs=hbm,
-        input_output_aliases={n + 1: 0} if old else {},
+        input_output_aliases={n + 2: 0} if old else {},
         scratch_shapes=[pltpu.VMEM((total, 4, P_SIZE, P_SIZE), F32), pltpu.SemaphoreType.DMA((total,))],
         compiler_params=pltpu.CompilerParams(vmem_limit_bytes=16 * 1024 * 1024),
         cost_estimate=pl.CostEstimate(flops=200_000 * total, bytes_accessed=400_000 * total, transcendentals=0),
         name="deposit",
-    )(region, *blocks, *old)
+    )(shard, region, *blocks, *old)
 
 
 def shift(v, axis, by):
     n = lax.axis_size(axis)
-    return lax.ppermute(v, axis, [(i, (i + by) % n) for i in range(n)])
+    first = axis == "x"
+    place_of = (lambda core, i: i * NC + core) if first else (lambda core, i: core * n + i)
+    ring = [(place_of(core, i), place_of(core, (i + (by if core == 0 else -by)) % n)) for core in range(NC) for i in range(n)]
+    return lax.ppermute(v, ("x", "core") if first else ("core", axis), ring)
 
 
 def sum_along_z(slots):
@@ -370,11 +384,11 @@
     return own + near + shift(two.astype(BF), "z", 2).astype(F32) + shift(six.astype(BF), "z", -2).astype(F32)
 
 
-def spread(part, region):
+def spread(part, shard, region):
     own = jnp.concatenate([part, shift(part, "y", 2)])
     ups, downs = shift(own, "z", 1), shift(own, "z", -1)
     came = [(shift(own, "y", 1), 0, (1, 3))]
-    out = deposit(region, None, [(own, 0, (0, 2))])
+    out = deposit(shard, region, None, [(own, 0, (0, 2))])
     for d in (1, 2, 3):
         ups, downs, out = lax.optimization_barrier((ups, downs, out))
         here = [(ups, -d, (0, 2)), (downs, d, (0, 2))]
@@ -382,12 +396,12 @@
         if d < 3:
             downs = shift(downs, "z", -1)
         side = [(shift(here[0][0], "y", 1), -d, (1, 3)), (shift(here[1][0], "y", -1), d, (3, 1))]
-        out = deposit(region, out, here + came)
+        out = deposit(shard, region, out, here + came)
         came = side
     ups, out = lax.optimization_barrier((ups, out))
     side = shift(ups, "y", 1)
-    out = deposit(region, out, [(ups, -4, (0, 2))] + came)
-    out = deposit(region, out, [(side, -4, (1, 3))])
+    out = deposit(shard, region, out, [(ups, -4, (0, 2))] + came)
+    out = deposit(shard, region, out, [(side, -4, (1, 3))])
     return out.reshape(MAS_DEV, P_SIZE, P_SIZE)
 
 
@@ -396,20 +410,21 @@
     region = lax.axis_index(("z", "y")).reshape(1)
     tmid = target[0]
     mine, theirs, info = place(shard, inst_master, inst_row, inst_col, masters, tmid)
-    other = shift(theirs, "core", 1)
+    other = lax.ppermute(theirs, "core", [(0, 1), (1, 0)])
     rims = other[NX * EXT :]
     sums = [mine[d] + other[EXT * d : EXT * d + EXT].astype(F32) for d in range(NX)]
-    sends = [jnp.concatenate([sums[d].astype(BF), rims]) if d != 2 else sums[d].astype(BF) for d in range(NX)]
+    sends = [jnp.concatenate([sums[d].astype(BF), rims]) if d == 1 else sums[d].astype(BF) for d in range(NX)]
     parts = [sums[0]] + [shift(sends[d], "x", d) for d in (1, 2, 3)]
     table = make_table(kernels)
     tmid = target[0]
     resist, grad = image(def_index, shard, def_weights, parts, rims, tmid, info, table)
-    grads = [grad] + [shift(grad, "y", k) for k in (1, 2, 3)]
+    across, before, after = [shift(grad, "y", k) for k in (2, 1, 3)]
+    grads = [grad, before, across, after]
     own = jnp.stack([g[:TR] for g in grads])
     up, down, far = [shift(own, "x", by) for by in (1, 3, 2)]
     bands = [lax.all_gather(v, "core") for v in (own, up, down, far)]
     part = sum_along_z(cut(shard, region, grads, bands)).astype(BF)
-    return (spread(part, region), resist[None])
+    return (spread(part, shard, region), resist[None])
 
 
 def solution(mesh):

time: 150 us -> 148 us (0.987)
  waiting for transfers between devices: 55.9 us -> 47.4 us
  starting transfers between devices: 48.9 us -> 56 us
    ppermute x34, waiting for transfers between devices: 55.9 us -> 47.4 us  [the longest x33 45.1 us: shift(): return lax.ppermute(v, ('x', 'core') if first else ('core', axis), ring)]
    ppermute x34, starting transfers between devices: 48.9 us -> 56 us  [the longest x33 55.9 us: shift(): return lax.ppermute(v, ('x', 'core') if first else ('core', axis), ring)]
  transfers between devices with their start and end apart: 34 -> 34, of which waited for: 22 -> 19; matrix products, arithmetic and copies ran while one was open for 1% -> 1% of each run, Pallas kernels for 7% -> 7%
where the time goes in v4:
time: 148 us; the launch traced here: 147 us
  starting transfers between devices  56 us (38%)
  waiting for transfers between devices  47.4 us (32%)
  Pallas kernels  29.9 us (20%)
  blocking collectives  9.43 us (6%)
  between operations  1.79 us (1%)
  other arithmetic  1.74 us (1%)
    ppermute x33, starting transfers between devices, shift(): return lax.ppermute(v, ('x', 'core') if first else ('core', axis), ring)  55.9 us
    ppermute x33, waiting for transfers between devices, shift(): return lax.ppermute(v, ('x', 'core') if first else ('core', axis), ring)  45.1 us
    all_gather x4, blocking collectives, body(): bands = [lax.all_gather(v, 'core') for v in (own, up, down, far)]  9.43 us
    pallas_call x1, Pallas kernels, image(): pl.pallas_call(image_kernel, out_shape=(jax.ShapeDtypeStruct((TR, TC), BF...  9.09 us
    pallas_call x6, Pallas kernels, deposit(): pl.pallas_call(functools.partial(deposit_kernel, places, n + len(old)), o...  6.84 us
    pallas_call x1, Pallas kernels, place(): pl.pallas_call(place_kernel, out_shape=(jax.ShapeDtypeStruct(bands, F32),...  4.84 us
    pallas_call x1, Pallas kernels, make_table(): pl.pallas_call(table_kernel, out_shape=jax.ShapeDtypeStruct((K, 2 * KERN...  4.74 us
    pallas_call x1, Pallas kernels, cut(): pl.pallas_call(cut_kernel, out_shape=[jax.ShapeDtypeStruct(slot, F32 if d...  4.44 us
  transfers between devices with their start and end apart: 34, of which 19 were waited for; matrix products, arithmetic and copies ran while one was open for 1% of the time, Pallas kernels for 7%

profile of v4, /device:TPU:6, one launch (start us, length us, event | category | flops | bytes accessed | tf_op | source)
XLA Modules:
  0.0 147.2 jit_solution(4206040295470251990)
XLA Ops:
  0.7 4.8 %place.1 = (f32[4,80,1024]{2,1,0:T(8,128)}, bf16[336,1024]{1,0:T(8,128)(2,1)}, s32[1,128]{1,0:T(1,128)}) custom-call(s32[1]{0:T(128)} %bitcast.shard_ref, s32[8,1,16]{2,1,0:T(1,128)} %ids_hbm.1, s32[8,1,16]{2,1,0:T(1,128)} %rows_hbm.1, s32[8,1,16]{2,1,0:T(1,128)} %cols_hbm.1, f32[128,128,128]{2,1,0:T(8,128)} %masters_hbm.1, bf16[48,1024]{1,0:T(8,128)(2,1)} %bitcast.37), custom_call_target="tpu_custom_call" | custom-call | flops 1000000 | bytes 12000000 | tf_op jit(solution)/shard_map/place/pallas_call | solution.py:240
  5.6 2.3 %collective-permute-done = bf16[336,1024]{1,0:T(8,128)(2,1)S(1)} collective-permute-done((bf16[336,1024]{1,0:T(8,128)(2,1)}, bf16[336,1024]{1,0:T(8,128)(2,1)S(1)}, u32[]{:S(2)}, u32[]{:S(2)}) %collective-permute-start) | collective-permute-done | bytes 688160 | tf_op jit(solution)/shard_map/ppermute | solution.py:413
  8.0 1.4 fusion
  9.5 2.3 %collective-permute-start.1 = (bf16[96,1024]{1,0:T(8,128)(2,1)S(1)}, bf16[96,1024]{1,0:T(8,128)(2,1)S(1)}, u32[]{:S(2)}, u32[]{:S(2)}) collective-permute-start(bf16[96,1024]{1,0:T(8,128)(2,1)S(1)} %pad_maximum_fusion.2), channel_id=1, source_target_pairs={{0,64},{64,128},{128,192},{192,0},{32,224},{96,32},{160,96},{224,1... | collective-permute-start | bytes 589832 | tf_op jit(solution)/shard_map/ppermute | solution.py:372
  11.8 1.6 %collective-permute-start.2 = (bf16[80,1024]{1,0:T(8,128)(2,1)S(1)}, bf16[80,1024]{1,0:T(8,128)(2,1)S(1)}, u32[]{:S(2)}, u32[]{:S(2)}) collective-permute-start(bf16[80,1024]{1,0:T(8,128)(2,1)S(1)} %get-tuple-element.59), channel_id=1, source_target_pairs={{0,128},{64,192},{128,0},{192,64},{32,160},{96,224},{160,32},{224,... | collective-permute-start | bytes 491528 | tf_op jit(solution)/shard_map/ppermute | solution.py:372
  14.1 0.1 copy.20
  14.6 0.2 reshape.42.v_ref
  14.8 4.7 %taps_table.1.w_ref = bf16[768,3072]{1,0:T(8,128)(2,1)S(1)} custom-call(f32[24,1,512]{2,1,0:T(1,128)S(1)} %reshape.42.v_ref), custom_call_target="tpu_custom_call" | custom-call | flops 20000000 | bytes 10000000 | tf_op jit(solution)/shard_map/taps_table/pallas_call | solution.py:91
  19.5 2.3 %collective-permute-done.3.m3_ref = bf16[80,1024]{1,0:T(8,128)(2,1)S(1)} collective-permute-done((bf16[80,1024]{1,0:T(8,128)(2,1)S(1)}, bf16[80,1024]{1,0:T(8,128)(2,1)S(1)}, u32[]{:S(2)}, u32[]{:S(2)}) %collective-permute-start.3) | collective-permute-done | bytes 163872 | tf_op jit(solution)/shard_map/ppermute | solution.py:372
  21.8 9.1 %image.1 = (bf16[48,1024]{1,0:T(8,128)(2,1)}, bf16[64,1024]{1,0:T(8,128)(2,1)S(1)}) custom-call(s32[1]{0:T(128)S(6)} %copy.29.level_ref, s32[1]{0:T(128)} %bitcast.shard_ref, f32[8,12]{1,0:T(8,128)S(1)} %copy-done.1, f32[80,1024]{1,0:T(8,128)S(1)} %get-tuple-element.61.m0_ref, bf16[96,1024]{1,0:T(8,128)(2,1)S(1)} %collective-permute-done.1.m1_ref, ...), custom_call_target="tpu_custom_call" | custom-call | flops 5000000000 | bytes 8000000 | tf_op jit(solution)/shard_map/image/pallas_call | solution.py:162
  30.9 2.1 %collective-permute-start.6 = (bf16[64,1024]{1,0:T(8,128)(2,1)S(1)}, bf16[64,1024]{1,0:T(8,128)(2,1)S(1)}, u32[]{:S(2)}, u32[]{:S(2)}) collective-permute-start(bf16[64,1024]{1,0:T(8,128)(2,1)S(1)} %get-tuple-element.33.g0), channel_id=1, source_target_pairs={{0,3},{1,0},{2,1},{3,2},{32,33},{33,34},{34,35},{35,32},{4,7},{5,4... | collective-permute-start | bytes 393224 | tf_op jit(solution)/shard_map/ppermute | solution.py:372
  33.0 0.6 collective-permute-start.5
  33.6 1.0 collective-permute-start.4
  34.6 4.1 %collective-permute-done.6.g3 = bf16[64,1024]{1,0:T(8,128)(2,1)S(1)} collective-permute-done((bf16[64,1024]{1,0:T(8,128)(2,1)S(1)}, bf16[64,1024]{1,0:T(8,128)(2,1)S(1)}, u32[]{:S(2)}, u32[]{:S(2)}) %collective-permute-start.6) | collective-permute-done | bytes 131104 | tf_op jit(solution)/shard_map/ppermute | solution.py:372
  38.7 0.9 collective-permute-done.5.g2
  39.6 1.3 collective-permute-done.4.g1
  40.9 1.2 collective-permute-start.9
  42.1 1.7 %collective-permute-start.8 = (bf16[4,48,1024]{2,1,0:T(8,128)(2,1)S(1)}, bf16[4,48,1024]{2,1,0:T(8,128)(2,1)S(1)}, u32[]{:S(2)}, u32[]{:S(2)}) collective-permute-start(bf16[4,48,1024]{2,1,0:T(8,128)(2,1)S(1)} %pad_maximum_fusion), channel_id=1, source_target_pairs={{0,192},{64,0},{128,64},{192,128},{32,96},{96,160},{160,224},{224,... | collective-permute-start | bytes 1179656 | tf_op jit(solution)/shard_map/ppermute | solution.py:372
  43.9 1.5 %collective-permute-start.7 = (bf16[4,48,1024]{2,1,0:T(8,128)(2,1)S(1)}, bf16[4,48,1024]{2,1,0:T(8,128)(2,1)S(1)}, u32[]{:S(2)}, u32[]{:S(2)}) collective-permute-start(bf16[4,48,1024]{2,1,0:T(8,128)(2,1)S(1)} %pad_maximum_fusion), channel_id=1, source_target_pairs={{0,64},{64,128},{128,192},{192,0},{32,224},{96,32},{160,96},{224,1... | collective-permute-start | bytes 1179656 | tf_op jit(solution)/shard_map/ppermute | solution.py:372
  45.4 2.4 %all-gather = bf16[8,48,1024]{2,1,0:T(8,128)(2,1)S(1)} all-gather(bf16[4,48,1024]{2,1,0:T(8,128)(2,1)S(1)} %pad_maximum_fusion), channel_id=2, replica_groups=mesh['x'=4,'core'=2,'z'=8,'y'=4] {'core'}, dimensions={0}, use_global_device_ids=true | all-gather | bytes 1179648 | tf_op jit(solution)/shard_map/all_gather | solution.py:425
  47.7 6.9 %collective-permute-done.9 = bf16[4,48,1024]{2,1,0:T(8,128)(2,1)S(1)} collective-permute-done((bf16[4,48,1024]{2,1,0:T(8,128)(2,1)S(1)}, bf16[4,48,1024]{2,1,0:T(8,128)(2,1)S(1)}, u32[]{:S(2)}, u32[]{:S(2)}) %collective-permute-start.9) | collective-permute-done | bytes 393248 | tf_op jit(solution)/shard_map/ppermute | solution.py:372
  54.6 2.4 %all-gather.3 = bf16[8,48,1024]{2,1,0:T(8,128)(2,1)S(1)} all-gather(bf16[4,48,1024]{2,1,0:T(8,128)(2,1)S(1)} %collective-permute-done.9), channel_id=5, replica_groups=mesh['x'=4,'core'=2,'z'=8,'y'=4] {'core'}, dimensions={0}, use_global_device_ids=true | all-gather | bytes 1179648 | tf_op jit(solution)/shard_map/all_gather | solution.py:425
  57.0 4.2 %collective-permute-done.8 = bf16[4,48,1024]{2,1,0:T(8,128)(2,1)S(1)} collective-permute-done((bf16[4,48,1024]{2,1,0:T(8,128)(2,1)S(1)}, bf16[4,48,1024]{2,1,0:T(8,128)(2,1)S(1)}, u32[]{:S(2)}, u32[]{:S(2)}) %collective-permute-start.8) | collective-permute-done | bytes 393248 | tf_op jit(solution)/shard_map/ppermute | solution.py:372
  61.1 2.4 %all-gather.2 = bf16[8,48,1024]{2,1,0:T(8,128)(2,1)S(1)} all-gather(bf16[4,48,1024]{2,1,0:T(8,128)(2,1)S(1)} %collective-permute-done.8), channel_id=4, replica_groups=mesh['x'=4,'core'=2,'z'=8,'y'=4] {'core'}, dimensions={0}, use_global_device_ids=true | all-gather | bytes 1179648 | tf_op jit(solution)/shard_map/all_gather | solution.py:425
  63.5 2.4 %all-gather.1 = bf16[8,48,1024]{2,1,0:T(8,128)(2,1)S(1)} all-gather(bf16[4,48,1024]{2,1,0:T(8,128)(2,1)S(1)} %collective-permute-done.7), channel_id=3, replica_groups=mesh['x'=4,'core'=2,'z'=8,'y'=4] {'core'}, dimensions={0}, use_global_device_ids=true | all-gather | bytes 1179648 | tf_op jit(solution)/shard_map/all_gather | solution.py:425
  65.9 4.4 %cut.1 = (f32[4,128,128]{2,1,0:T(8,128)S(1)}, bf16[4,128,128]{2,1,0:T(8,128)(2,1)S(1)}, f32[4,128,128]{2,1,0:T(8,128)S(1)}, bf16[4,128,128]{2,1,0:T(8,128)(2,1)S...) custom-call(s32[1]{0:T(128)} %bitcast.shard_ref, ...), custom_call_target="tpu_custom_call" | custom-call | flops 1000000 | bytes 12000000 | tf_op jit(solution)/shard_map/cut/pallas_call | solution.py:314
  70.3 1.4 collective-permute-start.10
  71.7 3.3 %collective-permute-start.13 = (bf16[2,128,128]{2,1,0:T(8,128)(2,1)S(1)}, bf16[2,128,128]{2,1,0:T(8,128)(2,1)S(1)}, u32[]{:S(2)}, u32[]{:S(2)}) collective-permute-start(bf16[2,128,128]{2,1,0:T(8,128)(2,1)S(1)} %get-tuple-element.42), channel_id=1, source_target_pairs={{0,8},{4,12},{8,16},{12,20},{16,24},{20,28},{24,0},{28,4},{32,56},... | collective-permute-start | bytes 196616 | tf_op jit(solution)/shard_map/ppermute | solution.py:372
  74.9 2.3 %collective-permute-start.16 = (bf16[2,128,128]{2,1,0:T(8,128)(2,1)S(1)}, bf16[2,128,128]{2,1,0:T(8,128)(2,1)S(1)}, u32[]{:S(2)}, u32[]{:S(2)}) collective-permute-start(bf16[2,128,128]{2,1,0:T(8,128)(2,1)S(1)} %get-tuple-element.45), channel_id=1, source_target_pairs={{0,24},{4,28},{8,0},{12,4},{16,8},{20,12},{24,16},{28,20},{32,40},... | collective-permute-start | bytes 196616 | tf_op jit(solution)/shard_map/ppermute | solution.py:372
  77.2 1.5 %collective-permute-start.15 = (bf16[4,128,128]{2,1,0:T(8,128)(2,1)S(1)}, bf16[4,128,128]{2,1,0:T(8,128)(2,1)S(1)}, u32[]{:S(2)}, u32[]{:S(2)}) collective-permute-start(bf16[4,128,128]{2,1,0:T(8,128)(2,1)S(1)} %get-tuple-element.44), channel_id=1, source_target_pairs={{0,28},{4,0},{8,4},{12,8},{16,12},{20,16},{24,20},{28,24},{32,36},... | collective-permute-start | bytes 393224 | tf_op jit(solution)/shard_map/ppermute | solution.py:372
  78.7 0.5 collective-permute-start.11
  79.2 2.7 %collective-permute-start.12 = (bf16[4,128,128]{2,1,0:T(8,128)(2,1)S(1)}, bf16[4,128,128]{2,1,0:T(8,128)(2,1)S(1)}, u32[]{:S(2)}, u32[]{:S(2)}) collective-permute-start(bf16[4,128,128]{2,1,0:T(8,128)(2,1)S(1)} %get-tuple-element.39), channel_id=1, source_target_pairs={{0,28},{4,0},{8,4},{12,8},{16,12},{20,16},{24,20},{28,24},{32,36},... | collective-permute-start | bytes 393224 | tf_op jit(solution)/shard_map/ppermute | solution.py:372
  82.0 0.8 collective-permute-done.13
  83.0 1.6 %collective-permute-done.15 = bf16[4,128,128]{2,1,0:T(8,128)(2,1)S(1)} collective-permute-done((bf16[4,128,128]{2,1,0:T(8,128)(2,1)S(1)}, bf16[4,128,128]{2,1,0:T(8,128)(2,1)S(1)}, u32[]{:S(2)}, u32[]{:S(2)}) %collective-permute-start.15) | collective-permute-done | bytes 131104 | tf_op jit(solution)/shard_map/ppermute | solution.py:372
  84.7 2.6 %collective-permute-start.17 = (bf16[4,128,128]{2,1,0:T(8,128)(2,1)S(1)}, bf16[4,128,128]{2,1,0:T(8,128)(2,1)S(1)}, u32[]{:S(2)}, u32[]{:S(2)}) collective-permute-start(bf16[4,128,128]{2,1,0:T(8,128)(2,1)S(1)} %pad_maximum_fusion.4), channel_id=1, source_target_pairs={{0,24},{4,28},{8,0},{12,4},{16,8},{20,12},{24,16},{28,20},{32,40},... | collective-permute-start | bytes 393224 | tf_op jit(solution)/shard_map/ppermute | solution.py:372
  87.3 3.0 %collective-permute-done.14 = bf16[4,128,128]{2,1,0:T(8,128)(2,1)S(1)} collective-permute-done((bf16[4,128,128]{2,1,0:T(8,128)(2,1)S(1)}, bf16[4,128,128]{2,1,0:T(8,128)(2,1)S(1)}, u32[]{:S(2)}, u32[]{:S(2)}) %collective-permute-start.14) | collective-permute-done | bytes 131104 | tf_op jit(solution)/shard_map/ppermute | solution.py:372
  90.2 0.7 collective-permute-done.17
  91.0 2.7 %collective-permute-start.18 = (bf16[4,128,128]{2,1,0:T(8,128)(2,1)S(1)}, bf16[4,128,128]{2,1,0:T(8,128)(2,1)S(1)}, u32[]{:S(2)}, u32[]{:S(2)}) collective-permute-start(bf16[4,128,128]{2,1,0:T(8,128)(2,1)S(1)} %add_convert_fusion), channel_id=1, source_target_pairs={{0,2},{1,3},{2,0},{3,1},{32,34},{33,35},{34,32},{35,33},{4,6},{5,7... | collective-permute-start | bytes 393224 | tf_op jit(solution)/shard_map/ppermute | solution.py:372
  93.7 3.9 %collective-permute-done.18 = bf16[4,128,128]{2,1,0:T(8,128)(2,1)S(1)} collective-permute-done((bf16[4,128,128]{2,1,0:T(8,128)(2,1)S(1)}, bf16[4,128,128]{2,1,0:T(8,128)(2,1)S(1)}, u32[]{:S(2)}, u32[]{:S(2)}) %collective-permute-start.18) | collective-permute-done | bytes 131104 | tf_op jit(solution)/shard_map/ppermute | solution.py:372
  97.6 4.4 %collective-permute-start.20 = (bf16[8,128,128]{2,1,0:T(8,128)(2,1)S(1)}, bf16[8,128,128]{2,1,0:T(8,128)(2,1)S(1)}, u32[]{:S(2)}, u32[]{:S(2)}) collective-permute-start(bf16[8,128,128]{2,1,0:T(8,128)(2,1)S(1)} %pad_maximum_fusion.1.refs_0_), channel_id=1, source_target_pairs={{0,28},{4,0},{8,4},{12,8},{16,12},{20,16},{24,20},{28,24},{32,36},... | collective-permute-start | bytes 786440 | tf_op jit(solution)/shard_map/ppermute | solution.py:372
  102.0 0.4 collective-permute-start.19
  102.4 1.7 %collective-permute-start.23 = (bf16[8,128,128]{2,1,0:T(8,128)(2,1)S(1)}, bf16[8,128,128]{2,1,0:T(8,128)(2,1)S(1)}, u32[]{:S(2)}, u32[]{:S(2)}) collective-permute-start(bf16[8,128,128]{2,1,0:T(8,128)(2,1)S(1)} %pad_maximum_fusion.1.refs_0_), channel_id=1, source_target_pairs={{0,1},{1,2},{2,3},{3,0},{32,35},{33,32},{34,33},{35,34},{4,5},{5,6... | collective-permute-start | bytes 786440 | tf_op jit(solution)/shard_map/ppermute | solution.py:372
  104.1 0.8 deposit.6.refs_3_
  104.9 3.1 %collective-permute-done.20.refs_1_ = bf16[8,128,128]{2,1,0:T(8,128)(2,1)S(1)} collective-permute-done((bf16[8,128,128]{2,1,0:T(8,128)(2,1)S(1)}, bf16[8,128,128]{2,1,0:T(8,128)(2,1)S(1)}, u32[]{:S(2)}, u32[]{:S(2)}) %collective-permute-start.20) | collective-permute-done | bytes 262176 | tf_op jit(solution)/shard_map/ppermute | solution.py:372
  108.0 1.6 %collective-permute-done.19.refs_0_ = bf16[8,128,128]{2,1,0:T(8,128)(2,1)S(1)} collective-permute-done((bf16[8,128,128]{2,1,0:T(8,128)(2,1)S(1)}, bf16[8,128,128]{2,1,0:T(8,128)(2,1)S(1)}, u32[]{:S(2)}, u32[]{:S(2)}) %collective-permute-start.19) | collective-permute-done | bytes 262176 | tf_op jit(solution)/shard_map/ppermute | solution.py:372
  109.6 3.2 %collective-permute-start.22 = (bf16[8,128,128]{2,1,0:T(8,128)(2,1)S(1)}, bf16[8,128,128]{2,1,0:T(8,128)(2,1)S(1)}, u32[]{:S(2)}, u32[]{:S(2)}) collective-permute-start(bf16[8,128,128]{2,1,0:T(8,128)(2,1)S(1)} %collective-permute-done.20.refs_1_), channel_id=1, source_target_pairs={{0,28},{4,0},{8,4},{12,8},{16,12},{20,16},{24,20},{28,24},{32,36},... | collective-permute-start | bytes 786440 | tf_op jit(solution)/shard_map/ppermute | solution.py:372
  112.8 0.8 collective-permute-start.26
  113.6 2.5 %collective-permute-start.27 = (bf16[8,128,128]{2,1,0:T(8,128)(2,1)S(1)}, bf16[8,128,128]{2,1,0:T(8,128)(2,1)S(1)}, u32[]{:S(2)}, u32[]{:S(2)}) collective-permute-start(bf16[8,128,128]{2,1,0:T(8,128)(2,1)S(1)} %collective-permute-done.20.refs_1_), channel_id=1, source_target_pairs={{0,3},{1,0},{2,1},{3,2},{32,33},{33,34},{34,35},{35,32},{4,7},{5,4... | collective-permute-start | bytes 786440 | tf_op jit(solution)/shard_map/ppermute | solution.py:372
  116.0 1.2 deposit.7.refs_4_
  117.3 2.4 %collective-permute-done.21.refs_0_ = bf16[8,128,128]{2,1,0:T(8,128)(2,1)S(1)} collective-permute-done((bf16[8,128,128]{2,1,0:T(8,128)(2,1)S(1)}, bf16[8,128,128]{2,1,0:T(8,128)(2,1)S(1)}, u32[]{:S(2)}, u32[]{:S(2)}) %collective-permute-start.21) | collective-permute-done | bytes 262176 | tf_op jit(solution)/shard_map/ppermute | solution.py:372
  119.6 3.2 %collective-permute-start.25 = (bf16[8,128,128]{2,1,0:T(8,128)(2,1)S(1)}, bf16[8,128,128]{2,1,0:T(8,128)(2,1)S(1)}, u32[]{:S(2)}, u32[]{:S(2)}) collective-permute-start(bf16[8,128,128]{2,1,0:T(8,128)(2,1)S(1)} %collective-permute-done.22.refs_1_), channel_id=1, source_target_pairs={{0,28},{4,0},{8,4},{12,8},{16,12},{20,16},{24,20},{28,24},{32,36},... | collective-permute-start | bytes 786440 | tf_op jit(solution)/shard_map/ppermute | solution.py:372
  122.9 1.6 %collective-permute-start.29 = (bf16[8,128,128]{2,1,0:T(8,128)(2,1)S(1)}, bf16[8,128,128]{2,1,0:T(8,128)(2,1)S(1)}, u32[]{:S(2)}, u32[]{:S(2)}) collective-permute-start(bf16[8,128,128]{2,1,0:T(8,128)(2,1)S(1)} %collective-permute-done.21.refs_0_), channel_id=1, source_target_pairs={{0,1},{1,2},{2,3},{3,0},{32,35},{33,32},{34,33},{35,34},{4,5},{5,6... | collective-permute-start | bytes 786440 | tf_op jit(solution)/shard_map/ppermute | solution.py:372
  124.5 2.3 %collective-permute-start.30 = (bf16[8,128,128]{2,1,0:T(8,128)(2,1)S(1)}, bf16[8,128,128]{2,1,0:T(8,128)(2,1)S(1)}, u32[]{:S(2)}, u32[]{:S(2)}) collective-permute-start(bf16[8,128,128]{2,1,0:T(8,128)(2,1)S(1)} %collective-permute-done.22.refs_1_), channel_id=1, source_target_pairs={{0,3},{1,0},{2,1},{3,2},{32,33},{33,34},{34,35},{35,32},{4,7},{5,4... | collective-permute-start | bytes 786440 | tf_op jit(solution)/shard_map/ppermute | solution.py:372
  126.8 1.4 deposit.8.refs_4_
  128.2 1.3 collective-permute-done.24.refs_0_
  129.6 3.7 %collective-permute-start.32 = (bf16[8,128,128]{2,1,0:T(8,128)(2,1)S(1)}, bf16[8,128,128]{2,1,0:T(8,128)(2,1)S(1)}, u32[]{:S(2)}, u32[]{:S(2)}) collective-permute-start(bf16[8,128,128]{2,1,0:T(8,128)(2,1)S(1)} %collective-permute-done.24.refs_0_), channel_id=1, source_target_pairs={{0,1},{1,2},{2,3},{3,0},{32,35},{33,32},{34,33},{35,34},{4,5},{5,6... | collective-permute-start | bytes 786440 | tf_op jit(solution)/shard_map/ppermute | solution.py:372
  133.3 1.3 collective-permute-start.33
  134.6 1.4 deposit.9.refs_3_
  136.0 1.1 collective-permute-done.28.refs_0_
  137.1 1.7 %collective-permute-start.31 = (bf16[8,128,128]{2,1,0:T(8,128)(2,1)S(1)}, bf16[8,128,128]{2,1,0:T(8,128)(2,1)S(1)}, u32[]{:S(2)}, u32[]{:S(2)}) collective-permute-start(bf16[8,128,128]{2,1,0:T(8,128)(2,1)S(1)} %collective-permute-done.28.refs_0_), channel_id=1, source_target_pairs={{0,1},{1,2},{2,3},{3,0},{32,35},{33,32},{34,33},{35,34},{4,5},{5,6... | collective-permute-start | bytes 786440 | tf_op jit(solution)/shard_map/ppermute | solution.py:372
  138.8 3.3 %collective-permute-done.33.refs_2_ = bf16[8,128,128]{2,1,0:T(8,128)(2,1)S(1)} collective-permute-done((bf16[8,128,128]{2,1,0:T(8,128)(2,1)S(1)}, bf16[8,128,128]{2,1,0:T(8,128)(2,1)S(1)}, u32[]{:S(2)}, u32[]{:S(2)}) %collective-permute-start.33) | collective-permute-done | bytes 262176 | tf_op jit(solution)/shard_map/ppermute | solution.py:372
  142.2 1.2 deposit.10.refs_1_
  143.4 2.8 %collective-permute-done.31.refs_0_ = bf16[8,128,128]{2,1,0:T(8,128)(2,1)S(1)} collective-permute-done((bf16[8,128,128]{2,1,0:T(8,128)(2,1)S(1)}, bf16[8,128,128]{2,1,0:T(8,128)(2,1)S(1)}, u32[]{:S(2)}, u32[]{:S(2)}) %collective-permute-start.31) | collective-permute-done | bytes 262176 | tf_op jit(solution)/shard_map/ppermute | solution.py:372
  146.2 0.8 deposit.11
  (50 shorter events, 1.1 us)
Async XLA Ops:
  0.6 13.3 %copy-start.3 = (bf16[24,225]{1,0:T(8,128)(2,1)S(1)}, bf16[24,225]{1,0:T(8,128)(2,1)}, u32[]{:S(2)}) copy-start(bf16[24,225]{1,0:T(8,128)(2,1)} %param.14) | copy-start | bytes 32404
  0.6 21.1 %copy-start = (bf16[1,48,1024]{2,1,0:T(8,128)(2,1)S(1)}, bf16[1,48,1024]{2,1,0:T(8,128)(2,1)}, u32[]{:S(2)}) copy-start(bf16[1,48,1024]{2,1,0:T(8,128)(2,1)} %param.15) | copy-start | bytes 294916
  0.7 21.1 %copy-start.1 = (f32[8,12]{1,0:T(8,128)S(1)}, f32[8,12]{1,0:T(8,128)}, u32[]{:S(2)}) copy-start(f32[8,12]{1,0:T(8,128)} %wgt_ref.1) | copy-start | bytes 1156
  5.5 16.3 %copy-start.2 = (s32[1,128]{1,0:T(1,128)S(1)}, s32[1,128]{1,0:T(1,128)}, u32[]{:S(2)}) copy-start(s32[1,128]{1,0:T(1,128)} %get-tuple-element.32.info_ref) | copy-start | bytes 1540
  5.5 2.4 %collective-permute-start = (bf16[336,1024]{1,0:T(8,128)(2,1)}, bf16[336,1024]{1,0:T(8,128)(2,1)S(1)}, u32[]{:S(2)}, u32[]{:S(2)}) collective-permute-start(bf16[336,1024]{1,0:T(8,128)(2,1)} %get-tuple-element.31), channel_id=1, source_target_pairs={{0,32},{32,0},{1,33},{33,1},{2,34},{34,2},{3,35},{35,3},{4,36},{36... | collective-permute-start | bytes 2064392 | tf_op jit(solution)/shard_map/ppermute | solution.py:413
  9.5 12.3 %collective-permute-start.1 = (bf16[96,1024]{1,0:T(8,128)(2,1)S(1)}, bf16[96,1024]{1,0:T(8,128)(2,1)S(1)}, u32[]{:S(2)}, u32[]{:S(2)}) collective-permute-start(bf16[96,1024]{1,0:T(8,128)(2,1)S(1)} %pad_maximum_fusion.2), channel_id=1, source_target_pairs={{0,64},{64,128},{128,192},{192,0},{32,224},{96,32},{160,96},{224,1... | collective-permute-start | bytes 589832 | tf_op jit(solution)/shard_map/ppermute | solution.py:372
  11.7 10.0 %collective-permute-start.3 = (bf16[80,1024]{1,0:T(8,128)(2,1)S(1)}, bf16[80,1024]{1,0:T(8,128)(2,1)S(1)}, u32[]{:S(2)}, u32[]{:S(2)}) collective-permute-start(bf16[80,1024]{1,0:T(8,128)(2,1)S(1)} %get-tuple-element.58), channel_id=1, source_target_pairs={{0,192},{64,0},{128,64},{192,128},{32,96},{96,160},{160,224},{224,... | collective-permute-start | bytes 491528 | tf_op jit(solution)/shard_map/ppermute | solution.py:372
  11.8 10.0 %collective-permute-start.2 = (bf16[80,1024]{1,0:T(8,128)(2,1)S(1)}, bf16[80,1024]{1,0:T(8,128)(2,1)S(1)}, u32[]{:S(2)}, u32[]{:S(2)}) collective-permute-start(bf16[80,1024]{1,0:T(8,128)(2,1)S(1)} %get-tuple-element.59), channel_id=1, source_target_pairs={{0,128},{64,192},{128,0},{192,64},{32,160},{96,224},{160,32},{224,... | collective-permute-start | bytes 491528 | tf_op jit(solution)/shard_map/ppermute | solution.py:372
  30.9 7.7 %collective-permute-start.6 = (bf16[64,1024]{1,0:T(8,128)(2,1)S(1)}, bf16[64,1024]{1,0:T(8,128)(2,1)S(1)}, u32[]{:S(2)}, u32[]{:S(2)}) collective-permute-start(bf16[64,1024]{1,0:T(8,128)(2,1)S(1)} %get-tuple-element.33.g0), channel_id=1, source_target_pairs={{0,3},{1,0},{2,1},{3,2},{32,33},{33,34},{34,35},{35,32},{4,7},{5,4... | collective-permute-start | bytes 393224 | tf_op jit(solution)/shard_map/ppermute | solution.py:372
  33.0 6.6 %collective-permute-start.5 = (bf16[64,1024]{1,0:T(8,128)(2,1)S(1)}, bf16[64,1024]{1,0:T(8,128)(2,1)S(1)}, u32[]{:S(2)}, u32[]{:S(2)}) collective-permute-start(bf16[64,1024]{1,0:T(8,128)(2,1)S(1)} %get-tuple-element.33.g0), channel_id=1, source_target_pairs={{0,2},{1,3},{2,0},{3,1},{32,34},{33,35},{34,32},{35,33},{4,6},{5,7... | collective-permute-start | bytes 393224 | tf_op jit(solution)/shard_map/ppermute | solution.py:372
  33.6 7.2 %collective-permute-start.4 = (bf16[64,1024]{1,0:T(8,128)(2,1)S(1)}, bf16[64,1024]{1,0:T(8,128)(2,1)S(1)}, u32[]{:S(2)}, u32[]{:S(2)}) collective-permute-start(bf16[64,1024]{1,0:T(8,128)(2,1)S(1)} %get-tuple-element.33.g0), channel_id=1, source_target_pairs={{0,1},{1,2},{2,3},{3,0},{32,35},{33,32},{34,33},{35,34},{4,5},{5,6... | collective-permute-start | bytes 393224 | tf_op jit(solution)/shard_map/ppermute | solution.py:372
  40.9 13.7 %collective-permute-start.9 = (bf16[4,48,1024]{2,1,0:T(8,128)(2,1)S(1)}, bf16[4,48,1024]{2,1,0:T(8,128)(2,1)S(1)}, u32[]{:S(2)}, u32[]{:S(2)}) collective-permute-start(bf16[4,48,1024]{2,1,0:T(8,128)(2,1)S(1)} %pad_maximum_fusion), channel_id=1, source_target_pairs={{0,128},{64,192},{128,0},{192,64},{32,160},{96,224},{160,32},{224,... | collective-permute-start | bytes 1179656 | tf_op jit(solution)/shard_map/ppermute | solution.py:372
  42.1 19.0 %collective-permute-start.8 = (bf16[4,48,1024]{2,1,0:T(8,128)(2,1)S(1)}, bf16[4,48,1024]{2,1,0:T(8,128)(2,1)S(1)}, u32[]{:S(2)}, u32[]{:S(2)}) collective-permute-start(bf16[4,48,1024]{2,1,0:T(8,128)(2,1)S(1)} %pad_maximum_fusion), channel_id=1, source_target_pairs={{0,192},{64,0},{128,64},{192,128},{32,96},{96,160},{160,224},{224,... | collective-permute-start | bytes 1179656 | tf_op jit(solution)/shard_map/ppermute | solution.py:372
  43.9 19.6 %collective-permute-start.7 = (bf16[4,48,1024]{2,1,0:T(8,128)(2,1)S(1)}, bf16[4,48,1024]{2,1,0:T(8,128)(2,1)S(1)}, u32[]{:S(2)}, u32[]{:S(2)}) collective-permute-start(bf16[4,48,1024]{2,1,0:T(8,128)(2,1)S(1)} %pad_maximum_fusion), channel_id=1, source_target_pairs={{0,64},{64,128},{128,192},{192,0},{32,224},{96,32},{160,96},{224,1... | collective-permute-start | bytes 1179656 | tf_op jit(solution)/shard_map/ppermute | solution.py:372
  70.3 8.4 %collective-permute-start.10 = (bf16[4,128,128]{2,1,0:T(8,128)(2,1)S(1)}, bf16[4,128,128]{2,1,0:T(8,128)(2,1)S(1)}, u32[]{:S(2)}, u32[]{:S(2)}) collective-permute-start(bf16[4,128,128]{2,1,0:T(8,128)(2,1)S(1)} %get-tuple-element.35), channel_id=1, source_target_pairs={{0,4},{4,8},{8,12},{12,16},{16,20},{20,24},{24,28},{28,0},{32,60},... | collective-permute-start | bytes 393224 | tf_op jit(solution)/shard_map/ppermute | solution.py:372
  71.7 11.1 %collective-permute-start.13 = (bf16[2,128,128]{2,1,0:T(8,128)(2,1)S(1)}, bf16[2,128,128]{2,1,0:T(8,128)(2,1)S(1)}, u32[]{:S(2)}, u32[]{:S(2)}) collective-permute-start(bf16[2,128,128]{2,1,0:T(8,128)(2,1)S(1)} %get-tuple-element.42), channel_id=1, source_target_pairs={{0,8},{4,12},{8,16},{12,20},{16,24},{20,28},{24,0},{28,4},{32,56},... | collective-permute-start | bytes 196616 | tf_op jit(solution)/shard_map/ppermute | solution.py:372
  74.9 9.7 %collective-permute-start.16 = (bf16[2,128,128]{2,1,0:T(8,128)(2,1)S(1)}, bf16[2,128,128]{2,1,0:T(8,128)(2,1)S(1)}, u32[]{:S(2)}, u32[]{:S(2)}) collective-permute-start(bf16[2,128,128]{2,1,0:T(8,128)(2,1)S(1)} %get-tuple-element.45), channel_id=1, source_target_pairs={{0,24},{4,28},{8,0},{12,4},{16,8},{20,12},{24,16},{28,20},{32,40},... | collective-permute-start | bytes 196616 | tf_op jit(solution)/shard_map/ppermute | solution.py:372
  77.2 7.4 %collective-permute-start.15 = (bf16[4,128,128]{2,1,0:T(8,128)(2,1)S(1)}, bf16[4,128,128]{2,1,0:T(8,128)(2,1)S(1)}, u32[]{:S(2)}, u32[]{:S(2)}) collective-permute-start(bf16[4,128,128]{2,1,0:T(8,128)(2,1)S(1)} %get-tuple-element.44), channel_id=1, source_target_pairs={{0,28},{4,0},{8,4},{12,8},{16,12},{20,16},{24,20},{28,24},{32,36},... | collective-permute-start | bytes 393224 | tf_op jit(solution)/shard_map/ppermute | solution.py:372
  78.7 8.5 %collective-permute-start.11 = (bf16[4,128,128]{2,1,0:T(8,128)(2,1)S(1)}, bf16[4,128,128]{2,1,0:T(8,128)(2,1)S(1)}, u32[]{:S(2)}, u32[]{:S(2)}) collective-permute-start(bf16[4,128,128]{2,1,0:T(8,128)(2,1)S(1)} %get-tuple-element.38), channel_id=1, source_target_pairs={{0,4},{4,8},{8,12},{12,16},{16,20},{20,24},{24,28},{28,0},{32,60},... | collective-permute-start | bytes 393224 | tf_op jit(solution)/shard_map/ppermute | solution.py:372
  79.2 8.0 %collective-permute-start.12 = (bf16[4,128,128]{2,1,0:T(8,128)(2,1)S(1)}, bf16[4,128,128]{2,1,0:T(8,128)(2,1)S(1)}, u32[]{:S(2)}, u32[]{:S(2)}) collective-permute-start(bf16[4,128,128]{2,1,0:T(8,128)(2,1)S(1)} %get-tuple-element.39), channel_id=1, source_target_pairs={{0,28},{4,0},{8,4},{12,8},{16,12},{20,16},{24,20},{28,24},{32,36},... | collective-permute-start | bytes 393224 | tf_op jit(solution)/shard_map/ppermute | solution.py:372
  82.9 7.4 %collective-permute-start.14 = (bf16[4,128,128]{2,1,0:T(8,128)(2,1)S(1)}, bf16[4,128,128]{2,1,0:T(8,128)(2,1)S(1)}, u32[]{:S(2)}, u32[]{:S(2)}) collective-permute-start(bf16[4,128,128]{2,1,0:T(8,128)(2,1)S(1)} %pad_maximum_fusion.3), channel_id=1, source_target_pairs={{0,8},{4,12},{8,16},{12,20},{16,24},{20,28},{24,0},{28,4},{32,56},... | collective-permute-start | bytes 393224 | tf_op jit(solution)/shard_map/ppermute | solution.py:372
  84.7 6.3 %collective-permute-start.17 = (bf16[4,128,128]{2,1,0:T(8,128)(2,1)S(1)}, bf16[4,128,128]{2,1,0:T(8,128)(2,1)S(1)}, u32[]{:S(2)}, u32[]{:S(2)}) collective-permute-start(bf16[4,128,128]{2,1,0:T(8,128)(2,1)S(1)} %pad_maximum_fusion.4), channel_id=1, source_target_pairs={{0,24},{4,28},{8,0},{12,4},{16,8},{20,12},{24,16},{28,20},{32,40},... | collective-permute-start | bytes 393224 | tf_op jit(solution)/shard_map/ppermute | solution.py:372
  91.0 6.6 %collective-permute-start.18 = (bf16[4,128,128]{2,1,0:T(8,128)(2,1)S(1)}, bf16[4,128,128]{2,1,0:T(8,128)(2,1)S(1)}, u32[]{:S(2)}, u32[]{:S(2)}) collective-permute-start(bf16[4,128,128]{2,1,0:T(8,128)(2,1)S(1)} %add_convert_fusion), channel_id=1, source_target_pairs={{0,2},{1,3},{2,0},{3,1},{32,34},{33,35},{34,32},{35,33},{4,6},{5,7... | collective-permute-start | bytes 393224 | tf_op jit(solution)/shard_map/ppermute | solution.py:372
  97.6 10.4 %collective-permute-start.20 = (bf16[8,128,128]{2,1,0:T(8,128)(2,1)S(1)}, bf16[8,128,128]{2,1,0:T(8,128)(2,1)S(1)}, u32[]{:S(2)}, u32[]{:S(2)}) collective-permute-start(bf16[8,128,128]{2,1,0:T(8,128)(2,1)S(1)} %pad_maximum_fusion.1.refs_0_), channel_id=1, source_target_pairs={{0,28},{4,0},{8,4},{12,8},{16,12},{20,16},{24,20},{28,24},{32,36},... | collective-permute-start | bytes 786440 | tf_op jit(solution)/shard_map/ppermute | solution.py:372
  102.0 7.6 %collective-permute-start.19 = (bf16[8,128,128]{2,1,0:T(8,128)(2,1)S(1)}, bf16[8,128,128]{2,1,0:T(8,128)(2,1)S(1)}, u32[]{:S(2)}, u32[]{:S(2)}) collective-permute-start(bf16[8,128,128]{2,1,0:T(8,128)(2,1)S(1)} %pad_maximum_fusion.1.refs_0_), channel_id=1, source_target_pairs={{0,4},{4,8},{8,12},{12,16},{16,20},{20,24},{24,28},{28,0},{32,60},... | collective-permute-start | bytes 786440 | tf_op jit(solution)/shard_map/ppermute | solution.py:372
  102.4 13.6 %collective-permute-start.23 = (bf16[8,128,128]{2,1,0:T(8,128)(2,1)S(1)}, bf16[8,128,128]{2,1,0:T(8,128)(2,1)S(1)}, u32[]{:S(2)}, u32[]{:S(2)}) collective-permute-start(bf16[8,128,128]{2,1,0:T(8,128)(2,1)S(1)} %pad_maximum_fusion.1.refs_0_), channel_id=1, source_target_pairs={{0,1},{1,2},{2,3},{3,0},{32,35},{33,32},{34,33},{35,34},{4,5},{5,6... | collective-permute-start | bytes 786440 | tf_op jit(solution)/shard_map/ppermute | solution.py:372
  109.6 10.1 %collective-permute-start.21 = (bf16[8,128,128]{2,1,0:T(8,128)(2,1)S(1)}, bf16[8,128,128]{2,1,0:T(8,128)(2,1)S(1)}, u32[]{:S(2)}, u32[]{:S(2)}) collective-permute-start(bf16[8,128,128]{2,1,0:T(8,128)(2,1)S(1)} %collective-permute-done.19.refs_0_), channel_id=1, source_target_pairs={{0,4},{4,8},{8,12},{12,16},{16,20},{20,24},{24,28},{28,0},{32,60},... | collective-permute-start | bytes 786440 | tf_op jit(solution)/shard_map/ppermute | solution.py:372
  109.6 10.1 %collective-permute-start.22 = (bf16[8,128,128]{2,1,0:T(8,128)(2,1)S(1)}, bf16[8,128,128]{2,1,0:T(8,128)(2,1)S(1)}, u32[]{:S(2)}, u32[]{:S(2)}) collective-permute-start(bf16[8,128,128]{2,1,0:T(8,128)(2,1)S(1)} %collective-permute-done.20.refs_1_), channel_id=1, source_target_pairs={{0,28},{4,0},{8,4},{12,8},{16,12},{20,16},{24,20},{28,24},{32,36},... | collective-permute-start | bytes 786440 | tf_op jit(solution)/shard_map/ppermute | solution.py:372
  112.8 11.7 %collective-permute-start.26 = (bf16[8,128,128]{2,1,0:T(8,128)(2,1)S(1)}, bf16[8,128,128]{2,1,0:T(8,128)(2,1)S(1)}, u32[]{:S(2)}, u32[]{:S(2)}) collective-permute-start(bf16[8,128,128]{2,1,0:T(8,128)(2,1)S(1)} %collective-permute-done.19.refs_0_), channel_id=1, source_target_pairs={{0,1},{1,2},{2,3},{3,0},{32,35},{33,32},{34,33},{35,34},{4,5},{5,6... | collective-permute-start | bytes 786440 | tf_op jit(solution)/shard_map/ppermute | solution.py:372
  113.6 13.2 %collective-permute-start.27 = (bf16[8,128,128]{2,1,0:T(8,128)(2,1)S(1)}, bf16[8,128,128]{2,1,0:T(8,128)(2,1)S(1)}, u32[]{:S(2)}, u32[]{:S(2)}) collective-permute-start(bf16[8,128,128]{2,1,0:T(8,128)(2,1)S(1)} %collective-permute-done.20.refs_1_), channel_id=1, source_target_pairs={{0,3},{1,0},{2,1},{3,2},{32,33},{33,34},{34,35},{35,32},{4,7},{5,4... | collective-permute-start | bytes 786440 | tf_op jit(solution)/shard_map/ppermute | solution.py:372
  119.6 9.9 %collective-permute-start.24 = (bf16[8,128,128]{2,1,0:T(8,128)(2,1)S(1)}, bf16[8,128,128]{2,1,0:T(8,128)(2,1)S(1)}, u32[]{:S(2)}, u32[]{:S(2)}) collective-permute-start(bf16[8,128,128]{2,1,0:T(8,128)(2,1)S(1)} %collective-permute-done.21.refs_0_), channel_id=1, source_target_pairs={{0,4},{4,8},{8,12},{12,16},{16,20},{20,24},{24,28},{28,0},{32,60},... | collective-permute-start | bytes 786440 | tf_op jit(solution)/shard_map/ppermute | solution.py:372
  119.6 9.9 %collective-permute-start.25 = (bf16[8,128,128]{2,1,0:T(8,128)(2,1)S(1)}, bf16[8,128,128]{2,1,0:T(8,128)(2,1)S(1)}, u32[]{:S(2)}, u32[]{:S(2)}) collective-permute-start(bf16[8,128,128]{2,1,0:T(8,128)(2,1)S(1)} %collective-permute-done.22.refs_1_), channel_id=1, source_target_pairs={{0,28},{4,0},{8,4},{12,8},{16,12},{20,16},{24,20},{28,24},{32,36},... | collective-permute-start | bytes 786440 | tf_op jit(solution)/shard_map/ppermute | solution.py:372
  122.9 11.7 %collective-permute-start.29 = (bf16[8,128,128]{2,1,0:T(8,128)(2,1)S(1)}, bf16[8,128,128]{2,1,0:T(8,128)(2,1)S(1)}, u32[]{:S(2)}, u32[]{:S(2)}) collective-permute-start(bf16[8,128,128]{2,1,0:T(8,128)(2,1)S(1)} %collective-permute-done.21.refs_0_), channel_id=1, source_target_pairs={{0,1},{1,2},{2,3},{3,0},{32,35},{33,32},{34,33},{35,34},{4,5},{5,6... | collective-permute-start | bytes 786440 | tf_op jit(solution)/shard_map/ppermute | solution.py:372
  124.5 10.1 %collective-permute-start.30 = (bf16[8,128,128]{2,1,0:T(8,128)(2,1)S(1)}, bf16[8,128,128]{2,1,0:T(8,128)(2,1)S(1)}, u32[]{:S(2)}, u32[]{:S(2)}) collective-permute-start(bf16[8,128,128]{2,1,0:T(8,128)(2,1)S(1)} %collective-permute-done.22.refs_1_), channel_id=1, source_target_pairs={{0,3},{1,0},{2,1},{3,2},{32,33},{33,34},{34,35},{35,32},{4,7},{5,4... | collective-permute-start | bytes 786440 | tf_op jit(solution)/shard_map/ppermute | solution.py:372
  129.5 7.6 %collective-permute-start.28 = (bf16[8,128,128]{2,1,0:T(8,128)(2,1)S(1)}, bf16[8,128,128]{2,1,0:T(8,128)(2,1)S(1)}, u32[]{:S(2)}, u32[]{:S(2)}) collective-permute-start(bf16[8,128,128]{2,1,0:T(8,128)(2,1)S(1)} %collective-permute-done.24.refs_0_), channel_id=1, source_target_pairs={{0,4},{4,8},{8,12},{12,16},{16,20},{20,24},{24,28},{28,0},{32,60},... | collective-permute-start | bytes 786440 | tf_op jit(solution)/shard_map/ppermute | solution.py:372
  129.6 12.6 %collective-permute-start.32 = (bf16[8,128,128]{2,1,0:T(8,128)(2,1)S(1)}, bf16[8,128,128]{2,1,0:T(8,128)(2,1)S(1)}, u32[]{:S(2)}, u32[]{:S(2)}) collective-permute-start(bf16[8,128,128]{2,1,0:T(8,128)(2,1)S(1)} %collective-permute-done.24.refs_0_), channel_id=1, source_target_pairs={{0,1},{1,2},{2,3},{3,0},{32,35},{33,32},{34,33},{35,34},{4,5},{5,6... | collective-permute-start | bytes 786440 | tf_op jit(solution)/shard_map/ppermute | solution.py:372
  133.3 8.9 %collective-permute-start.33 = (bf16[8,128,128]{2,1,0:T(8,128)(2,1)S(1)}, bf16[8,128,128]{2,1,0:T(8,128)(2,1)S(1)}, u32[]{:S(2)}, u32[]{:S(2)}) collective-permute-start(bf16[8,128,128]{2,1,0:T(8,128)(2,1)S(1)} %collective-permute-done.25.refs_1_), channel_id=1, source_target_pairs={{0,3},{1,0},{2,1},{3,2},{32,33},{33,34},{34,35},{35,32},{4,7},{5,4... | collective-permute-start | bytes 786440 | tf_op jit(solution)/shard_map/ppermute | solution.py:372
  137.1 9.1 %collective-permute-start.31 = (bf16[8,128,128]{2,1,0:T(8,128)(2,1)S(1)}, bf16[8,128,128]{2,1,0:T(8,128)(2,1)S(1)}, u32[]{:S(2)}, u32[]{:S(2)}) collective-permute-start(bf16[8,128,128]{2,1,0:T(8,128)(2,1)S(1)} %collective-permute-done.28.refs_0_), channel_id=1, source_target_pairs={{0,1},{1,2},{2,3},{3,0},{32,35},{33,32},{34,33},{35,34},{4,5},{5,6... | collective-permute-start | bytes 786440 | tf_op jit(solution)/shard_map/ppermute | solution.py:372
